TPU v7x, 32 devices: a whole 2x2x4 slice. The times are simulated.
32 devices in a mesh: dp: 4 (over x, core), fsdp: 8 (over z, y).
Axes of the slice: x: 2, y: 2, z: 4, core: 2. Of those that a mesh axis runs over, the one named last changes fastest.
Arguments:
- tokens: bfloat16 [64, 512, 768], P(('dp', 'fsdp')), may hold values from -6 to 6
- cotangent: bfloat16 [64, 512, 768], P(('dp', 'fsdp')), may hold values from -6 to 6
- segment_ids: int32 [64, 512], P(('dp', 'fsdp')), may hold values from 0 to 3, as said below
- pad_mask: int32 [64, 512], P(('dp', 'fsdp')), may hold values from 0 to 1, as said below
- row_counts: int32 [32], P(('dp', 'fsdp')), may hold values from 1 to 2, as said below
- query_weight: bfloat16 [768, 768], P(('dp', 'fsdp')), may hold values from -0.21875 to 0.21875
- query_bias: bfloat16 [768], P(('dp', 'fsdp')), may hold values from -3 to 3
- key_weight: bfloat16 [768, 768], P(('dp', 'fsdp')), may hold values from -0.21875 to 0.21875
- value_weight: bfloat16 [768, 768], P(('dp', 'fsdp')), may hold values from -0.21875 to 0.21875
- value_bias: bfloat16 [768], P(('dp', 'fsdp')), may hold values from -3 to 3
- out_weight: bfloat16 [768, 768], P(('dp', 'fsdp')), may hold values from -1.75 to 1.75
- out_bias: bfloat16 [768], P(('dp', 'fsdp')), may hold values from -3 to 3
- first_gain: bfloat16 [768], P(('dp', 'fsdp')), may hold values from 0.25 to 1.75
- first_shift: bfloat16 [768], P(('dp', 'fsdp')), may hold values from -3 to 3
- up_weight: bfloat16 [3072, 768], P(('dp', 'fsdp')), may hold values from -0.21875 to 0.21875
- up_bias: bfloat16 [3072], P(('dp', 'fsdp')), may hold values from -3 to 3
- down_weight: bfloat16 [768, 3072], P(('dp', 'fsdp')), may hold values from -0.109375 to 0.109375
- down_bias: bfloat16 [768], P(('dp', 'fsdp')), may hold values from -3 to 3
- second_gain: bfloat16 [768], P(('dp', 'fsdp')), may hold values from 0.25 to 1.75
- second_shift: bfloat16 [768], P(('dp', 'fsdp')), may hold values from -3 to 3
Outputs:
- outputs: bfloat16 [64, 512, 768], P(('dp', 'fsdp'))
- tokens_grad: float32 [64, 512, 768], P(('dp', 'fsdp'))
- query_weight_grad: float32 [768, 768], P(('dp', 'fsdp'))
- query_bias_grad: float32 [768], P(('dp', 'fsdp'))
- key_weight_grad: float32 [768, 768], P(('dp', 'fsdp'))
- value_weight_grad: float32 [768, 768], P(('dp', 'fsdp'))
- value_bias_grad: float32 [768], P(('dp', 'fsdp'))
- out_weight_grad: float32 [768, 768], P(('dp', 'fsdp'))
- out_bias_grad: float32 [768], P(('dp', 'fsdp'))
- first_gain_grad: float32 [768], P(('dp', 'fsdp'))
- first_shift_grad: float32 [768], P(('dp', 'fsdp'))
- up_weight_grad: float32 [3072, 768], P(('dp', 'fsdp'))
- up_bias_grad: float32 [3072], P(('dp', 'fsdp'))
- down_weight_grad: float32 [768, 3072], P(('dp', 'fsdp'))
- down_bias_grad: float32 [768], P(('dp', 'fsdp'))
- second_gain_grad: float32 [768], P(('dp', 'fsdp'))
- second_shift_grad: float32 [768], P(('dp', 'fsdp'))
Inputs may be any that keep to these rules, and one draw needn't show every extreme that they name: `segment_ids`: each row holds one bucket: segment number = position // length with length 512, 256 or 128 for the whole row. `pad_mask`: within every sequence of segment_ids, the ones form a leading run of at least half its length. A device uses its first row_counts row slots; some device uses all 2.
All inputs are finite; a program needn't handle non-finite values.
Results may differ from a plain program's by a relative error of at most 0.024.
Values may be sent and summed in bfloat16 or wider, within the bound.
No kernel may reach another device: no remote copies, remote signals or barrier semaphores. Data moves between devices by JAX's collectives and lax.ppermute only.
A program may use at most 192 MiB of HBM per device.

v0:
```python
from functools import partial
import math

import jax
import jax.numpy as jnp
from jax import lax
from jax.sharding import PartitionSpec as P

HEAD = 64
LAYERS = 2


norm_eps = 1e-06
masked_score = -1000000000.0


def project(inputs, weight):
    return lax.dot_general(
        inputs, weight, (((1,), (1,)), ((), ())), preferred_element_type=jnp.float32
    )


def weight_grad(grad_low, inputs):
    return lax.dot_general(
        grad_low, inputs, (((0,), (0,)), ((), ())), preferred_element_type=jnp.float32
    )


def back_project(grad_low, weight):
    return jnp.dot(grad_low, weight, preferred_element_type=jnp.float32)


def column_sum(grad_low):
    return jnp.sum(grad_low, axis=0, dtype=jnp.float32)


def layer_norm(inputs, norm_gain, norm_shift):
    average = jnp.mean(inputs, axis=-1, keepdims=True)
    centered = inputs - average
    variance = jnp.mean(centered * centered, axis=-1, keepdims=True)
    return centered * lax.rsqrt(variance + norm_eps) * norm_gain + norm_shift


def attention_mask(segments, alive):
    length = segments.shape[-1]
    position = jnp.arange(length, dtype=jnp.int32)
    diagonal = position[:, None] == position[None, :]
    same = segments[:, :, None] == segments[:, None, :]
    return same & ((alive[:, None, :] > 0) | diagonal[None])


def masked_scores(queries, key_rows, segments, alive):
    scaling = queries.shape[-1] ** (-0.5)
    scores = (
        jnp.einsum("glhe,gmhe->ghlm", queries, key_rows, preferred_element_type=jnp.float32)
        * scaling
    )
    return jnp.where(attention_mask(segments, alive)[:, None], scores, masked_score)


def attend_forward(blocks):
    queries, key_rows, value_rows, segments, alive = blocks
    scores = masked_scores(queries, key_rows, segments, alive)
    highest = jnp.max(scores, axis=-1, keepdims=True)
    weights = jnp.exp(scores - highest)
    total = jnp.sum(weights, axis=-1, keepdims=True)
    probs = (weights / total).astype(jnp.bfloat16)
    context = jnp.einsum("ghlm,gmhe->glhe", probs, value_rows, preferred_element_type=jnp.float32)
    return (context.astype(jnp.bfloat16), (highest + jnp.log(total))[..., 0])


def attend_backward(blocks):
    queries, key_rows, value_rows, segments, alive, log_total, grad_context = blocks
    scaling = queries.shape[-1] ** (-0.5)
    scores = masked_scores(queries, key_rows, segments, alive)
    probs = jnp.exp(scores - log_total[..., None])
    grad_probs = jnp.einsum(
        "glhe,gmhe->ghlm", grad_context, value_rows, preferred_element_type=jnp.float32
    )
    inner = jnp.sum(grad_probs * probs, axis=-1, keepdims=True)
    grad_scores = (probs * (grad_probs - inner)).astype(jnp.bfloat16)
    grad_query = jnp.einsum(
        "ghlm,gmhe->glhe", grad_scores, key_rows, preferred_element_type=jnp.float32
    )
    grad_key = jnp.einsum(
        "ghlm,glhe->gmhe", grad_scores, queries, preferred_element_type=jnp.float32
    )
    grad_value = jnp.einsum(
        "ghlm,glhe->gmhe",
        probs.astype(jnp.bfloat16),
        grad_context,
        preferred_element_type=jnp.float32,
    )
    return (
        (grad_query * scaling).astype(jnp.bfloat16),
        (grad_key * scaling).astype(jnp.bfloat16),
        grad_value.astype(jnp.bfloat16),
    )


def head_shape(blocks_seg, width):
    blocks, group, row_len = blocks_seg.shape
    return (blocks, group, row_len, width // HEAD, HEAD)


def forward_use(hidden, mixer_params, feed_params, blocks_seg, blocks_alive):
    (
        query_weight,
        query_bias,
        key_weight,
        value_weight,
        value_bias,
        out_weight,
        out_bias,
        first_gain,
        first_shift,
    ) = mixer_params
    up_weight, up_bias, down_weight, down_bias, second_gain, second_shift = feed_params
    count, width = hidden.shape
    shape = head_shape(blocks_seg, width)
    inputs = hidden.astype(jnp.bfloat16)
    queries = (project(inputs, query_weight) + query_bias.astype(jnp.float32)).astype(jnp.bfloat16)
    key_rows = project(inputs, key_weight).astype(jnp.bfloat16)
    value_rows = (project(inputs, value_weight) + value_bias.astype(jnp.float32)).astype(
        jnp.bfloat16
    )
    context, log_total = lax.map(
        attend_forward,
        (
            queries.reshape(shape),
            key_rows.reshape(shape),
            value_rows.reshape(shape),
            blocks_seg,
            blocks_alive,
        ),
    )
    context = context.reshape(count, width)
    mixed = hidden + project(context, out_weight) + out_bias.astype(jnp.float32)
    normed = layer_norm(mixed, first_gain.astype(jnp.float32), first_shift.astype(jnp.float32))
    normed_low = normed.astype(jnp.bfloat16)
    upward = project(normed_low, up_weight) + up_bias.astype(jnp.float32)
    activated = jax.nn.gelu(upward, approximate=True).astype(jnp.bfloat16)
    combined = normed + project(activated, down_weight) + down_bias.astype(jnp.float32)
    output = layer_norm(combined, second_gain.astype(jnp.float32), second_shift.astype(jnp.float32))
    kept = (
        inputs,
        queries,
        key_rows,
        value_rows,
        context,
        log_total,
        mixed,
        normed_low,
        upward,
        activated,
        combined,
    )
    return (output, kept)


def feed_backward(grad_out, kept, feed_params):
    (
        inputs,
        queries,
        key_rows,
        value_rows,
        context,
        log_total,
        mixed,
        normed_low,
        upward,
        activated,
        combined,
    ) = kept
    up_weight, up_bias, down_weight, down_bias, second_gain, second_shift = feed_params
    unused, norm_back = jax.vjp(
        layer_norm, combined, second_gain.astype(jnp.float32), second_shift.astype(jnp.float32)
    )
    grad_combined, grad_second_gain, grad_second_shift = norm_back(grad_out)
    grad_branch = grad_combined.astype(jnp.bfloat16)
    grad_activated = back_project(grad_branch, down_weight)
    unused, gelu_back = jax.vjp(partial(jax.nn.gelu, approximate=True), upward)
    grad_upward = gelu_back(grad_activated)[0].astype(jnp.bfloat16)
    grad_normed = grad_combined + back_project(grad_upward, up_weight)
    grads = (
        weight_grad(grad_upward, normed_low),
        column_sum(grad_upward),
        weight_grad(grad_branch, activated),
        column_sum(grad_branch),
        grad_second_gain,
        grad_second_shift,
    )
    return (grad_normed, grads)


def mixer_backward(grad_normed, kept, mixer_params, blocks_seg, blocks_alive):
    (
        inputs,
        queries,
        key_rows,
        value_rows,
        context,
        log_total,
        mixed,
        normed_low,
        upward,
        activated,
        combined,
    ) = kept
    (
        query_weight,
        query_bias,
        key_weight,
        value_weight,
        value_bias,
        out_weight,
        out_bias,
        first_gain,
        first_shift,
    ) = mixer_params
    count, width = queries.shape
    shape = head_shape(blocks_seg, width)
    unused, norm_back = jax.vjp(
        layer_norm, mixed, first_gain.astype(jnp.float32), first_shift.astype(jnp.float32)
    )
    grad_mixed, grad_first_gain, grad_first_shift = norm_back(grad_normed)
    grad_branch = grad_mixed.astype(jnp.bfloat16)
    grad_context = back_project(grad_branch, out_weight).astype(jnp.bfloat16)
    grad_query, grad_key, grad_value = lax.map(
        attend_backward,
        (
            queries.reshape(shape),
            key_rows.reshape(shape),
            value_rows.reshape(shape),
            blocks_seg,
            blocks_alive,
            log_total,
            grad_context.reshape(shape),
        ),
    )
    grad_query = grad_query.reshape(count, width)
    grad_key = grad_key.reshape(count, width)
    grad_value = grad_value.reshape(count, width)
    grad_hidden = (
        grad_mixed
        + back_project(grad_query, query_weight)
        + back_project(grad_key, key_weight)
        + back_project(grad_value, value_weight)
    )
    grads = (
        weight_grad(grad_query, inputs),
        column_sum(grad_query),
        weight_grad(grad_key, inputs),
        weight_grad(grad_value, inputs),
        column_sum(grad_value),
        weight_grad(grad_branch, context),
        column_sum(grad_branch),
        grad_first_gain,
        grad_first_shift,
    )
    return (grad_hidden, grads)


def accumulate(total, term):
    if total is None:
        return term
    return jax.tree.map(jnp.add, total, term)


def body(
    tokens,
    cotangent,
    segment_ids,
    pad_mask,
    row_counts,
    query_weight,
    query_bias,
    key_weight,
    value_weight,
    value_bias,
    out_weight,
    out_bias,
    first_gain,
    first_shift,
    up_weight,
    up_bias,
    down_weight,
    down_bias,
    second_gain,
    second_shift,
):
    rows_here, row_len, width = tokens.shape
    count = rows_here * row_len
    present = (jnp.arange(rows_here, dtype=jnp.int32) < row_counts[0]).astype(jnp.int32)
    alive = pad_mask * present[:, None]
    alive_flat = alive.reshape(count, 1).astype(jnp.float32)
    group = math.gcd(rows_here, max(1, 512 // row_len))
    blocks_seg = segment_ids.reshape(rows_here // group, group, row_len)
    blocks_alive = alive.reshape(rows_here // group, group, row_len)
    mixer_params = (
        lax.all_gather(query_weight, ("dp", "fsdp"), axis=0, tiled=True),
        lax.all_gather(query_bias, ("dp", "fsdp"), axis=0, tiled=True),
        lax.all_gather(key_weight, ("dp", "fsdp"), axis=0, tiled=True),
        lax.all_gather(value_weight, ("dp", "fsdp"), axis=0, tiled=True),
        lax.all_gather(value_bias, ("dp", "fsdp"), axis=0, tiled=True),
        lax.all_gather(out_weight, ("dp", "fsdp"), axis=0, tiled=True),
        lax.all_gather(out_bias, ("dp", "fsdp"), axis=0, tiled=True),
        lax.all_gather(first_gain, ("dp", "fsdp"), axis=0, tiled=True),
        lax.all_gather(first_shift, ("dp", "fsdp"), axis=0, tiled=True),
    )
    feed_params = (
        lax.all_gather(up_weight, ("dp", "fsdp"), axis=0, tiled=True),
        lax.all_gather(up_bias, ("dp", "fsdp"), axis=0, tiled=True),
        lax.all_gather(down_weight, ("dp", "fsdp"), axis=0, tiled=True),
        lax.all_gather(down_bias, ("dp", "fsdp"), axis=0, tiled=True),
        lax.all_gather(second_gain, ("dp", "fsdp"), axis=0, tiled=True),
        lax.all_gather(second_shift, ("dp", "fsdp"), axis=0, tiled=True),
    )
    hidden = tokens.reshape(count, width).astype(jnp.float32)
    saved = []
    for layer in range(LAYERS):
        hidden, kept = forward_use(hidden, mixer_params, feed_params, blocks_seg, blocks_alive)
        saved.append(kept)
    outputs = (hidden * alive_flat).astype(jnp.bfloat16).reshape(rows_here, row_len, width)
    grad_hidden = cotangent.reshape(count, width).astype(jnp.float32) * alive_flat
    mixer_total = None
    feed_total = None
    for layer in reversed(range(LAYERS)):
        grad_normed, feed_grads = feed_backward(grad_hidden, saved[layer], feed_params)
        feed_total = accumulate(feed_total, feed_grads)
        grad_hidden, mixer_grads = mixer_backward(
            grad_normed, saved[layer], mixer_params, blocks_seg, blocks_alive
        )
        mixer_total = accumulate(mixer_total, mixer_grads)
    mixer_total = lax.psum_scatter(mixer_total, ("dp", "fsdp"), scatter_dimension=0, tiled=True)
    feed_total = lax.psum_scatter(feed_total, ("dp", "fsdp"), scatter_dimension=0, tiled=True)
    tokens_grad = grad_hidden.reshape(rows_here, row_len, width)
    return (
        outputs,
        tokens_grad,
        mixer_total[0],
        mixer_total[1],
        mixer_total[2],
        mixer_total[3],
        mixer_total[4],
        mixer_total[5],
        mixer_total[6],
        mixer_total[7],
        mixer_total[8],
        feed_total[0],
        feed_total[1],
        feed_total[2],
        feed_total[3],
        feed_total[4],
        feed_total[5],
    )


def solution(mesh):
    placed = (
        P(("dp", "fsdp"), None, None),
        P(("dp", "fsdp"), None, None),
        P(("dp", "fsdp"), None),
        P(("dp", "fsdp"), None),
        P(("dp", "fsdp")),
        P(("dp", "fsdp"), None),
        P(("dp", "fsdp")),
        P(("dp", "fsdp"), None),
        P(("dp", "fsdp"), None),
        P(("dp", "fsdp")),
        P(("dp", "fsdp"), None),
        P(("dp", "fsdp")),
        P(("dp", "fsdp")),
        P(("dp", "fsdp")),
        P(("dp", "fsdp"), None),
        P(("dp", "fsdp")),
        P(("dp", "fsdp"), None),
        P(("dp", "fsdp")),
        P(("dp", "fsdp")),
        P(("dp", "fsdp")),
    )
    return jax.shard_map(
        body,
        mesh=mesh,
        in_specs=placed,
        out_specs=(
            P(("dp", "fsdp"), None, None),
            P(("dp", "fsdp"), None, None),
            P(("dp", "fsdp"), None),
            P(("dp", "fsdp")),
            P(("dp", "fsdp"), None),
            P(("dp", "fsdp"), None),
            P(("dp", "fsdp")),
            P(("dp", "fsdp"), None),
            P(("dp", "fsdp")),
            P(("dp", "fsdp")),
            P(("dp", "fsdp")),
            P(("dp", "fsdp"), None),
            P(("dp", "fsdp")),
            P(("dp", "fsdp"), None),
            P(("dp", "fsdp")),
            P(("dp", "fsdp")),
            P(("dp", "fsdp")),
        ),
        check_vma=False,
    )
```

profile of v0, /device:TPU:0, one launch (start us, length us, event | category | flops | bytes accessed | tf_op | source)
XLA Modules:
  0.0 1314.8 jit_solution(918816413954848563)
XLA Ops:
  20.8 42.4 %all-reduce.19 = (bf16[768]{0:T(1024)(128)(2,1)S(1)}, bf16[768]{0:T(1024)(128)(2,1)S(1)}, bf16[768]{0:T(1024)(128)(2,1)S(1)}, bf16[768]{0:T(1024)(128)(2,1)S(1)}...) all-reduce(bf16[768]{0:T(1024)(128)(2,1)S(1)} %dynamic-update-slice, ...), channel_id=1, replica_groups=mesh['dp'=4,'fsdp'=8] {'dp','fsdp'}, use_global_device_ids=true, to_apply=%add | all-reduce | flops 9216 | bytes 36864
  74.7 49.2 %all-gather.9.cloned.1.call-done = bf16[768,768]{1,0:T(8,128)(2,1)} async-done(((bf16[24,768]{1,0:T(8,128)(2,1)}), bf16[768,768]{1,0:T(8,128)(2,1)}) %all-gather.9.cloned.1.call-update) | async-done | bytes 1179664 | tf_op jit(solution)/shard_map/all_gather | solution.py:301
  128.9 51.0 %all-gather.11.cloned.1.call-done = bf16[768,768]{1,0:T(8,128)(2,1)} async-done(((bf16[24,768]{1,0:T(8,128)(2,1)}), bf16[768,768]{1,0:T(8,128)(2,1)}) %all-gather.11.cloned.1.call-update) | async-done | bytes 1179664 | tf_op jit(solution)/shard_map/all_gather | solution.py:303
  191.4 21.1 %while.52 = (s32[]{:T(128)}, bf16[2,1,512,12,64]{2,4,3,1,0:T(8,128)(2,1)}, f32[2,1,12,512]{3,2,1,0:T(8,128)S(1)}, bf16[2,1,512,12,64]{2,4,3,1,0:T(8,128)(2,1)}, ...) while((s32[]{:T(128)}, ...), condition=%wide.region_3.4_spmd, body=%wide.region_0.3_spmd.sunk | while | flops 844491264 | bytes 42175592 | solution.py:127
  218.2 17.6 %all-gather.13.cloned.1.call-done = bf16[768,768]{1,0:T(8,128)(2,1)} async-done(((bf16[24,768]{1,0:T(8,128)(2,1)}), bf16[768,768]{1,0:T(8,128)(2,1)}) %all-gather.13.cloned.1.call-update) | async-done | bytes 1179664 | tf_op jit(solution)/shard_map/all_gather | solution.py:306
  240.2 60.9 %all-gather.15.cloned.1.call-done = bf16[3072,768]{1,0:T(8,128)(2,1)} async-done(((bf16[96,768]{1,0:T(8,128)(2,1)}), bf16[3072,768]{1,0:T(8,128)(2,1)}) %all-gather.15.cloned.1.call-update) | async-done | bytes 4718608 | tf_op jit(solution)/shard_map/all_gather | solution.py:312
  301.1 10.8 fusion.149
  312.0 54.5 %all-gather.17.cloned.1.call-done = bf16[768,3072]{1,0:T(8,128)(2,1)} async-done(((bf16[24,3072]{1,0:T(8,128)(2,1)}), bf16[768,3072]{1,0:T(8,128)(2,1)}) %all-gather.17.cloned.1.call-update) | async-done | bytes 4718608 | tf_op jit(solution)/shard_map/all_gather | solution.py:314
  366.4 12.6 fusion.158
  409.6 21.1 %while.53 = (s32[]{:T(128)}, bf16[2,1,512,12,64]{2,4,3,1,0:T(8,128)(2,1)}, f32[2,1,12,512]{3,2,1,0:T(8,128)S(1)}, bf16[2,1,512,12,64]{2,4,3,1,0:T(8,128)(2,1)}, ...) while((s32[]{:T(128)}, ...), condition=%wide.region_11.12_spmd, body=%wide.region_8.11_spmd.sunk | while | flops 844491264 | bytes 42175592 | solution.py:127
  445.9 12.7 fusion.160
  466.1 18.3 %convert_reduce_fusion.1 = (f32[3072]{0:T(1024)}, bf16[1024,3072]{1,0:T(8,128)(2,1)}) fusion(f32[1024,3072]{1,0:T(8,128)} %fusion.146, f32[3072]{0:T(1024)S(1)} %copy-done.103, bf16[1024,768]{1,0:T(8,128)(2,1)S(1)} %get-tuple-element.455, bf16[768,3072]{1,0:T(8,128)(2,1)} %all-gather.17.cloned.1.call-done), kind=kOutput, calls=%fused_computation.161 | convolution fusion | flops 4904186880 | bytes 25190400 | tf_op jit(solution)/shard_map/dot_general | solution.py:30
  515.3 49.3 %while.54 = (s32[]{:T(128)}, bf16[2,1,512,12,64]{2,4,3,1,0:T(8,128)(2,1)}, bf16[2,1,512,12,64]{2,4,3,1,0:T(8,128)(2,1)}, bf16[2,1,512,12,64]{2,4,3,1,0:T(8,128)(...) while((s32[]{:T(128)}, ...), condition=%wide.region_22.23_spmd, body=%wide.region_20.22_spmd.sunk | while | flops 2063460864 | bytes 147528016 | solution.py:229
  583.5 15.6 %convert_reduce_fusion = (f32[3072]{0:T(1024)}, bf16[1024,3072]{1,0:T(8,128)(2,1)S(1)}) fusion(f32[1024,3072]{1,0:T(8,128)} %fusion.149, f32[3072]{0:T(1024)S(1)} %copy-done.104, bf16[1024,768]{1,0:T(8,128)(2,1)S(1)} %get-tuple-element.453, bf16[768,3072]{1,0:T(8,128)(2,1)S(1)} %bitcast.406), kind=kOutput, calls=%fused_computation.160 | convolution fusion | flops 4904186880 | bytes 25190400 | tf_op jit(solution)/shard_map/dot_general | solution.py:30
  623.9 49.4 %while.55 = (s32[]{:T(128)}, bf16[2,1,512,12,64]{2,4,3,1,0:T(8,128)(2,1)}, bf16[2,1,512,12,64]{2,4,3,1,0:T(8,128)(2,1)}, bf16[2,1,512,12,64]{2,4,3,1,0:T(8,128)(...) while((s32[]{:T(128)}, ...), condition=%wide.region_29.30_spmd, body=%wide.region_27.29_spmd.sunk | while | flops 2063460864 | bytes 147528016 | solution.py:229
  707.3 11.6 convolution_add_fusion
  719.6 9.0 fusion.144
  728.6 11.8 convolution_add_fusion.1
  745.2 40.9 %all-reduce.18 = (f32[768]{0:T(1024)S(1)}, f32[768]{0:T(1024)S(1)}, f32[768]{0:T(1024)S(1)}, f32[768]{0:T(1024)S(1)}, f32[768]{0:T(1024)S(1)}, /*index=5*/f32[30...) all-reduce(f32[768]{0:T(1024)S(1)} %add.362, ...), channel_id=3, replica_groups=mesh['dp'=4,'fsdp'=8] {'dp','fsdp'}, use_global_device_ids=true, to_apply=%region_33.34.clone | all-reduce | flops 9216 | bytes 73728
  799.2 16.9 %reduce-scatter.11.cloned.1.call-done = f32[24,768]{1,0:T(8,128)} async-done(((f32[768,768]{1,0:T(8,128)}), f32[24,768]{1,0:T(8,128)}) %reduce-scatter.11.cloned.1.call-update) | async-done | bytes 73744 | tf_op jit(solution)/shard_map/reduce_scatter | solution.py:335
  816.1 103.9 %reduce-scatter.9.cloned.1.call-done = f32[24,768]{1,0:T(8,128)} async-done(((f32[768,768]{1,0:T(8,128)}), f32[24,768]{1,0:T(8,128)}) %reduce-scatter.9.cloned.1.call-update) | async-done | bytes 73744 | tf_op jit(solution)/shard_map/reduce_scatter | solution.py:335
  920.0 104.7 %reduce-scatter.7.cloned.1.call-done = f32[24,768]{1,0:T(8,128)} async-done(((f32[768,768]{1,0:T(8,128)}), f32[24,768]{1,0:T(8,128)}) %reduce-scatter.7.cloned.1.call-update) | async-done | bytes 73744 | tf_op jit(solution)/shard_map/reduce_scatter | solution.py:335
  1024.7 141.0 %reduce-scatter.17.cloned.1.call-done = f32[24,3072]{1,0:T(8,128)} async-done(((f32[768,3072]{1,0:T(8,128)}), f32[24,3072]{1,0:T(8,128)}) %reduce-scatter.17.cloned.1.call-update) | async-done | bytes 294928 | tf_op jit(solution)/shard_map/reduce_scatter | solution.py:336
  1165.7 141.8 %reduce-scatter.15.cloned.1.call-done = f32[96,768]{1,0:T(8,128)} async-done(((f32[3072,768]{1,0:T(8,128)}), f32[96,768]{1,0:T(8,128)}) %reduce-scatter.15.cloned.1.call-update) | async-done | bytes 294928 | tf_op jit(solution)/shard_map/reduce_scatter | solution.py:336
  (573 shorter events, 369.3 us)
Async XLA Ops:
  7.2 60.9 %all-gather.7.cloned.1.call-start = ((), (), s32[]{:S(2)}) async-start(), calls=%async_computation.6 | async-start | bytes 1216512 | tf_op jit(solution)/shard_map/all_gather | solution.py:304
  7.9 116.0 %all-gather.9.cloned.1.call-start = ((), (), s32[]{:S(2)}) async-start(), calls=%async_computation.7 | async-start | bytes 1216512 | tf_op jit(solution)/shard_map/all_gather | solution.py:301
  8.7 171.3 %all-gather.11.cloned.1.call-start = ((), (), s32[]{:S(2)}) async-start(), calls=%async_computation.8 | async-start | bytes 1216512 | tf_op jit(solution)/shard_map/all_gather | solution.py:303
  9.4 226.4 %all-gather.13.cloned.1.call-start = ((), (), s32[]{:S(2)}) async-start(), calls=%async_computation.9 | async-start | bytes 1216512 | tf_op jit(solution)/shard_map/all_gather | solution.py:306
  10.0 291.1 %all-gather.15.cloned.1.call-start = ((), (), s32[]{:S(2)}) async-start(), calls=%async_computation.10 | async-start | bytes 4866048 | tf_op jit(solution)/shard_map/all_gather | solution.py:312
  10.6 355.8 %all-gather.17.cloned.1.call-start = ((), (), s32[]{:S(2)}) async-start(), calls=%async_computation.11 | async-start | bytes 4866048 | tf_op jit(solution)/shard_map/all_gather | solution.py:314
  11.1 788.0 %reduce-scatter.13.cloned.1.call-start = ((), (), s32[]{:S(2)}) async-start(), calls=%async_computation.15 | async-start | bytes 2433024 | tf_op jit(solution)/shard_map/reduce_scatter | solution.py:335
  63.2 60.7 %copy-start.121 = (f32[768]{0:T(1024)}, f32[768]{0:T(1024)S(1)}, u32[]{:S(2)}) copy-start(f32[768]{0:T(1024)S(1)} %convert_element_type.266) | copy-start | bytes 9220
  63.9 171.9 %copy-start.117 = (f32[768]{0:T(1024)}, f32[768]{0:T(1024)S(1)}, u32[]{:S(2)}) copy-start(f32[768]{0:T(1024)S(1)} %convert_element_type.269) | copy-start | bytes 9220
  239.6 126.8 %copy-start.27 = (f32[1024,768]{1,0:T(8,128)}, f32[1024,768]{1,0:T(8,128)S(1)}, u32[]{:S(2)}) copy-start(f32[1024,768]{1,0:T(8,128)S(1)} %get-tuple-element.478) | copy-start | bytes 9437188
  239.6 61.5 %copy-start.72 = (f32[768]{0:T(1024)S(1)}, f32[768]{0:T(1024)}, u32[]{:S(2)}) copy-start(f32[768]{0:T(1024)} %convert_element_type.270) | copy-start | bytes 9220
  239.6 61.5 %copy-start.112 = (f32[768]{0:T(1024)S(1)}, f32[768]{0:T(1024)}, u32[]{:S(2)}) copy-start(f32[768]{0:T(1024)} %convert_element_type.271) | copy-start | bytes 9220
  239.7 126.8 %copy-start.76 = (f32[1024]{0:T(1024)}, f32[1024]{0:T(1024)S(1)}, u32[]{:S(2)}) copy-start(f32[1024]{0:T(1024)S(1)} %broadcast_multiply_fusion.4) | copy-start | bytes 12292
  240.2 71.8 %copy-start.83 = (f32[1024]{0:T(1024)}, f32[1024]{0:T(1024)S(1)}, u32[]{:S(2)}) copy-start(f32[1024]{0:T(1024)S(1)} %multiply_reduce_fusion.14) | copy-start | bytes 12292
  240.2 126.2 %copy-start.95 = (f32[1024]{0:T(1024)}, f32[1024]{0:T(1024)S(1)}, u32[]{:S(2)}) copy-start(f32[1024]{0:T(1024)S(1)} %fusion.140) | copy-start | bytes 12292
  240.2 126.2 %copy-start.102 = (f32[3072]{0:T(1024)S(1)}, f32[3072]{0:T(1024)}, u32[]{:S(2)}) copy-start(f32[3072]{0:T(1024)} %convert_element_type.273) | copy-start | bytes 36868
  240.2 126.2 %copy-start.115 = (f32[768]{0:T(1024)S(1)}, f32[768]{0:T(1024)}, u32[]{:S(2)}) copy-start(f32[768]{0:T(1024)} %convert_element_type.275) | copy-start | bytes 9220
  436.8 56.4 %copy-start.30 = (f32[1024,768]{1,0:T(8,128)}, f32[1024,768]{1,0:T(8,128)S(1)}, u32[]{:S(2)}) copy-start(f32[1024,768]{1,0:T(8,128)S(1)} %get-tuple-element.482) | copy-start | bytes 9437188
  436.8 56.4 %copy-start.79 = (f32[1024]{0:T(1024)}, f32[1024]{0:T(1024)S(1)}, u32[]{:S(2)}) copy-start(f32[1024]{0:T(1024)S(1)} %broadcast_multiply_fusion.2) | copy-start | bytes 12292
  613.3 202.8 %reduce-scatter.11.cloned.1.call-start = ((), (), s32[]{:S(2)}) async-start(), calls=%async_computation.14 | async-start | bytes 2433024 | tf_op jit(solution)/shard_map/reduce_scatter | solution.py:335
  681.7 238.3 %reduce-scatter.9.cloned.1.call-start = ((), (), s32[]{:S(2)}) async-start(), calls=%async_computation.13 | async-start | bytes 2433024 | tf_op jit(solution)/shard_map/reduce_scatter | solution.py:335
  690.0 334.7 %reduce-scatter.7.cloned.1.call-start = ((), (), s32[]{:S(2)}) async-start(), calls=%async_computation.12 | async-start | bytes 2433024 | tf_op jit(solution)/shard_map/reduce_scatter | solution.py:335
  698.4 467.3 %reduce-scatter.17.cloned.1.call-start = ((), (), s32[]{:S(2)}) async-start(), calls=%async_computation.17 | async-start | bytes 9732096 | tf_op jit(solution)/shard_map/reduce_scatter | solution.py:336
  718.9 588.5 %reduce-scatter.15.cloned.1.call-start = ((), (), s32[]{:S(2)}) async-start(), calls=%async_computation.16 | async-start | bytes 9732096 | tf_op jit(solution)/shard_map/reduce_scatter | solution.py:336
  (144 other events, 824.2 us)
Sparse Core Ops, SparseCore 0:
  10.9 56.9 all-gather.6
  70.8 53.0 all-gather.8
  126.8 53.0 all-gather.10
  182.7 53.0 all-gather.12
  238.6 62.5 all-gather.14
  303.9 62.4 all-gather.16
  613.4 97.8 reduce-scatter.12
  718.1 97.9 reduce-scatter.10
  822.0 97.9 reduce-scatter.8
  926.6 98.0 reduce-scatter.6
  1031.1 134.4 reduce-scatter.16
  1173.0 134.4 reduce-scatter.14
where the time goes:
time: 1320 us; the launch traced here: 1310 us
  waiting for transfers between devices  745 us (56%)
  matrix products  287 us (22%)
  local copies, waits for them, and re-layouts  114 us (9%)
  blocking collectives  83.3 us (6%)
  other arithmetic  65.8 us (5%)
  between operations  17.2 us (1%)
    reduce_scatter x2, waiting for transfers between devices, body(): lax.psum_scatter(feed_total, ('dp', 'fsdp'), scatter_dimension=0, tiled=T...  283 us
    reduce_scatter x4, waiting for transfers between devices, body(): lax.psum_scatter(mixer_total, ('dp', 'fsdp'), scatter_dimension=0, tiled=...  225 us
    unnamed x2, blocking collectives  83.3 us
    dot_general x12, matrix products, project(): lax.dot_general(inputs, weight, (((1,), (1,)), ((), ())), preferred_eleme...  67.3 us
    dot_general x12, matrix products, back_project(): return jnp.dot(grad_low, weight, preferred_element_type=jnp.float32)  66.7 us
    all_gather x1, waiting for transfers between devices, body(): lax.all_gather(up_weight, ('dp', 'fsdp'), axis=0, tiled=True)  60.9 us
    dot_general x12, matrix products, weight_grad(): lax.dot_general(grad_low, inputs, (((0,), (0,)), ((), ())), preferred_ele...  59.5 us
    all_gather x1, waiting for transfers between devices, body(): lax.all_gather(down_weight, ('dp', 'fsdp'), axis=0, tiled=True)  54.5 us
  transfers between devices with their start and end apart: 12, of which 10 were waited for; matrix products, arithmetic and copies ran while one was open for 16% of the time, Pallas kernels for 0%

commit v1 on v0

v1 whole, which is shorter than its diff:
```python
from functools import partial
import math

import jax
import jax.numpy as jnp
from jax import lax
from jax.experimental import pallas as pl
from jax.experimental.pallas import tpu as pltpu
from jax.sharding import PartitionSpec as P

HEAD = 64
LAYERS = 2
QUAD = 4 * HEAD
TILE = 256
norm_eps = 1e-06
masked_score = -1000000000.0
VMEM = 60 * 1024 * 1024
bf16 = jnp.bfloat16
f32 = jnp.float32

QB, VB, OB, G1, S1, DB, G2, S2 = range(8)


def dot_nt(left, right):
    return lax.dot_general(left, right, (((1,), (1,)), ((), ())), preferred_element_type=f32)


def dot_nn(left, right):
    return lax.dot_general(left, right, (((1,), (0,)), ((), ())), preferred_element_type=f32)


def normalize(v):
    mean = jnp.mean(v, axis=-1, keepdims=True)
    centered = v - mean
    rstd = lax.rsqrt(jnp.mean(centered * centered, axis=-1, keepdims=True) + norm_eps)
    return centered * rstd, rstd


def normalize_back(grad, gain, unit, rstd):
    scaled = grad * gain
    first = jnp.mean(scaled, axis=-1, keepdims=True)
    second = jnp.mean(scaled * unit, axis=-1, keepdims=True)
    return rstd * (scaled - first - unit * second)


def partial_sum(v):
    return jnp.sum(v.reshape(v.shape[0] // 8, 8, v.shape[1]), axis=0)


def piece_copies(core, pieces, place, sems, which=None):
    copies = []
    for index, piece in enumerate(pieces):
        source = piece if which is None else piece.at[which]
        _, rows, half = source.shape
        sibling, side = index // 2, index % 2
        for x in range(2):
            slot = 2 * x + (core if sibling == 0 else 1 - core)
            start = pl.multiple_of(slot * rows, rows)
            copies.append(
                pltpu.make_async_copy(
                    source.at[x],
                    place.at[pl.ds(start, rows), pl.ds(side * half, half)],
                    sems.at[index * 2 + x],
                )
            )
    return copies


def start_all(copies):
    for copy in copies:
        copy.start()


def wait_all(copies):
    for copy in copies:
        copy.wait()


def params():
    return pltpu.CompilerParams(vmem_limit_bytes=VMEM)


ANY = pl.BlockSpec(memory_space=pl.ANY)
SMEM = pl.BlockSpec(memory_space=pltpu.SMEM)


def whole(shape):
    return pl.BlockSpec(shape, lambda *_: (0,) * len(shape))


def mask_into(mask, seg_col, alive_col, seg_row):
    length = mask.shape[0]
    key = lax.broadcasted_iota(jnp.int32, (length, length), 0)
    query = lax.broadcasted_iota(jnp.int32, (length, length), 1)
    same = seg_col[:, 0:1] == seg_row[0]
    allowed = same & ((alive_col[:, 0:1] > 0) | (key == query))
    mask[...] = jnp.where(allowed, 0.0, masked_score)


def attend_forward_kernel(
    core_ref, x, seg_col, alive_col, seg_row, vecs, own_a, own_b, sib_a, sib_b,
    q_out, k_out, v_out, ctx_out, lse_out, weights, mask, sems,
):
    row, quad = pl.program_id(0), pl.program_id(1)
    core = core_ref[0]
    first = (row == 0) & (quad == 0)
    copies = [
        piece_copies(core, (own_a, own_b, sib_a, sib_b), weights.at[w], sems.at[w], w)
        for w in range(3)
    ]

    @pl.when(first)
    def _():
        for group in copies:
            start_all(group)

    @pl.when(quad == 0)
    def _():
        mask_into(mask, seg_col, alive_col, seg_row)

    @pl.when(first)
    def _():
        for group in copies:
            wait_all(group)

    inputs = x[...]
    heads = pl.ds(pl.multiple_of(quad * QUAD, QUAD), QUAD)
    queries = (dot_nt(inputs, weights[0, heads, :]) + vecs[QB : QB + 1, :]).astype(bf16)
    keys = dot_nt(inputs, weights[1, heads, :]).astype(bf16)
    values = (dot_nt(inputs, weights[2, heads, :]) + vecs[VB : VB + 1, :]).astype(bf16)
    q_out[...] = queries
    k_out[...] = keys
    v_out[...] = values
    scaled = queries * bf16(HEAD**-0.5)
    length = inputs.shape[0]
    lane = lax.broadcasted_iota(jnp.int32, (length, 2 * HEAD), 1)
    for pair in range(2):
        cols = slice(pair * 2 * HEAD, (pair + 1) * 2 * HEAD)
        kp, qp = keys[:, cols], scaled[:, cols]
        vt = values[:, cols].T
        parts = []
        for h in range(2):
            km = jnp.where((lane >= HEAD) if h else (lane < HEAD), kp, bf16(0))
            scores = dot_nt(km, qp) + mask[...]
            highest = jnp.max(scores, axis=0, keepdims=True)
            weight = jnp.exp(scores - highest)
            total = jnp.sum(weight, axis=0, keepdims=True)
            parts.append(dot_nn(vt[h * HEAD : (h + 1) * HEAD], weight.astype(bf16)) / total)
            lse_out[0, 0, pl.ds(2 * pair + h, 1), :] = highest + jnp.log(total)
        ctx_out[:, cols] = jnp.concatenate(parts, axis=0).T.astype(bf16)


def attend_forward(core, x, seg_col, alive_col, seg_row, vecs, qkv):
    count, width = x.shape
    rows, _, length = seg_row.shape
    quads = width // QUAD
    full = pl.BlockSpec((length, width), lambda r, j: (r, 0))
    col = pl.BlockSpec((length, 128), lambda r, j: (r, 0))
    block = pl.BlockSpec((length, QUAD), lambda r, j: (r, j))
    low = jax.ShapeDtypeStruct((count, width), bf16)
    return pl.pallas_call(
        attend_forward_kernel,
        grid=(rows, quads),
        in_specs=[SMEM, full, col, col, pl.BlockSpec((1, 1, length), lambda r, j: (r, 0, 0)),
                  pl.BlockSpec((8, QUAD), lambda r, j: (0, j)), ANY, ANY, ANY, ANY],
        out_specs=[block] * 4 + [pl.BlockSpec((1, 1, 8, length), lambda r, j: (r, j, 0, 0))],
        out_shape=[low] * 4 + [jax.ShapeDtypeStruct((rows, quads, 8, length), f32)],
        scratch_shapes=[
            pltpu.VMEM((3, width, width), bf16),
            pltpu.VMEM((length, length), f32),
            pltpu.SemaphoreType.DMA((3, 8)),
        ],
        compiler_params=params(),
        cost_estimate=pl.CostEstimate(
            flops=2 * count * width * width * 3 + 4 * 4 * count * length * width,
            bytes_accessed=count * width * 10 + 3 * width * width * 2, transcendentals=0),
        name="attend_forward",
    )(core, x, seg_col, alive_col, seg_row, vecs, *qkv)


GELU_A = math.sqrt(2.0 / math.pi)
GELU_B = 0.044715


def gelu_both(u):
    square = u * u
    t = jnp.tanh(u * (GELU_A + (GELU_A * GELU_B) * square))
    half = 0.5 + 0.5 * t
    slope = half + (u * (1.0 - t * t)) * (0.5 * GELU_A + (1.5 * GELU_A * GELU_B) * square)
    return u * half, slope


def widen_kernel(
    top, core_ref, ctx, resid, vecs, up_bias, oo_a, oo_b, os_a, os_b, uo_a, uo_b, us_a, us_b,
    mixed_out, low_out, act_out, slope_out, out_weight, up_weight, sems,
):
    core = core_ref[0]
    first = pl.program_id(0) == 0
    out_copies = piece_copies(core, (oo_a, oo_b, os_a, os_b), out_weight, sems.at[0])
    up_copies = piece_copies(core, (uo_a, uo_b, us_a, us_b), up_weight, sems.at[1])

    @pl.when(first)
    def _():
        start_all(out_copies)
        start_all(up_copies)
        wait_all(out_copies)

    if top:
        hidden = normalize(resid[...])[0] * vecs[G2 : G2 + 1, :] + vecs[S2 : S2 + 1, :]
    else:
        hidden = resid[...].astype(f32)
    mixed = hidden + dot_nt(ctx[...], out_weight[...]) + vecs[OB : OB + 1, :]
    mixed_out[...] = mixed
    normed = normalize(mixed)[0] * vecs[G1 : G1 + 1, :] + vecs[S1 : S1 + 1, :]
    low = normed.astype(bf16)
    low_out[...] = low

    @pl.when(first)
    def _():
        wait_all(up_copies)

    width = low.shape[1]
    for chunk in range(up_weight.shape[0] // width):
        cols = slice(chunk * width, (chunk + 1) * width)
        upward = dot_nt(low, up_weight[cols, :]) + up_bias[0:1, cols]
        act, slope = gelu_both(upward)
        act_out[:, cols] = act.astype(bf16)
        slope_out[:, cols] = slope.astype(bf16)


def widen(top, core, ctx, resid, vecs, up_bias, out_weight, up_weight):
    count, width = ctx.shape
    wide = up_bias.shape[1]
    tile = pl.BlockSpec((TILE, width), lambda i: (i, 0))
    broad = pl.BlockSpec((TILE, wide), lambda i: (i, 0))
    return pl.pallas_call(
        partial(widen_kernel, top),
        grid=(count // TILE,),
        in_specs=[SMEM, tile, tile, whole((8, width)), whole((8, wide))] + [ANY] * 8,
        out_specs=[tile, tile, broad, broad],
        out_shape=[
            jax.ShapeDtypeStruct((count, width), f32),
            jax.ShapeDtypeStruct((count, width), bf16),
            jax.ShapeDtypeStruct((count, wide), bf16),
            jax.ShapeDtypeStruct((count, wide), bf16),
        ],
        scratch_shapes=[
            pltpu.VMEM((width, width), bf16),
            pltpu.VMEM((wide, width), bf16),
            pltpu.SemaphoreType.DMA((2, 8)),
        ],
        compiler_params=params(),
        cost_estimate=pl.CostEstimate(
            flops=2 * count * width * (width + wide),
            bytes_accessed=count * (width * 12 + wide * 4), transcendentals=0),
        name="widen",
    )(core, ctx, resid, vecs, up_bias, *out_weight, *up_weight)


def narrow_kernel(core_ref, act, mixed, vecs, do_a, do_b, ds_a, ds_b, combined_out, low_out, down_weight, sems):
    core = core_ref[0]
    copies = piece_copies(core, (do_a, do_b, ds_a, ds_b), down_weight, sems)

    @pl.when(pl.program_id(0) == 0)
    def _():
        start_all(copies)
        wait_all(copies)

    normed = normalize(mixed[...])[0] * vecs[G1 : G1 + 1, :] + vecs[S1 : S1 + 1, :]
    combined = normed + dot_nt(act[...], down_weight[...]) + vecs[DB : DB + 1, :]
    combined_out[...] = combined
    hidden = normalize(combined)[0] * vecs[G2 : G2 + 1, :] + vecs[S2 : S2 + 1, :]
    low_out[...] = hidden.astype(bf16)


def narrow(core, act, mixed, vecs, down_weight):
    count, width = mixed.shape
    wide = act.shape[1]
    tile = pl.BlockSpec((TILE, width), lambda i: (i, 0))
    broad = pl.BlockSpec((TILE, wide), lambda i: (i, 0))
    return pl.pallas_call(
        narrow_kernel,
        grid=(count // TILE,),
        in_specs=[SMEM, broad, tile, whole((8, width))] + [ANY] * 4,
        out_specs=[tile, tile],
        out_shape=[jax.ShapeDtypeStruct((count, width), f32), jax.ShapeDtypeStruct((count, width), bf16)],
        scratch_shapes=[pltpu.VMEM((width, wide), bf16), pltpu.SemaphoreType.DMA((8,))],
        compiler_params=params(),
        cost_estimate=pl.CostEstimate(
            flops=2 * count * width * wide, bytes_accessed=count * (width * 10 + wide * 2), transcendentals=0),
        name="narrow",
    )(core, act, mixed, vecs, *down_weight)


def add_rows(out, first, values):
    @pl.when(first)
    def _():
        out[...] = jnp.zeros_like(out)

    for index, value in enumerate(values):
        out[index] += partial_sum(value)


def narrow_top_kernel(
    core_ref, act, mixed, vecs, cot, alive_col, do_a, do_b, ds_a, ds_b,
    outputs, gc_out, gb_out, sums, down_weight, sems,
):
    core = core_ref[0]
    first = pl.program_id(0) == 0
    copies = piece_copies(core, (do_a, do_b, ds_a, ds_b), down_weight, sems)

    @pl.when(first)
    def _():
        start_all(copies)
        wait_all(copies)

    normed = normalize(mixed[...])[0] * vecs[G1 : G1 + 1, :] + vecs[S1 : S1 + 1, :]
    combined = normed + dot_nt(act[...], down_weight[...]) + vecs[DB : DB + 1, :]
    unit, rstd = normalize(combined)
    gain = vecs[G2 : G2 + 1, :]
    alive = alive_col[:, 0:1].astype(f32)
    outputs[...] = ((unit * gain + vecs[S2 : S2 + 1, :]) * alive).astype(bf16)
    grad = cot[...].astype(f32) * alive
    grad_combined = normalize_back(grad, gain, unit, rstd)
    branch = grad_combined.astype(bf16)
    gc_out[...] = grad_combined
    gb_out[...] = branch
    add_rows(sums, first, (grad * unit, grad, branch.astype(f32)))


def narrow_top(core, act, mixed, vecs, cot, alive_col, down_weight):
    count, width = mixed.shape
    wide = act.shape[1]
    tile = pl.BlockSpec((TILE, width), lambda i: (i, 0))
    broad = pl.BlockSpec((TILE, wide), lambda i: (i, 0))
    return pl.pallas_call(
        narrow_top_kernel,
        grid=(count // TILE,),
        in_specs=[SMEM, broad, tile, whole((8, width)), tile, pl.BlockSpec((TILE, 128), lambda i: (i, 0))] + [ANY] * 4,
        out_specs=[tile, tile, tile, whole((3, 8, width))],
        out_shape=[
            jax.ShapeDtypeStruct((count, width), bf16),
            jax.ShapeDtypeStruct((count, width), f32),
            jax.ShapeDtypeStruct((count, width), bf16),
            jax.ShapeDtypeStruct((3, 8, width), f32),
        ],
        scratch_shapes=[pltpu.VMEM((width, wide), bf16), pltpu.SemaphoreType.DMA((8,))],
        compiler_params=params(),
        cost_estimate=pl.CostEstimate(
            flops=2 * count * width * wide, bytes_accessed=count * (width * 14 + wide * 2), transcendentals=0),
        name="narrow_top",
    )(core, act, mixed, vecs, cot, alive_col, *down_weight)


def feed_back_kernel(
    core_ref, gb, gc, slope, mixed, vecs, do_a, do_b, ds_a, ds_b, uo_a, uo_b, us_a, us_b, oo_a, oo_b, os_a, os_b,
    gu_out, gm_out, ga_out, gctx_out, sums, up_sums, down_weight, up_weight, out_weight, sems,
):
    core = core_ref[0]
    first = pl.program_id(0) == 0
    down_copies = piece_copies(core, (do_a, do_b, ds_a, ds_b), down_weight, sems.at[0])
    up_copies = piece_copies(core, (uo_a, uo_b, us_a, us_b), up_weight, sems.at[1])
    out_copies = piece_copies(core, (oo_a, oo_b, os_a, os_b), out_weight, sems.at[2])

    @pl.when(first)
    def _():
        start_all(down_copies)
        start_all(up_copies)
        start_all(out_copies)
        up_sums[...] = jnp.zeros_like(up_sums)
        wait_all(down_copies)
        wait_all(up_copies)

    branch = gb[...]
    grad_normed = gc[...]
    width = branch.shape[1]
    for chunk in range(up_weight.shape[0] // width):
        cols = slice(chunk * width, (chunk + 1) * width)
        grad_up = (dot_nn(branch, down_weight[:, cols]) * slope[:, cols].astype(f32)).astype(bf16)
        gu_out[:, cols] = grad_up
        up_sums[:, cols] += partial_sum(grad_up.astype(f32))
        grad_normed = grad_normed + dot_nn(grad_up, up_weight[cols, :])
    unit, rstd = normalize(mixed[...])
    grad_mixed = normalize_back(grad_normed, vecs[G1 : G1 + 1, :], unit, rstd)
    gm_out[...] = grad_mixed
    attn = grad_mixed.astype(bf16)
    ga_out[...] = attn
    add_rows(sums, first, (grad_normed * unit, grad_normed, attn.astype(f32)))

    @pl.when(first)
    def _():
        wait_all(out_copies)

    gctx_out[...] = dot_nn(attn, out_weight[...]).astype(bf16)


def feed_back(core, gb, gc, slope, mixed, vecs, down_weight, up_weight, out_weight):
    count, width = mixed.shape
    wide = slope.shape[1]
    tile = pl.BlockSpec((TILE, width), lambda i: (i, 0))
    broad = pl.BlockSpec((TILE, wide), lambda i: (i, 0))
    return pl.pallas_call(
        feed_back_kernel,
        grid=(count // TILE,),
        in_specs=[SMEM, tile, tile, broad, tile, whole((8, width))] + [ANY] * 12,
        out_specs=[broad, tile, tile, tile, whole((3, 8, width)), whole((8, wide))],
        out_shape=[
            jax.ShapeDtypeStruct((count, wide), bf16),
            jax.ShapeDtypeStruct((count, width), f32),
            jax.ShapeDtypeStruct((count, width), bf16),
            jax.ShapeDtypeStruct((count, width), bf16),
            jax.ShapeDtypeStruct((3, 8, width), f32),
            jax.ShapeDtypeStruct((8, wide), f32),
        ],
        scratch_shapes=[
            pltpu.VMEM((width, wide), bf16),
            pltpu.VMEM((wide, width), bf16),
            pltpu.VMEM((width, width), bf16),
            pltpu.SemaphoreType.DMA((3, 8)),
        ],
        compiler_params=params(),
        cost_estimate=pl.CostEstimate(
            flops=2 * count * width * (width + 2 * wide),
            bytes_accessed=count * (width * 20 + wide * 4), transcendentals=0),
        name="feed_back",
    )(core, gb, gc, slope, mixed, vecs, *down_weight, *up_weight, *out_weight)


def attend_back_kernel(
    q, k, v, gctx, lse, seg_col, alive_col, seg_row, grads, sums, mask,
):
    @pl.when(pl.program_id(1) == 0)
    def _():
        mask_into(mask, seg_col, alive_col, seg_row)

    length = q.shape[0]
    lane = lax.broadcasted_iota(jnp.int32, (length, 2 * HEAD), 1)
    scaling = HEAD**-0.5
    for pair in range(2):
        cols = slice(pair * 2 * HEAD, (pair + 1) * 2 * HEAD)
        kp, vp, go = k[:, cols], v[:, cols], gctx[:, cols]
        qp = q[:, cols] * bf16(scaling)
        kt = kp.T
        dq_parts = []
        dk = dv = None
        for h in range(2):
            here = (lane >= HEAD) if h else (lane < HEAD)
            zero = bf16(0)
            qm, gm = jnp.where(here, qp, zero), jnp.where(here, go, zero)
            scores = dot_nt(kp, qm) + mask[...]
            probs = jnp.exp(scores - lse[0, 0, pl.ds(2 * pair + h, 1), :])
            weighted = probs * dot_nt(vp, gm)
            inner = jnp.sum(weighted, axis=0, keepdims=True)
            grad_scores = (weighted - probs * inner).astype(bf16)
            dv_h = dot_nn(probs.astype(bf16), gm)
            dk_h = dot_nn(grad_scores, qm)
            dv = dv_h if dv is None else dv + dv_h
            dk = dk_h if dk is None else dk + dk_h
            dq_parts.append(dot_nn(kt[h * HEAD : (h + 1) * HEAD], grad_scores))
        dq = (jnp.concatenate(dq_parts, axis=0).T * scaling).astype(bf16)
        dv = dv.astype(bf16)
        grads[0, :, cols] = dq
        grads[1, :, cols] = dk.astype(bf16)
        grads[2, :, cols] = dv
        sums[0, 0, :, cols] = partial_sum(dq.astype(f32))
        sums[0, 1, :, cols] = partial_sum(dv.astype(f32))


def attend_back(q, k, v, gctx, lse, seg_col, alive_col, seg_row):
    count, width = q.shape
    rows, _, length = seg_row.shape
    col = pl.BlockSpec((length, 128), lambda r, j: (r, 0))
    block = pl.BlockSpec((length, QUAD), lambda r, j: (r, j))
    return pl.pallas_call(
        attend_back_kernel,
        grid=(rows, width // QUAD),
        in_specs=[block] * 4 + [pl.BlockSpec((1, 1, 8, length), lambda r, j: (r, j, 0, 0)), col, col,
                                pl.BlockSpec((1, 1, length), lambda r, j: (r, 0, 0))],
        out_specs=[pl.BlockSpec((3, length, QUAD), lambda r, j: (0, r, j)),
                   pl.BlockSpec((1, 2, 8, QUAD), lambda r, j: (r, 0, 0, j))],
        out_shape=[jax.ShapeDtypeStruct((3, count, width), bf16), jax.ShapeDtypeStruct((rows, 2, 8, width), f32)],
        scratch_shapes=[pltpu.VMEM((length, length), f32)],
        compiler_params=params(),
        cost_estimate=pl.CostEstimate(
            flops=4 * 10 * count * length * width, bytes_accessed=count * width * 16, transcendentals=0),
        name="attend_back",
    )(q, k, v, gctx, lse, seg_col, alive_col, seg_row)


def input_back_kernel(below, core_ref, grads, gm, *rest):
    if below:
        combined, vecs, own_a, own_b, sib_a, sib_b, gc_out, gb_out, sums, weights, sems = rest
    else:
        own_a, own_b, sib_a, sib_b, grad_out, weights, sems = rest
    core = core_ref[0]
    first = pl.program_id(0) == 0
    copies = [
        piece_copies(core, (own_a, own_b, sib_a, sib_b), weights.at[w], sems.at[w], w)
        for w in range(3)
    ]

    @pl.when(first)
    def _():
        for group in copies:
            start_all(group)
        for group in copies:
            wait_all(group)

    grad = gm[...]
    for w in range(3):
        grad = grad + dot_nn(grads[w], weights[w])
    if below:
        unit, rstd = normalize(combined[...])
        grad_combined = normalize_back(grad, vecs[G2 : G2 + 1, :], unit, rstd)
        branch = grad_combined.astype(bf16)
        gc_out[...] = grad_combined
        gb_out[...] = branch
        add_rows(sums, first, (grad * unit, grad, branch.astype(f32)))
    else:
        grad_out[...] = grad


def input_back(core, grads, gm, qkv, combined=None, vecs=None):
    count, width = gm.shape
    below = combined is not None
    tile = pl.BlockSpec((TILE, width), lambda i: (i, 0))
    high = jax.ShapeDtypeStruct((count, width), f32)
    extra, extra_specs = ((combined, vecs), [tile, whole((8, width))]) if below else ((), [])
    out_specs, out_shape = [tile], [high]
    if below:
        out_specs += [tile, whole((3, 8, width))]
        out_shape += [jax.ShapeDtypeStruct((count, width), bf16), jax.ShapeDtypeStruct((3, 8, width), f32)]
    return pl.pallas_call(
        partial(input_back_kernel, below),
        grid=(count // TILE,),
        in_specs=[SMEM, pl.BlockSpec((3, TILE, width), lambda i: (0, i, 0)), tile] + extra_specs + [ANY] * 4,
        out_specs=out_specs,
        out_shape=out_shape,
        scratch_shapes=[pltpu.VMEM((3, width, width), bf16), pltpu.SemaphoreType.DMA((3, 8))],
        compiler_params=params(),
        cost_estimate=pl.CostEstimate(
            flops=2 * count * width * width * 3, bytes_accessed=count * width * 14, transcendentals=0),
        name="input_back",
    )(core, grads, gm, *extra, *qkv)


def weight_grad_kernel(layers, place_ref, *refs):
    grads, inputs = refs[:layers], refs[layers : 2 * layers]
    keep, send, turned = refs[2 * layers :]
    core, flip = place_ref[0], place_ref[1]
    rows = turned.shape[0] // 4
    span = grads[0].shape[-2]

    @pl.when(pl.program_id(1) == 0)
    def _():
        for layer in range(layers):
            flat = grads[layer][0].T
            for block in range(4):
                x, c = block // 2, block % 2
                slot = 2 * ((x + flip) % 2) + (c + core) % 2
                turned[pl.ds(pl.multiple_of(slot * rows, rows), rows), layer * span : (layer + 1) * span] = (
                    flat[block * rows : (block + 1) * rows]
                )

    total = None
    for layer in range(layers):
        term = dot_nn(turned[:, layer * span : (layer + 1) * span], inputs[layer][...])
        total = term if total is None else total + term
    total = total.astype(bf16)
    halves = keep.shape[1]
    wide = keep.shape[-1]
    for half in range(halves):
        for x in range(2):
            for c, out in ((0, keep), (1, send)):
                start = (2 * x + c) * rows
                out[0, half, x] = total[start : start + rows, half * wide : (half + 1) * wide]


def weight_grad(place, grads, inputs):
    layers = len(grads)
    count_w, span, n = grads[0].shape
    depth = inputs[0].shape[1]
    chunk = min(depth, n)
    chunks = depth // chunk
    halves = 2 if chunks == 1 else 1
    wide = chunk // halves
    per_half = depth // 2 // wide
    rows = n // 4
    if chunks == 1:
        out_spec = pl.BlockSpec((1, 2, 2, rows, wide), lambda w, j: (w, 0, 0, 0, 0))
    else:
        out_spec = pl.BlockSpec((1, 1, 2, rows, wide), lambda w, j: (w, j // per_half, 0, 0, j % per_half))
    out = jax.ShapeDtypeStruct((count_w, 2, 2, rows, depth // 2), bf16)
    return pl.pallas_call(
        partial(weight_grad_kernel, layers),
        grid=(count_w, chunks),
        in_specs=[SMEM] + [pl.BlockSpec((1, span, n), lambda w, j: (w, 0, 0))] * layers
        + [pl.BlockSpec((span, chunk), lambda w, j: (0, j))] * layers,
        out_specs=[out_spec, out_spec],
        out_shape=[out, out],
        scratch_shapes=[pltpu.VMEM((n, layers * span), bf16)],
        compiler_params=params(),
        cost_estimate=pl.CostEstimate(
            flops=2 * layers * span * n * depth * count_w,
            bytes_accessed=2 * layers * span * (n * count_w + depth) + 2 * n * depth * count_w, transcendentals=0),
        name="weight_grad",
    )(place, *grads, *inputs)


def tall_grad_kernel(layers, place_ref, *refs):
    grads, inputs = refs[:layers], refs[layers : 2 * layers]
    keep, send = refs[2 * layers :]
    total = None
    for layer in range(layers):
        term = dot_nn(grads[layer][...].T, inputs[layer][...])
        total = term if total is None else total + term
    total = total.astype(bf16)
    wide = keep.shape[-1]

    for c, out in ((0, keep), (1, send)):
        @pl.when(pl.program_id(1) == c)
        def _():
            for half in range(2):
                out[half, 0] = total[:, half * wide : (half + 1) * wide]


def tall_grad(place, grads, inputs):
    layers = len(grads)
    span, n = grads[0].shape
    depth = inputs[0].shape[1]
    rows = n // 4

    def column(x, c, place):
        return 0, 2 * ((x + place[1]) % 2) + (c + place[0]) % 2

    out_spec = pl.BlockSpec((2, 1, rows, depth // 2), lambda x, c, place: (0, x, 0, 0))
    out = jax.ShapeDtypeStruct((2, 2, rows, depth // 2), bf16)
    return pl.pallas_call(
        partial(tall_grad_kernel, layers),
        grid_spec=pltpu.PrefetchScalarGridSpec(
            num_scalar_prefetch=1,
            grid=(2, 2),
            in_specs=[pl.BlockSpec((span, rows), column)] * layers
            + [pl.BlockSpec((span, depth), lambda x, c, place: (0, 0))] * layers,
            out_specs=[out_spec, out_spec],
        ),
        out_shape=[out, out],
        compiler_params=params(),
        cost_estimate=pl.CostEstimate(
            flops=2 * layers * span * n * depth,
            bytes_accessed=2 * layers * span * (n + depth) + 2 * n * depth, transcendentals=0),
        name="tall_grad",
    )(place, *grads, *inputs)


AXES = ("dp", "fsdp")


def halves(v):
    middle = v.shape[-1] // 2
    return v[..., :middle], v[..., middle:]


def pack_vectors(parts):
    return jnp.concatenate(parts, axis=-1)


class Plain:
    def __init__(self, mesh):
        self.devices = math.prod(mesh.shape.values())

    def place(self):
        return jnp.zeros((2,), jnp.int32)

    def gather(self, shards, vector):
        def pieces(full):
            blocks = full.reshape(full.shape[:-2] + (2, 2, full.shape[-2] // 4, full.shape[-1]))
            own, sibling = blocks[..., 0, :, :], blocks[..., 1, :, :]
            return (*halves(own), *halves(sibling))

        def full(shard):
            return lax.all_gather(shard, AXES, axis=0, tiled=True)

        query, key, value, out, up, down = shards
        qkv = jnp.stack([full(query), full(key), full(value)])
        return (pieces(qkv), pieces(full(out)), pieces(full(up)), pieces(full(down))), full(vector[None])

    def scatter(self, keep, send):
        count, sides, xs, rows, half = keep.shape
        both = jnp.stack([keep, send], axis=3).astype(f32)
        full = jnp.moveaxis(both, 1, 4).reshape(count, xs * 2 * rows, sides * half)
        return lax.psum_scatter(full, AXES, scatter_dimension=1, tiled=True)

    def scatter_vector(self, vector):
        return lax.psum_scatter(vector, AXES, scatter_dimension=0, tiled=True)[0]


class Grid:
    def __init__(self, mesh):
        pass

    def where(self):
        dp, fsdp = lax.axis_index("dp"), lax.axis_index("fsdp")
        return dp // 2, dp % 2, fsdp // 2, fsdp % 2

    def place(self):
        x, core, _, _ = self.where()
        return jnp.stack([core, x]).astype(jnp.int32)

    def swap(self, value, x=0, core=0, z=0, y=0):
        flip = ((x * 2 + core) * 4 + z) * 2 + y
        return lax.ppermute(value, AXES, [(i, i ^ flip) for i in range(32)])

    def ordered(self, mine, other, side, axis=0):
        return jnp.stack([jnp.where(side == 0, mine, other), jnp.where(side == 0, other, mine)], axis=axis)

    def spread(self, payload):
        x, _, z, y = self.where()
        parts = [payload] + [self.swap(payload, z=k) for k in range(1, 4)]
        odd, high = z % 2, z // 2
        parts = [jnp.where(odd == 0, parts[k], parts[k ^ 1]) for k in range(4)]
        parts = jnp.stack([jnp.where(high == 0, parts[k], parts[k ^ 2]) for k in range(4)])
        left, right = halves(parts)
        left_x = self.ordered(left, self.swap(left, x=1), x)
        right_y = self.ordered(right, self.swap(right, y=1), y, axis=1)
        left_xy = self.ordered(left_x, self.swap(left_x, y=1), y, axis=2)
        right_xy = self.ordered(right_y, self.swap(right_y, x=1), x)
        return left_xy, right_xy, parts

    def pieces(self, left, right, start, rows):
        def section(v):
            v = v[:, :, :, start : start + rows]
            return v.reshape(2, 8 * rows, v.shape[-1])

        return section(left), section(right)

    def with_sibling(self, left, right):
        return left, right, self.swap(left, core=1), self.swap(right, core=1)

    def gather(self, shards, vector):
        query, key, value, out, up, down = shards
        _, core, _, _ = self.where()
        small, width = query.shape
        tail = jnp.zeros((8, width), bf16).at[0, : vector.shape[0]].set(vector)
        left, right, token = self.spread(jnp.concatenate([query, key, value, tail], axis=0))
        stack = [self.pieces(left, right, w * small, small) for w in range(3)]
        qkv = self.with_sibling(jnp.stack([s[0] for s in stack]), jnp.stack([s[1] for s in stack]))
        mine = left[:, :, :, 3 * small, : vector.shape[0]].reshape(2, 8, -1)
        vectors = self.ordered(mine, self.swap(mine, core=1), core, axis=1).reshape(32, -1)
        second = jnp.concatenate([out, up], axis=0)
        second, token = lax.optimization_barrier((second, token))
        left, right, token = self.spread(second)
        out_w = self.with_sibling(*self.pieces(left, right, 0, out.shape[0]))
        up_w = self.with_sibling(*self.pieces(left, right, out.shape[0], up.shape[0]))
        down, token = lax.optimization_barrier((down, token))
        left, right, _ = self.spread(down)
        down_w = self.with_sibling(*self.pieces(left, right, 0, down.shape[0]))
        return (qkv, out_w, up_w, down_w), vectors

    def scatter(self, keep, send):
        _, _, z, y = self.where()
        count, _, _, rows, half = keep.shape
        mine = rows // 8

        def add(a, b):
            return (a.astype(f32) + b.astype(f32)).astype(bf16)

        def pick(v, index, axis):
            return lax.dynamic_index_in_dim(v, index, axis, keepdims=False)

        total = add(keep, self.swap(send, core=1)).reshape(count, 2, 2, 4, 2, mine, half)
        left, right = total[:, 0], total[:, 1]
        left = add(left[:, 0], self.swap(left[:, 1], x=1))
        right = add(pick(right, y, 3), self.swap(pick(right, 1 - y, 3), y=1))
        left = add(pick(left, y, 2), self.swap(pick(left, 1 - y, 2), y=1))
        right = add(right[:, 0], self.swap(right[:, 1], x=1))
        both = jnp.concatenate([left, right], axis=-1)
        result = pick(both, z, 1).astype(f32)
        for k in range(1, 4):
            result = result + self.swap(pick(both, z ^ k, 1), z=k).astype(f32)
        return result

    def scatter_vector(self, vector):
        x, core, z, y = self.where()

        def pick(v, index, axis):
            return lax.dynamic_index_in_dim(v, index, axis, keepdims=False)

        total = vector.reshape(2, 2, 4, 2, -1)
        total = pick(total, core, 1) + self.swap(pick(total, 1 - core, 1), core=1)
        total = pick(total, x, 0) + self.swap(pick(total, 1 - x, 0), x=1)
        total = pick(total, y, 1) + self.swap(pick(total, 1 - y, 1), y=1)
        result = pick(total, z, 0)
        for k in range(1, 4):
            result = result + self.swap(pick(total, z ^ k, 0), z=k)
        return result


def column_info(values, count):
    return jnp.broadcast_to(values.reshape(count, 1), (count, 128))


def body(
    exchange,
    tokens,
    cotangent,
    segment_ids,
    pad_mask,
    row_counts,
    query_weight,
    query_bias,
    key_weight,
    value_weight,
    value_bias,
    out_weight,
    out_bias,
    first_gain,
    first_shift,
    up_weight,
    up_bias,
    down_weight,
    down_bias,
    second_gain,
    second_shift,
):
    rows_here, row_len, width = tokens.shape
    count = rows_here * row_len
    present = (jnp.arange(rows_here, dtype=jnp.int32) < row_counts[0]).astype(jnp.int32)
    alive = pad_mask * present[:, None]
    alive_col = column_info(alive, count)
    seg_col = column_info(segment_ids, count)
    seg_row = segment_ids.reshape(rows_here, 1, row_len)
    place = exchange.place()

    mine = jnp.concatenate(
        [query_bias, value_bias, out_bias, first_gain, first_shift, down_bias, second_gain, second_shift, up_bias]
    )
    (qkv, out_w, up_w, down_w), vectors = exchange.gather(
        (query_weight, key_weight, value_weight, out_weight, up_weight, down_weight), mine
    )
    devices = vectors.shape[0]
    small = query_bias.shape[0]
    vectors = vectors.astype(f32)
    vecs = vectors[:, : 8 * small].reshape(devices, 8, small).transpose(1, 0, 2).reshape(8, width)
    wide = up_bias.shape[0] * devices
    up_vec = jnp.broadcast_to(vectors[:, 8 * small :].reshape(1, wide), (8, wide))

    flat = tokens.reshape(count, width)
    saved = []
    inputs, resid = flat, flat
    for layer in range(LAYERS):
        top = layer == LAYERS - 1
        queries, keys, values, context, lse = attend_forward(
            place, inputs, seg_col, alive_col, seg_row, vecs, qkv
        )
        mixed, low, act, slope = widen(layer > 0, place, context, resid, vecs, up_vec, out_w, up_w)
        kept = dict(inputs=inputs, q=queries, k=keys, v=values, ctx=context, lse=lse, mixed=mixed, low=low, act=act, slope=slope)
        if top:
            outputs, gc, gb, norm_sums = narrow_top(
                place, act, mixed, vecs, cotangent.reshape(count, width), alive_col, down_w
            )
        else:
            resid, inputs = narrow(place, act, mixed, vecs, down_w)
            kept["combined"] = resid
        saved.append(kept)

    terms = [[] for _ in range(4)]
    second_sums, first_sums, up_sums, bias_sums = 0, 0, 0, 0
    results = {}
    for layer in reversed(range(LAYERS)):
        kept = saved[layer]
        last = layer == 0
        second_sums = second_sums + norm_sums
        terms[0].append((gb, kept["act"]))
        if last:
            results["down"] = exchange.scatter(*weight_grad(place, [g[None] for g, _ in terms[0]], [v for _, v in terms[0]]))
        gu, gm, ga, gctx, sums, wide_sums = feed_back(
            place, gb, gc, kept["slope"], kept["mixed"], vecs, down_w, up_w, out_w
        )
        first_sums, up_sums = first_sums + sums, up_sums + wide_sums
        terms[1].append((gu, kept["low"]))
        terms[2].append((ga, kept["ctx"]))
        if last:
            keep, send = tall_grad(place, [g for g, _ in terms[1]], [v for _, v in terms[1]])
            results["up"] = exchange.scatter(keep[None], send[None])
            results["out"] = exchange.scatter(*weight_grad(place, [g[None] for g, _ in terms[2]], [v for _, v in terms[2]]))
        grads, sums = attend_back(
            kept["q"], kept["k"], kept["v"], gctx, kept["lse"], seg_col, alive_col, seg_row
        )
        bias_sums = bias_sums + jnp.sum(sums, axis=0)
        terms[3].append((grads, kept["inputs"]))
        if last:
            results["qkv"] = exchange.scatter(*weight_grad(place, [g for g, _ in terms[3]], [v for _, v in terms[3]]))
            (tokens_grad,) = input_back(place, grads, gm, qkv)
        else:
            gc, gb, norm_sums = input_back(place, grads, gm, qkv, saved[layer - 1]["combined"], vecs)

    bias_sums = jnp.sum(bias_sums, axis=1)
    first_sums = jnp.sum(first_sums, axis=1)
    second_sums = jnp.sum(second_sums, axis=1)
    up_sums = jnp.sum(up_sums, axis=0)
    stacked = jnp.stack(
        [bias_sums[0], bias_sums[1], first_sums[2], first_sums[0], first_sums[1], second_sums[2], second_sums[0], second_sums[1]]
    )
    vector = jnp.concatenate(
        [
            stacked.reshape(8, devices, small).transpose(1, 0, 2).reshape(devices, 8 * small),
            up_sums.reshape(devices, wide // devices),
        ],
        axis=1,
    )
    vector = exchange.scatter_vector(vector)
    piece = [vector[i * small : (i + 1) * small] for i in range(8)]
    query_grad, key_grad, value_grad = results["qkv"]
    return (
        outputs.reshape(rows_here, row_len, width),
        tokens_grad.reshape(rows_here, row_len, width),
        query_grad,
        piece[QB],
        key_grad,
        value_grad,
        piece[VB],
        results["out"][0],
        piece[OB],
        piece[G1],
        piece[S1],
        results["up"][0],
        vector[8 * small :],
        results["down"][0],
        piece[DB],
        piece[G2],
        piece[S2],
    )


def solution(mesh):
    rows = P(AXES, None, None)
    flat = P(AXES, None)
    line = P(AXES)
    matrices = (flat, line, flat, flat, line, flat, line, line, line, flat, line, flat, line, line, line)
    exchange = Grid(mesh) if dict(mesh.shape) == {"dp": 4, "fsdp": 8} else Plain(mesh)
    return jax.shard_map(
        partial(body, exchange),
        mesh=mesh,
        in_specs=(rows, rows, flat, flat, line) + matrices,
        out_specs=(rows, rows) + matrices,
        check_vma=False,
    )
```

time: 1320 us -> 505 us (0.38)
  waiting for transfers between devices: 745 us -> 96 us
  matrix products: 287 us -> 0 us
  Pallas kernels: 0 us -> 276 us
  local copies, waits for them, and re-layouts: 114 us -> 21.5 us
  blocking collectives: 83.3 us -> 0 us
  starting transfers between devices: 1.34 us -> 76.3 us
  other arithmetic: 65.8 us -> 24.1 us
  between operations: 17.2 us -> 3.21 us
    reduce_scatter x6 -> x0, waiting for transfers between devices: 508 us -> none  [the longest x2 283 us: body(): lax.psum_scatter(feed_total, ('dp', 'fsdp'), scatter_dimension=0, tiled=T...]
    dot_general x64 -> x0, matrix products: 287 us -> none  [the longest x12 67.3 us: project(): lax.dot_general(inputs, weight, (((1,), (1,)), ((), ())), preferred_eleme...]
    pallas_call x0 -> x16, Pallas kernels: none -> 276 us  [the longest x2 48.6 us: attend_back(): pl.pallas_call(attend_back_kernel, grid=(rows, width // QUAD), in_specs=[...]
    all_gather x6 -> x0, waiting for transfers between devices: 233 us -> none  [the longest x1 60.9 us: body(): lax.all_gather(up_weight, ('dp', 'fsdp'), axis=0, tiled=True)]
    ppermute x0 -> x68, waiting for transfers between devices: none -> 96 us  [swap(): return lax.ppermute(value, AXES, [(i, i ^ flip) for i in range(32)])]
    unnamed x2 -> x0, blocking collectives: 83.3 us -> none
    ppermute x0 -> x68, starting transfers between devices: none -> 76.3 us  [swap(): return lax.ppermute(value, AXES, [(i, i ^ flip) for i in range(32)])]
    while x72 -> x0, local copies, waits for them, and re-layouts: 38.1 us -> none  [the longest x8 17.2 us: mixer_backward(): lax.map(attend_backward, (queries.reshape(shape), key_rows.reshape(shape)...]
  transfers between devices with their start and end apart: 12 -> 68, of which waited for: 10 -> 23; matrix products, arithmetic and copies ran while one was open for 16% -> 7% of each run, Pallas kernels for 0% -> 23%
where the time goes in v1:
time: 505 us; the launch traced here: 498 us
  Pallas kernels  276 us (55%)
  waiting for transfers between devices  96 us (19%)
  starting transfers between devices  76.3 us (15%)
  other arithmetic  24.1 us (5%)
  local copies, waits for them, and re-layouts  21.5 us (4%)
    ppermute x68, waiting for transfers between devices, swap(): return lax.ppermute(value, AXES, [(i, i ^ flip) for i in range(32)])  96 us
    ppermute x68, starting transfers between devices, swap(): return lax.ppermute(value, AXES, [(i, i ^ flip) for i in range(32)])  76.3 us
    pallas_call x2, Pallas kernels, attend_back(): pl.pallas_call(attend_back_kernel, grid=(rows, width // QUAD), in_specs=[...  48.6 us
    pallas_call x2, Pallas kernels, feed_back(): pl.pallas_call(feed_back_kernel, grid=(count // TILE,), in_specs=[SMEM, t...  44.8 us
    pallas_call x2, Pallas kernels, attend_forward(): pl.pallas_call(attend_forward_kernel, grid=(rows, quads), in_specs=[SMEM,...  43.6 us
    pallas_call x3, Pallas kernels, weight_grad(): pl.pallas_call(partial(weight_grad_kernel, layers), grid=(count_w, chunks...  37.4 us
    pallas_call x2, Pallas kernels, widen(): pl.pallas_call(partial(widen_kernel, top), grid=(count // TILE,), in_spec...  37.1 us
    pallas_call x2, Pallas kernels, input_back(): pl.pallas_call(partial(input_back_kernel, below), grid=(count // TILE,),...  22 us
  transfers between devices with their start and end apart: 68, of which 23 were waited for; matrix products, arithmetic and copies ran while one was open for 7% of the time, Pallas kernels for 23%

profile of v1, /device:TPU:0, one launch (start us, length us, event | category | flops | bytes accessed | tf_op | source)
XLA Modules:
  0.0 497.5 jit_solution(10665142357759584621)
XLA Ops:
  0.7 6.1 %concatenate.32 = bf16[288]{0:T(512)(128)(2,1)S(1)} concatenate(bf16[24]{0:T(256)(128)(2,1)} %param.28, bf16[24]{0:T(256)(128)(2,1)} %param.31, bf16[24]{0:T(256)(128)(2,1)} %param.33, bf16[24]{0:T(256)(128)(2,1)} %param.34, bf16[24]{0:T(256)(128)(2,1)} %param.35, bf16[24]{0:T(256)(128)(2,1)} %param.39, bf16[24]{0:T(256)(128)(2,1)} %param.40, bf16[24]{0:T(256)(128)(2,1)} %param.41, ...), dimensions={0} | concatenate | bytes 1152 | tf_op jit(solution)/shard_map/concatenate | solution.py:835
  32.0 9.6 %collective-permute-done.11 = bf16[120,768]{1,0:T(8,128)(2,1)S(1)} collective-permute-done((bf16[120,768]{1,0:T(8,128)(2,1)S(1)}, bf16[120,768]{1,0:T(8,128)(2,1)S(1)}, u32[]{:S(2)}, u32[]{:S(2)}) %collective-permute-start.11) | collective-permute-done | bytes 184352 | tf_op jit(solution)/shard_map/ppermute | solution.py:712
  51.3 6.5 %collective-permute-done.22 = bf16[24,3072]{1,0:T(8,128)(2,1)S(1)} collective-permute-done((bf16[24,3072]{1,0:T(8,128)(2,1)S(1)}, bf16[24,3072]{1,0:T(8,128)(2,1)S(1)}, u32[]{:S(2)}, u32[]{:S(2)}) %collective-permute-start.22) | collective-permute-done | bytes 147488 | tf_op jit(solution)/shard_map/ppermute | solution.py:712
  64.4 11.4 %collective-permute-done.24 = bf16[4,24,1536]{2,1,0:T(8,128)(2,1)S(1)} collective-permute-done((bf16[4,24,1536]{2,1,0:T(8,128)(2,1)S(1)}, bf16[4,24,1536]{2,1,0:T(8,128)(2,1)S(1)}, u32[]{:S(2)}, u32[]{:S(2)}) %collective-permute-start.24) | collective-permute-done | bytes 294944 | tf_op jit(solution)/shard_map/ppermute | solution.py:712
  83.8 18.0 %collective-permute-done.27 = bf16[4,2,24,1536]{3,2,0,1:T(8,128)(2,1)} collective-permute-done((bf16[4,2,24,1536]{3,2,0,1:T(8,128)(2,1)S(1)}, bf16[4,2,24,1536]{3,2,0,1:T(8,128)(2,1)}, u32[]{:S(2)}, u32[]{:S(2)}) %collective-permute-start.27) | collective-permute-done | bytes 589856 | tf_op jit(solution)/shard_map/ppermute | solution.py:712
  117.4 21.9 %attend_forward.2 = (bf16[1024,768]{1,0:T(8,128)(2,1)}, bf16[1024,768]{1,0:T(8,128)(2,1)}, bf16[1024,768]{1,0:T(8,128)(2,1)}, bf16[1024,768]{1,0:T(8,128)(2,1)}, f32[2,3,8,512]{3,2,1,0:T(8,128)}) custom-call(s32[2]{0:T(128)} %pad_add_fusion.core_ref.place_ref, bf16[1024,768]{1,0:T(8,128)(2,1)} %bitcast.351, s32[1024,128]{1,0:T(8,128)} %broadcast_in_dim.40.seg_col, ...), custom_call_target="tpu_custom_call" | custom-call | flops 10066329600 | bytes 11403264 | tf_op jit(solution)/shard_map/attend_forward/pallas_call | solution.py:161
  140.1 18.2 %widen.2 = (f32[1024,768]{1,0:T(8,128)}, bf16[1024,768]{1,0:T(8,128)(2,1)}, bf16[1024,3072]{1,0:T(8,128)(2,1)}, bf16[1024,3072]{1,0:T(8,128)(2,1)}) custom-call(s32[2]{0:T(128)} %pad_add_fusion.core_ref.place_ref, bf16[1024,768]{1,0:T(8,128)(2,1)} %get-tuple-element.82.ctx.refs_3_, bf16[1024,768]{1,0:T(8,128)(2,1)} %bitcast.352, ...), custom_call_target="tpu_custom_call" | custom-call | flops 6039797760 | bytes 22020096 | tf_op jit(solution)/shard_map/widen/pallas_call | solution.py:236
  158.3 11.9 %narrow.1 = (f32[1024,768]{1,0:T(8,128)}, bf16[1024,768]{1,0:T(8,128)(2,1)}) custom-call(s32[2]{0:T(128)} %pad_add_fusion.core_ref.place_ref, bf16[1024,3072]{1,0:T(8,128)(2,1)} %get-tuple-element.84.act.refs_3_, f32[1024,768]{1,0:T(8,128)} %get-tuple-element.85.mixed, f32[8,768]{1,0:T(8,128)} %reshape.383.vecs.rest_1_, bf16[2,192,1536]{2,1,0:T(8,128)(2,1)} %bitcast.53.do_a, ...), custom_call_target="tpu_custom_call" | custom-call | flops 4831838208 | bytes 14155776 | tf_op jit(solution)/shard_map/narrow/pallas_call | solution.py:281
  170.2 21.7 %attend_forward.3 = (bf16[1024,768]{1,0:T(8,128)(2,1)}, bf16[1024,768]{1,0:T(8,128)(2,1)}, bf16[1024,768]{1,0:T(8,128)(2,1)}, bf16[1024,768]{1,0:T(8,128)(2,1)}, f32[2,3,8,512]{3,2,1,0:T(8,128)}) custom-call(s32[2]{0:T(128)} %pad_add_fusion.core_ref.place_ref, bf16[1024,768]{1,0:T(8,128)(2,1)} %get-tuple-element.87.x.refs_2_, ...), custom_call_target="tpu_custom_call" | custom-call | flops 10066329600 | bytes 11403264 | tf_op jit(solution)/shard_map/attend_forward/pallas_call | solution.py:161
  191.9 18.9 %widen.3 = (f32[1024,768]{1,0:T(8,128)}, bf16[1024,768]{1,0:T(8,128)(2,1)}, bf16[1024,3072]{1,0:T(8,128)(2,1)}, bf16[1024,3072]{1,0:T(8,128)(2,1)}) custom-call(s32[2]{0:T(128)} %pad_add_fusion.core_ref.place_ref, bf16[1024,768]{1,0:T(8,128)(2,1)} %get-tuple-element.88.ctx.refs_2_, f32[1024,768]{1,0:T(8,128)} %get-tuple-element.89.resid.rest_0_, ...), custom_call_target="tpu_custom_call" | custom-call | flops 6039797760 | bytes 22020096 | tf_op jit(solution)/shard_map/widen/pallas_call | solution.py:236
  210.8 14.8 %narrow_top.1 = (bf16[1024,768]{1,0:T(8,128)(2,1)}, f32[1024,768]{1,0:T(8,128)}, bf16[1024,768]{1,0:T(8,128)(2,1)}, f32[3,8,768]{2,1,0:T(8,128)}) custom-call(s32[2]{0:T(128)} %pad_add_fusion.core_ref.place_ref, bf16[1024,3072]{1,0:T(8,128)(2,1)} %get-tuple-element.90.act.refs_2_, f32[1024,768]{1,0:T(8,128)} %get-tuple-element.91.mixed, ...), custom_call_target="tpu_custom_call" | custom-call | flops 4831838208 | bytes 17301504 | tf_op jit(solution)/shard_map/narrow_top/pallas_call | solution.py:336
  225.7 22.4 %feed_back.2 = (bf16[1024,3072]{1,0:T(8,128)(2,1)}, f32[1024,768]{1,0:T(8,128)}, bf16[1024,768]{1,0:T(8,128)(2,1)}, bf16[1024,768]{1,0:T(8,128)(2,1)}, f32[3,8,768]{2,1,0:T(8,128)}, /*index=5*/f32[8,3072]{1,0:T(8,128)}) custom-call(s32[2]{0:T(128)} %pad_add_fusion.core_ref.place_ref, bf16[1024,768]{1,0:T(8,128)(2,1)} %get-tuple-element.99.gb, ...), custom_call_target="tpu_custom_call" | custom-call | flops 10871635968 | bytes 28311552 | tf_op jit(solution)/shard_map/feed_back/pallas_call | solution.py:402
  248.1 24.3 %attend_back.2 = (bf16[3,1024,768]{2,1,0:T(8,128)(2,1)}, f32[2,2,8,768]{3,2,1,0:T(8,128)}) custom-call(bf16[1024,768]{1,0:T(8,128)(2,1)} %get-tuple-element.96.q, bf16[1024,768]{1,0:T(8,128)(2,1)} %get-tuple-element.97.k, bf16[1024,768]{1,0:T(8,128)(2,1)} %get-tuple-element.98.v, bf16[1024,768]{1,0:T(8,128)(2,1)} %get-tuple-element.102.gctx, ...), custom_call_target="tpu_custom_call" | custom-call | flops 16106127360 | bytes 12582912 | tf_op jit(solution)/shard_map/attend_back/pallas_call | solution.py:474
  272.4 11.8 %input_back.2 = (f32[1024,768]{1,0:T(8,128)}, bf16[1024,768]{1,0:T(8,128)(2,1)}, f32[3,8,768]{2,1,0:T(8,128)}) custom-call(s32[2]{0:T(128)} %pad_add_fusion.core_ref.place_ref, bf16[3,1024,768]{2,1,0:T(8,128)(2,1)} %get-tuple-element.104.grads.refs_0_, f32[1024,768]{1,0:T(8,128)} %get-tuple-element.105.gm, f32[1024,768]{1,0:T(8,128)} %get-tuple-element.89.resid.rest_0_, ...), custom_call_target="tpu_custom_call" | custom-call | flops 3623878656 | bytes 11010048 | tf_op jit(solution)/shard_map/input_back/pallas_call | solution.py:533
  285.2 22.4 %feed_back.3 = (bf16[1024,3072]{1,0:T(8,128)(2,1)}, f32[1024,768]{1,0:T(8,128)}, bf16[1024,768]{1,0:T(8,128)(2,1)}, bf16[1024,768]{1,0:T(8,128)(2,1)}, f32[3,8,768]{2,1,0:T(8,128)}, /*index=5*/f32[8,3072]{1,0:T(8,128)}) custom-call(s32[2]{0:T(128)} %pad_add_fusion.core_ref.place_ref, bf16[1024,768]{1,0:T(8,128)(2,1)} %get-tuple-element.106.gb, ...), custom_call_target="tpu_custom_call" | custom-call | flops 10871635968 | bytes 28311552 | tf_op jit(solution)/shard_map/feed_back/pallas_call | solution.py:402
  308.6 15.6 %weight_grad.5 = (bf16[1,2,2,192,1536]{4,3,2,1,0:T(8,128)(2,1)}, bf16[1,2,2,192,1536]{4,3,2,1,0:T(8,128)(2,1)}) custom-call(s32[2]{0:T(128)} %pad_add_fusion.core_ref.place_ref, bf16[1,1024,768]{2,1,0:T(8,128)(2,1)} %bitcast.358, bf16[1,1024,768]{2,1,0:T(8,128)(2,1)} %bitcast.354, bf16[1024,3072]{1,0:T(8,128)(2,1)} %get-tuple-element.90.act.refs_2_, ...), custom_call_target="tpu_custom_call" | custom-call | flops 9663676416 | bytes 20447232 | tf_op jit(solution)/shard_map/weight_grad/pallas_call | solution.py:594
  324.8 24.3 %attend_back.3 = (bf16[3,1024,768]{2,1,0:T(8,128)(2,1)}, f32[2,2,8,768]{3,2,1,0:T(8,128)}) custom-call(bf16[1024,768]{1,0:T(8,128)(2,1)} %get-tuple-element.93.q, bf16[1024,768]{1,0:T(8,128)(2,1)} %get-tuple-element.94.k, bf16[1024,768]{1,0:T(8,128)(2,1)} %get-tuple-element.95.v, bf16[1024,768]{1,0:T(8,128)(2,1)} %get-tuple-element.109.gctx, ...), custom_call_target="tpu_custom_call" | custom-call | flops 16106127360 | bytes 12582912 | tf_op jit(solution)/shard_map/attend_back/pallas_call | solution.py:474
  350.8 7.4 %weight_grad.4 = (bf16[1,2,2,192,384]{4,3,2,1,0:T(8,128)(2,1)}, bf16[1,2,2,192,384]{4,3,2,1,0:T(8,128)(2,1)}) custom-call(s32[2]{0:T(128)} %pad_add_fusion.core_ref.place_ref, bf16[1,1024,768]{2,1,0:T(8,128)(2,1)} %bitcast.356, bf16[1,1024,768]{2,1,0:T(8,128)(2,1)} %bitcast.357, bf16[1024,768]{1,0:T(8,128)(2,1)} %get-tuple-element.88.ctx.refs_2_, ...), custom_call_target="tpu_custom_call" | custom-call | flops 2415919104 | bytes 7471104 | tf_op jit(solution)/shard_map/weight_grad/pallas_call | solution.py:594
  360.1 16.2 %tall_grad.1 = (bf16[2,2,768,384]{3,2,1,0:T(8,128)(2,1)}, bf16[2,2,768,384]{3,2,1,0:T(8,128)(2,1)}) custom-call(s32[2]{0:T(128)} %pad_add_fusion.core_ref.place_ref, bf16[1024,3072]{1,0:T(8,128)(2,1)} %get-tuple-element.127.refs_0_, bf16[1024,3072]{1,0:T(8,128)(2,1)} %get-tuple-element.128.refs_1_, bf16[1024,768]{1,0:T(8,128)(2,1)} %get-tuple-element.129.refs_2_, ...), custom_call_target="tpu_custom_call" | custom-call | flops 9663676416 | bytes 20447232 | tf_op jit(solution)/shard_map/tall_grad/pallas_call | solution.py:638
  378.0 14.4 %weight_grad.3 = (bf16[3,2,2,192,384]{4,3,2,1,0:T(8,128)(2,1)}, bf16[3,2,2,192,384]{4,3,2,1,0:T(8,128)(2,1)}) custom-call(s32[2]{0:T(128)} %pad_add_fusion.core_ref.place_ref, bf16[3,1024,768]{2,1,0:T(8,128)(2,1)} %get-tuple-element.104.grads.refs_0_, bf16[3,1024,768]{2,1,0:T(8,128)(2,1)} %get-tuple-element.111.grads.refs_1_, ...), custom_call_target="tpu_custom_call" | custom-call | flops 7247757312 | bytes 16121856 | tf_op jit(solution)/shard_map/weight_grad/pallas_call | solution.py:594
  396.9 10.2 %input_back.3 = f32[1024,768]{1,0:T(8,128)} custom-call(s32[2]{0:T(128)} %pad_add_fusion.core_ref.place_ref, bf16[3,1024,768]{2,1,0:T(8,128)(2,1)} %get-tuple-element.111.grads.refs_1_, f32[1024,768]{1,0:T(8,128)} %get-tuple-element.112.gm, bf16[3,2,192,384]{3,2,1,0:T(8,128)(2,1)} %copy-done.1, bf16[3,2,192,384]{3,2,1,0:T(8,128)(2,1)} %copy-done, ...), custom_call_target="tpu_custom_call" | custom-call | flops 3623878656 | bytes 11010048 | tf_op jit(solution)/shard_map/input_back/pallas_call | solution.py:533
  436.8 5.3 %collective-permute-done.31 = bf16[3,4,2,24,384]{4,3,0,1,2:T(8,128)(2,1)S(1)} collective-permute-done((bf16[3,4,2,24,384]{4,3,0,1,2:T(8,128)(2,1)S(1)}, bf16[3,4,2,24,384]{4,3,0,1,2:T(8,128)(2,1)S(1)}, u32[]{:S(2)}, u32[]{:S(2)}) %collective-permute-start.31) | collective-permute-done | bytes 442400 | tf_op jit(solution)/shard_map/ppermute | solution.py:712
  464.6 8.9 %collective-permute-done.55 = bf16[1,2,4,96,384]{4,3,2,1,0:T(8,128)(2,1)S(1)} collective-permute-done((bf16[1,2,4,96,384]{4,3,2,1,0:T(8,128)(2,1)S(1)}, bf16[1,2,4,96,384]{4,3,2,1,0:T(8,128)(2,1)S(1)}, u32[]{:S(2)}, u32[]{:S(2)}) %collective-permute-start.55) | collective-permute-done | bytes 589856 | tf_op jit(solution)/shard_map/ppermute | solution.py:712
  487.3 5.9 %collective-permute-done.66 = bf16[1,24,3072]{2,1,0:T(8,128)(2,1)S(1)} collective-permute-done((bf16[1,24,3072]{2,1,0:T(8,128)(2,1)S(1)}, bf16[1,24,3072]{2,1,0:T(8,128)(2,1)S(1)}, u32[]{:S(2)}, u32[]{:S(2)}) %collective-permute-start.66) | collective-permute-done | bytes 147488 | tf_op jit(solution)/shard_map/ppermute | solution.py:712
  (353 shorter events, 146.1 us)
Async XLA Ops:
  28.7 18.7 %collective-permute-start.3 = (bf16[4,80,384]{2,1,0:T(8,128)(2,1)S(1)}, bf16[4,80,384]{2,1,0:T(8,128)(2,1)S(1)}, u32[]{:S(2)}, u32[]{:S(2)}) collective-permute-start(bf16[4,80,384]{2,1,0:T(8,128)(2,1)S(1)} %get-tuple-element.204), channel_id=1, source_target_pairs={{0,16},{1,17},{2,18},{3,19},{4,20},{5,21},{6,22},{7,23},{8,24},{9,... | collective-permute-start | bytes 737288 | tf_op jit(solution)/shard_map/ppermute | solution.py:712
  30.2 18.7 %collective-permute-start.6 = (bf16[4,80,384]{2,1,0:T(8,128)(2,1)S(1)}, bf16[4,80,384]{2,1,0:T(8,128)(2,1)S(1)}, u32[]{:S(2)}, u32[]{:S(2)}) collective-permute-start(bf16[4,80,384]{2,1,0:T(8,128)(2,1)S(1)} %get-tuple-element.203), channel_id=1, source_target_pairs={{0,1},{1,0},{2,3},{3,2},{4,5},{5,4},{6,7},{7,6},{8,9},{9,8},{10,11... | collective-permute-start | bytes 737288 | tf_op jit(solution)/shard_map/ppermute | solution.py:712
  50.7 30.1 %collective-permute-start.7 = (bf16[4,2,80,384]{3,2,0,1:T(8,128)(2,1)S(1)}, bf16[4,2,80,384]{3,2,0,1:T(8,128)(2,1)S(1)}, u32[]{:S(2)}, u32[]{:S(2)}) collective-permute-start(bf16[4,2,80,384]{3,2,0,1:T(8,128)(2,1)S(1)} %pad_maximum_fusion.14), channel_id=1, source_target_pairs={{0,16},{1,17},{2,18},{3,19},{4,20},{5,21},{6,22},{7,23},{8,24},{9,... | collective-permute-start | bytes 1474568 | tf_op jit(solution)/shard_map/ppermute | solution.py:712
  57.8 22.2 %collective-permute-start.4 = (bf16[2,4,80,384]{3,2,1,0:T(8,128)(2,1)S(1)}, bf16[2,4,80,384]{3,2,1,0:T(8,128)(2,1)S(1)}, u32[]{:S(2)}, u32[]{:S(2)}) collective-permute-start(bf16[2,4,80,384]{3,2,1,0:T(8,128)(2,1)S(1)} %pad_maximum_fusion.13), channel_id=1, source_target_pairs={{0,1},{1,0},{2,3},{3,2},{4,5},{5,4},{6,7},{7,6},{8,9},{9,8},{10,11... | collective-permute-start | bytes 1474568 | tf_op jit(solution)/shard_map/ppermute | solution.py:712
  59.6 16.2 %collective-permute-start.24 = (bf16[4,24,1536]{2,1,0:T(8,128)(2,1)S(1)}, bf16[4,24,1536]{2,1,0:T(8,128)(2,1)S(1)}, u32[]{:S(2)}, u32[]{:S(2)}) collective-permute-start(bf16[4,24,1536]{2,1,0:T(8,128)(2,1)S(1)} %get-tuple-element.196), channel_id=1, source_target_pairs={{0,16},{1,17},{2,18},{3,19},{4,20},{5,21},{6,22},{7,23},{8,24},{9,... | collective-permute-start | bytes 884744 | tf_op jit(solution)/shard_map/ppermute | solution.py:712
  61.1 16.2 %collective-permute-start.26 = (bf16[4,24,1536]{2,1,0:T(8,128)(2,1)S(1)}, bf16[4,24,1536]{2,1,0:T(8,128)(2,1)S(1)}, u32[]{:S(2)}, u32[]{:S(2)}) collective-permute-start(bf16[4,24,1536]{2,1,0:T(8,128)(2,1)S(1)} %get-tuple-element.195), channel_id=1, source_target_pairs={{0,1},{1,0},{2,3},{3,2},{4,5},{5,4},{6,7},{7,6},{8,9},{9,8},{10,11... | collective-permute-start | bytes 884744 | tf_op jit(solution)/shard_map/ppermute | solution.py:712
  62.9 42.8 %collective-permute-start.16 = (bf16[4,2,120,384]{3,2,0,1:T(8,128)(2,1)}, bf16[4,2,120,384]{3,2,0,1:T(8,128)(2,1)}, u32[]{:S(2)}, u32[]{:S(2)}) collective-permute-start(bf16[4,2,120,384]{3,2,0,1:T(8,128)(2,1)} %pad_maximum_fusion.8), channel_id=1, source_target_pairs={{0,16},{1,17},{2,18},{3,19},{4,20},{5,21},{6,22},{7,23},{8,24},{9,... | collective-permute-start | bytes 2211848 | tf_op jit(solution)/shard_map/ppermute | solution.py:712
  75.8 33.1 %collective-permute-start.14 = (bf16[2,4,120,384]{3,2,1,0:T(8,128)(2,1)}, bf16[2,4,120,384]{3,2,1,0:T(8,128)(2,1)}, u32[]{:S(2)}, u32[]{:S(2)}) collective-permute-start(bf16[2,4,120,384]{3,2,1,0:T(8,128)(2,1)} %pad_maximum_fusion.7), channel_id=1, source_target_pairs={{0,1},{1,0},{2,3},{3,2},{4,5},{5,4},{6,7},{7,6},{8,9},{9,8},{10,11... | collective-permute-start | bytes 2211848 | tf_op jit(solution)/shard_map/ppermute | solution.py:712
  77.6 24.2 %collective-permute-start.27 = (bf16[4,2,24,1536]{3,2,0,1:T(8,128)(2,1)S(1)}, bf16[4,2,24,1536]{3,2,0,1:T(8,128)(2,1)}, u32[]{:S(2)}, u32[]{:S(2)}) collective-permute-start(bf16[4,2,24,1536]{3,2,0,1:T(8,128)(2,1)S(1)} %pad_maximum_fusion.11), channel_id=1, source_target_pairs={{0,16},{1,17},{2,18},{3,19},{4,20},{5,21},{6,22},{7,23},{8,24},{9,... | collective-permute-start | bytes 1769480 | tf_op jit(solution)/shard_map/ppermute | solution.py:712
  80.0 23.1 %collective-permute-start.25 = (bf16[2,4,24,1536]{3,2,1,0:T(8,128)(2,1)}, bf16[2,4,24,1536]{3,2,1,0:T(8,128)(2,1)}, u32[]{:S(2)}, u32[]{:S(2)}) collective-permute-start(bf16[2,4,24,1536]{3,2,1,0:T(8,128)(2,1)} %pad_maximum_fusion.10), channel_id=1, source_target_pairs={{0,1},{1,0},{2,3},{3,2},{4,5},{5,4},{6,7},{7,6},{8,9},{9,8},{10,11... | collective-permute-start | bytes 1769480 | tf_op jit(solution)/shard_map/ppermute | solution.py:712
  82.6 32.3 %collective-permute-start.9 = (bf16[3,2,192,384]{3,2,1,0:T(8,128)(2,1)S(1)}, bf16[3,2,192,384]{3,2,1,0:T(8,128)(2,1)S(1)}, u32[]{:S(2)}, u32[]{:S(2)}) collective-permute-start(bf16[3,2,192,384]{3,2,1,0:T(8,128)(2,1)S(1)} %pad_maximum_fusion.5.own_b.rest_3_.rest_1_), channel_id=1, source_target_pairs={{0,8},{1,9},{2,10},{3,11},{4,12},{5,13},{6,14},{7,15},{8,0},{9,1},... | collective-permute-start | bytes 2654216 | tf_op jit(solution)/shard_map/ppermute | solution.py:712
  108.4 31.0 %collective-permute-start.20 = (bf16[2,768,384]{2,1,0:T(8,128)(2,1)}, bf16[2,768,384]{2,1,0:T(8,128)(2,1)}, u32[]{:S(2)}, u32[]{:S(2)}) collective-permute-start(bf16[2,768,384]{2,1,0:T(8,128)(2,1)} %bitcast.44.uo_b), channel_id=1, source_target_pairs={{0,8},{1,9},{2,10},{3,11},{4,12},{5,13},{6,14},{7,15},{8,0},{9,1},... | collective-permute-start | bytes 3538952 | tf_op jit(solution)/shard_map/ppermute | solution.py:712
  111.5 27.9 %collective-permute-start.19 = (bf16[2,768,384]{2,1,0:T(8,128)(2,1)}, bf16[2,768,384]{2,1,0:T(8,128)(2,1)}, u32[]{:S(2)}, u32[]{:S(2)}) collective-permute-start(bf16[2,768,384]{2,1,0:T(8,128)(2,1)} %bitcast.43.uo_a), channel_id=1, source_target_pairs={{0,8},{1,9},{2,10},{3,11},{4,12},{5,13},{6,14},{7,15},{8,0},{9,1},... | collective-permute-start | bytes 3538952 | tf_op jit(solution)/shard_map/ppermute | solution.py:712
  114.8 43.5 %collective-permute-start.29 = (bf16[2,192,1536]{2,1,0:T(8,128)(2,1)}, bf16[2,192,1536]{2,1,0:T(8,128)(2,1)}, u32[]{:S(2)}, u32[]{:S(2)}) collective-permute-start(bf16[2,192,1536]{2,1,0:T(8,128)(2,1)} %pad_maximum_fusion.3.do_b), channel_id=1, source_target_pairs={{0,8},{1,9},{2,10},{3,11},{4,12},{5,13},{6,14},{7,15},{8,0},{9,1},... | collective-permute-start | bytes 3538952 | tf_op jit(solution)/shard_map/ppermute | solution.py:712
  114.9 43.4 %collective-permute-start.28 = (bf16[2,192,1536]{2,1,0:T(8,128)(2,1)}, bf16[2,192,1536]{2,1,0:T(8,128)(2,1)}, u32[]{:S(2)}, u32[]{:S(2)}) collective-permute-start(bf16[2,192,1536]{2,1,0:T(8,128)(2,1)} %bitcast.53.do_a), channel_id=1, source_target_pairs={{0,8},{1,9},{2,10},{3,11},{4,12},{5,13},{6,14},{7,15},{8,0},{9,1},... | collective-permute-start | bytes 3538952 | tf_op jit(solution)/shard_map/ppermute | solution.py:712
  115.3 24.0 %collective-permute-start.17 = (bf16[2,192,384]{2,1,0:T(8,128)(2,1)}, bf16[2,192,384]{2,1,0:T(8,128)(2,1)S(1)}, u32[]{:S(2)}, u32[]{:S(2)}) collective-permute-start(bf16[2,192,384]{2,1,0:T(8,128)(2,1)} %bitcast.37.oo_a), channel_id=1, source_target_pairs={{0,8},{1,9},{2,10},{3,11},{4,12},{5,13},{6,14},{7,15},{8,0},{9,1},... | collective-permute-start | bytes 884744 | tf_op jit(solution)/shard_map/ppermute | solution.py:712
  324.2 119.5 %collective-permute-start.60 = (bf16[1,2,2,192,1536]{4,3,2,1,0:T(8,128)(2,1)}, bf16[1,2,2,192,1536]{4,3,2,1,0:T(8,128)(2,1)S(1)}, u32[]{:S(2)}, u32[]{:S(2)}) collective-permute-start(bf16[1,2,2,192,1536]{4,3,2,1,0:T(8,128)(2,1)} %get-tuple-element.134), channel_id=1, source_target_pairs={{0,8},{1,9},{2,10},{3,11},{4,12},{5,13},{6,14},{7,15},{8,0},{9,1},... | collective-permute-start | bytes 7077896 | tf_op jit(solution)/shard_map/ppermute | solution.py:712
  358.1 50.8 %collective-permute-start.44 = (bf16[1,2,2,192,384]{4,3,2,1,0:T(8,128)(2,1)}, bf16[1,2,2,192,384]{4,3,2,1,0:T(8,128)(2,1)S(1)}, u32[]{:S(2)}, u32[]{:S(2)}) collective-permute-start(bf16[1,2,2,192,384]{4,3,2,1,0:T(8,128)(2,1)} %get-tuple-element.126), channel_id=1, source_target_pairs={{0,8},{1,9},{2,10},{3,11},{4,12},{5,13},{6,14},{7,15},{8,0},{9,1},... | collective-permute-start | bytes 1769480 | tf_op jit(solution)/shard_map/ppermute | solution.py:712
  358.6 17.7 %collective-permute-start.39 = (f32[4,2,288]{2,1,0:T(2,128)S(1)}, f32[4,2,288]{2,1,0:T(2,128)S(1)}, u32[]{:S(2)}, u32[]{:S(2)}) collective-permute-start(f32[4,2,288]{2,1,0:T(2,128)S(1)} %fusion.69), channel_id=1, source_target_pairs={{0,16},{1,17},{2,18},{3,19},{4,20},{5,21},{6,22},{7,23},{8,24},{9,... | collective-permute-start | bytes 27656 | tf_op jit(solution)/shard_map/ppermute | solution.py:712
  407.1 40.0 %collective-permute-start.52 = (bf16[1,2,2,768,384]{4,3,2,1,0:T(8,128)(2,1)}, bf16[1,2,2,768,384]{4,3,2,1,0:T(8,128)(2,1)S(1)}, u32[]{:S(2)}, u32[]{:S(2)}) collective-permute-start(bf16[1,2,2,768,384]{4,3,2,1,0:T(8,128)(2,1)} %bitcast.349), channel_id=1, source_target_pairs={{0,8},{1,9},{2,10},{3,11},{4,12},{5,13},{6,14},{7,15},{8,0},{9,1},... | collective-permute-start | bytes 7077896 | tf_op jit(solution)/shard_map/ppermute | solution.py:712
  444.5 17.6 %collective-permute-start.63 = (bf16[1,2,4,24,1536]{4,3,2,1,0:T(8,128)(2,1)S(1)}, bf16[1,2,4,24,1536]{4,3,2,1,0:T(8,128)(2,1)S(1)}, u32[]{:S(2)}, u32[]{:S(2)}) collective-permute-start(bf16[1,2,4,24,1536]{4,3,2,1,0:T(8,128)(2,1)S(1)} %dynamic-slice_bitcast_fusion), channel_id=1, source_target_pairs={{0,1},{1,0},{2,3},{3,2},{4,5},{5,4},{6,7},{7,6},{8,9},{9,8},{10,11... | collective-permute-start | bytes 1769480 | tf_op jit(solution)/shard_map/ppermute | solution.py:712
  445.5 18.3 %collective-permute-start.61 = (bf16[1,4,2,24,1536]{4,3,1,2,0:T(8,128)(2,1)S(1)}, bf16[1,4,2,24,1536]{4,3,1,2,0:T(8,128)(2,1)S(1)}, u32[]{:S(2)}, u32[]{:S(2)}) collective-permute-start(bf16[1,4,2,24,1536]{4,3,1,2,0:T(8,128)(2,1)S(1)} %slice_bitcast_fusion), channel_id=1, source_target_pairs={{0,16},{1,17},{2,18},{3,19},{4,20},{5,21},{6,22},{7,23},{8,24},{9,... | collective-permute-start | bytes 1769480 | tf_op jit(solution)/shard_map/ppermute | solution.py:712
  455.6 17.9 %collective-permute-start.55 = (bf16[1,2,4,96,384]{4,3,2,1,0:T(8,128)(2,1)S(1)}, bf16[1,2,4,96,384]{4,3,2,1,0:T(8,128)(2,1)S(1)}, u32[]{:S(2)}, u32[]{:S(2)}) collective-permute-start(bf16[1,2,4,96,384]{4,3,2,1,0:T(8,128)(2,1)S(1)} %dynamic-slice_bitcast_fusion.1), channel_id=1, source_target_pairs={{0,1},{1,0},{2,3},{3,2},{4,5},{5,4},{6,7},{7,6},{8,9},{9,8},{10,11... | collective-permute-start | bytes 1769480 | tf_op jit(solution)/shard_map/ppermute | solution.py:712
  456.8 18.6 %collective-permute-start.53 = (bf16[1,4,2,96,384]{4,3,1,2,0:T(8,128)(2,1)S(1)}, bf16[1,4,2,96,384]{4,3,1,2,0:T(8,128)(2,1)S(1)}, u32[]{:S(2)}, u32[]{:S(2)}) collective-permute-start(bf16[1,4,2,96,384]{4,3,1,2,0:T(8,128)(2,1)S(1)} %slice_bitcast_fusion.2), channel_id=1, source_target_pairs={{0,16},{1,17},{2,18},{3,19},{4,20},{5,21},{6,22},{7,23},{8,24},{9,... | collective-permute-start | bytes 1769480 | tf_op jit(solution)/shard_map/ppermute | solution.py:712
  (81 other events, 885.7 us)

commit v2 on v1

v2 whole, which is shorter than its diff:
```python
from functools import partial
import math

import jax
import jax.numpy as jnp
from jax import lax
from jax.experimental import pallas as pl
from jax.experimental.pallas import tpu as pltpu
from jax.sharding import PartitionSpec as P

HEAD = 64
LAYERS = 2
QUAD = 4 * HEAD
TILE = 256
SUB = 256
norm_eps = 1e-06
masked_score = -1000000000.0
VMEM = 60 * 1024 * 1024
bf16 = jnp.bfloat16
f32 = jnp.float32

QB, VB, OB, G1, S1, DB, G2, S2 = range(8)


def dot_nt(left, right):
    return lax.dot_general(left, right, (((1,), (1,)), ((), ())), preferred_element_type=f32)


def dot_nn(left, right):
    return lax.dot_general(left, right, (((1,), (0,)), ((), ())), preferred_element_type=f32)


def normalize(v):
    mean = jnp.mean(v, axis=-1, keepdims=True)
    centered = v - mean
    rstd = lax.rsqrt(jnp.mean(centered * centered, axis=-1, keepdims=True) + norm_eps)
    return centered * rstd, rstd


def normalize_back(grad, gain, unit, rstd):
    scaled = grad * gain
    first = jnp.mean(scaled, axis=-1, keepdims=True)
    second = jnp.mean(scaled * unit, axis=-1, keepdims=True)
    return rstd * (scaled - first - unit * second)


def partial_sum(v):
    return jnp.sum(v.reshape(v.shape[0] // 8, 8, v.shape[1]), axis=0)


def piece_copies(core, pieces, place, sems, which=None):
    copies = []
    for sibling, piece in enumerate(pieces):
        source = piece if which is None else piece.at[which]
        sides, _, rows, half = source.shape
        for side in range(sides):
            for x in range(2):
                slot = 2 * x + (1 - core if sibling else core)
                start = pl.multiple_of(slot * rows, rows)
                copies.append(
                    pltpu.make_async_copy(
                        source.at[side, x],
                        place.at[pl.ds(start, rows), pl.ds(side * half, half)],
                        sems.at[4 * sibling + 2 * side + x],
                    )
                )
    return copies


def start_all(copies):
    for copy in copies:
        copy.start()


def wait_all(copies):
    for copy in copies:
        copy.wait()


def params():
    return pltpu.CompilerParams(vmem_limit_bytes=VMEM)


ANY = pl.BlockSpec(memory_space=pl.ANY)
SMEM = pl.BlockSpec(memory_space=pltpu.SMEM)


def whole(shape):
    return pl.BlockSpec(shape, lambda *_: (0,) * len(shape))


def mask_into(mask, seg_col, alive_col, seg_row):
    length = mask.shape[0]
    key = lax.broadcasted_iota(jnp.int32, (length, length), 0)
    query = lax.broadcasted_iota(jnp.int32, (length, length), 1)
    same = seg_col[:, 0:1] == seg_row[0]
    allowed = same & ((alive_col[:, 0:1] > 0) | (key == query))
    mask[...] = jnp.where(allowed, 0.0, masked_score)


def attend_forward_kernel(
    core_ref, x, seg_col, alive_col, seg_row, vecs, own, sib, *rest
):
    q_out, k_out, v_out, ctx_out, lse_out, weights, mask, sems = rest[-8:]
    row, quad = pl.program_id(0), pl.program_id(1)
    core = core_ref[0]
    first = (row == 0) & (quad == 0)
    copies = [
        piece_copies(core, (own, sib), weights.at[w], sems.at[w], w)
        for w in range(3)
    ]

    @pl.when(first)
    def _():
        for group in copies:
            start_all(group)

    @pl.when(quad == 0)
    def _():
        mask_into(mask, seg_col, alive_col, seg_row)

    @pl.when(first)
    def _():
        for group in copies:
            wait_all(group)

    inputs = x[...]
    heads = pl.ds(pl.multiple_of(quad * QUAD, QUAD), QUAD)
    queries = (dot_nt(inputs, weights[0, heads, :]) + vecs[QB : QB + 1, :]).astype(bf16)
    keys = dot_nt(inputs, weights[1, heads, :]).astype(bf16)
    values = (dot_nt(inputs, weights[2, heads, :]) + vecs[VB : VB + 1, :]).astype(bf16)
    q_out[...] = queries
    k_out[...] = keys
    v_out[...] = values
    scaled = queries * bf16(HEAD**-0.5)
    length = inputs.shape[0]
    lane = lax.broadcasted_iota(jnp.int32, (length, 2 * HEAD), 1)
    for pair in range(2):
        cols = slice(pair * 2 * HEAD, (pair + 1) * 2 * HEAD)
        kp, qp = keys[:, cols], scaled[:, cols]
        vt = values[:, cols].T
        parts = []
        for h in range(2):
            km = jnp.where((lane >= HEAD) if h else (lane < HEAD), kp, bf16(0))
            scores = dot_nt(km, qp) + mask[...]
            highest = jnp.max(scores, axis=0, keepdims=True)
            weight = jnp.exp(scores - highest)
            total = jnp.sum(weight, axis=0, keepdims=True)
            parts.append(dot_nn(vt[h * HEAD : (h + 1) * HEAD], weight.astype(bf16)) / total)
            lse_out[0, 0, pl.ds(2 * pair + h, 1), :] = highest + jnp.log(total)
        ctx_out[:, cols] = jnp.concatenate(parts, axis=0).T.astype(bf16)


def attend_forward(core, x, seg_col, alive_col, seg_row, vecs, qkv, start=0, stop=None, before=()):
    count, width = x.shape
    rows, _, length = seg_row.shape
    stop = rows if stop is None else stop
    quads = width // QUAD
    full = pl.BlockSpec((length, width), lambda r, j: (r + start, 0))
    col = pl.BlockSpec((length, 128), lambda r, j: (r + start, 0))
    block = pl.BlockSpec((length, QUAD), lambda r, j: (r + start, j))
    low = jax.ShapeDtypeStruct((count, width), bf16)
    share = (stop - start) / rows
    return pl.pallas_call(
        attend_forward_kernel,
        grid=(stop - start, quads),
        in_specs=[SMEM, full, col, col, pl.BlockSpec((1, 1, length), lambda r, j: (r + start, 0, 0)),
                  pl.BlockSpec((8, QUAD), lambda r, j: (0, j)), ANY, ANY] + [ANY] * len(before),
        out_specs=[block] * 4 + [pl.BlockSpec((1, 1, 8, length), lambda r, j: (r + start, j, 0, 0))],
        out_shape=[low] * 4 + [jax.ShapeDtypeStruct((rows, quads, 8, length), f32)],
        scratch_shapes=[
            pltpu.VMEM((3, width, width), bf16),
            pltpu.VMEM((length, length), f32),
            pltpu.SemaphoreType.DMA((3, 8)),
        ],
        input_output_aliases={8 + i: i for i in range(len(before))},
        compiler_params=params(),
        cost_estimate=pl.CostEstimate(
            flops=int(share * (2 * count * width * width * 3 + 4 * 4 * count * length * width)),
            bytes_accessed=int(share * count * width * 10) + 3 * width * width * 2, transcendentals=0),
        name="attend_forward",
    )(core, x, seg_col, alive_col, seg_row, vecs, *qkv, *before)


GELU_A = math.sqrt(2.0 / math.pi)
GELU_B = 0.044715


def gelu_both(u):
    square = u * u
    t = jnp.tanh(u * (GELU_A + (GELU_A * GELU_B) * square))
    half = 0.5 + 0.5 * t
    slope = half + (u * (1.0 - t * t)) * (0.5 * GELU_A + (1.5 * GELU_A * GELU_B) * square)
    return u * half, slope


def widen_kernel(
    core_ref, ctx, resid, vecs, up_bias, o_own, o_sib, u_own, u_sib,
    mixed_out, low_out, act_out, slope_out, out_weight, up_weight, sems,
):
    core = core_ref[0]
    first = pl.program_id(0) == 0
    out_copies = piece_copies(core, (o_own, o_sib), out_weight, sems.at[0])
    up_copies = piece_copies(core, (u_own, u_sib), up_weight, sems.at[1])

    @pl.when(first)
    def _():
        start_all(out_copies)
        start_all(up_copies)
        wait_all(out_copies)

    mixed = resid[...].astype(f32) + dot_nt(ctx[...], out_weight[...]) + vecs[OB : OB + 1, :]
    mixed_out[...] = mixed
    normed = normalize(mixed)[0] * vecs[G1 : G1 + 1, :] + vecs[S1 : S1 + 1, :]
    low = normed.astype(bf16)
    low_out[...] = low

    @pl.when(first)
    def _():
        wait_all(up_copies)

    width = low.shape[1]
    for chunk in range(up_weight.shape[0] // width):
        cols = slice(chunk * width, (chunk + 1) * width)
        upward = dot_nt(low, up_weight[cols, :]) + up_bias[0:1, cols]
        act, slope = gelu_both(upward)
        act_out[:, cols] = act.astype(bf16)
        slope_out[:, cols] = slope.astype(bf16)


def widen(core, ctx, resid, vecs, up_bias, out_weight, up_weight):
    count, width = ctx.shape
    wide = up_bias.shape[1]
    tile = pl.BlockSpec((TILE, width), lambda i: (i, 0))
    broad = pl.BlockSpec((TILE, wide), lambda i: (i, 0))
    return pl.pallas_call(
        widen_kernel,
        grid=(count // TILE,),
        in_specs=[SMEM, tile, tile, whole((8, width)), whole((8, wide))] + [ANY] * 4,
        out_specs=[tile, tile, broad, broad],
        out_shape=[
            jax.ShapeDtypeStruct((count, width), f32),
            jax.ShapeDtypeStruct((count, width), bf16),
            jax.ShapeDtypeStruct((count, wide), bf16),
            jax.ShapeDtypeStruct((count, wide), bf16),
        ],
        scratch_shapes=[
            pltpu.VMEM((width, width), bf16),
            pltpu.VMEM((wide, width), bf16),
            pltpu.SemaphoreType.DMA((2, 8)),
        ],
        compiler_params=params(),
        cost_estimate=pl.CostEstimate(
            flops=2 * count * width * (width + wide),
            bytes_accessed=count * (width * 12 + wide * 4), transcendentals=0),
        name="widen",
    )(core, ctx, resid, vecs, up_bias, *out_weight, *up_weight)


def narrow_kernel(core_ref, act, mixed, vecs, d_own, d_sib, combined_out, low_out, down_weight, sems):
    core = core_ref[0]
    copies = piece_copies(core, (d_own, d_sib), down_weight, sems)

    @pl.when(pl.program_id(0) == 0)
    def _():
        start_all(copies)
        wait_all(copies)

    normed = normalize(mixed[...])[0] * vecs[G1 : G1 + 1, :] + vecs[S1 : S1 + 1, :]
    combined = normed + dot_nt(act[...], down_weight[...]) + vecs[DB : DB + 1, :]
    combined_out[...] = combined
    hidden = normalize(combined)[0] * vecs[G2 : G2 + 1, :] + vecs[S2 : S2 + 1, :]
    low_out[...] = hidden.astype(bf16)


def narrow(core, act, mixed, vecs, down_weight):
    count, width = mixed.shape
    wide = act.shape[1]
    tile = pl.BlockSpec((TILE, width), lambda i: (i, 0))
    broad = pl.BlockSpec((TILE, wide), lambda i: (i, 0))
    return pl.pallas_call(
        narrow_kernel,
        grid=(count // TILE,),
        in_specs=[SMEM, broad, tile, whole((8, width))] + [ANY] * 2,
        out_specs=[tile, tile],
        out_shape=[jax.ShapeDtypeStruct((count, width), f32), jax.ShapeDtypeStruct((count, width), bf16)],
        scratch_shapes=[pltpu.VMEM((width, wide), bf16), pltpu.SemaphoreType.DMA((8,))],
        compiler_params=params(),
        cost_estimate=pl.CostEstimate(
            flops=2 * count * width * wide, bytes_accessed=count * (width * 10 + wide * 2), transcendentals=0),
        name="narrow",
    )(core, act, mixed, vecs, *down_weight)


def add_rows(out, first, values):
    @pl.when(first)
    def _():
        out[...] = jnp.zeros_like(out)

    for index, value in enumerate(values):
        out[index] += partial_sum(value)


def top_kernel(
    core_ref, ctx, resid, cot, alive_col, vecs, up_bias,
    o_own, o_sib, u_own, u_sib, d_own, d_sib,
    outputs, low_out, act_out, gb_out, gu_out, ga_out, gm_out, gctx_out, sums, up_sums,
    out_weight, up_weight, down_weight, slopes, sems,
):
    core = core_ref[0]
    first = pl.program_id(0) == 0
    out_copies = piece_copies(core, (o_own, o_sib), out_weight, sems.at[0])
    up_copies = piece_copies(core, (u_own, u_sib), up_weight, sems.at[1])
    down_copies = piece_copies(core, (d_own, d_sib), down_weight, sems.at[2])

    @pl.when(first)
    def _():
        start_all(out_copies)
        start_all(up_copies)
        start_all(down_copies)
        sums[...] = jnp.zeros_like(sums)
        up_sums[...] = jnp.zeros_like(up_sums)
        wait_all(out_copies)
        wait_all(up_copies)
        wait_all(down_copies)

    width = ctx.shape[1]
    chunks = [slice(c * width, (c + 1) * width) for c in range(up_weight.shape[0] // width)]
    for part in range(ctx.shape[0] // SUB):
        rows = slice(part * SUB, (part + 1) * SUB)
        hidden = normalize(resid[rows, :])[0] * vecs[G2 : G2 + 1, :] + vecs[S2 : S2 + 1, :]
        mixed = hidden + dot_nt(ctx[rows, :], out_weight[...]) + vecs[OB : OB + 1, :]
        first_unit, first_rstd = normalize(mixed)
        combined = first_unit * vecs[G1 : G1 + 1, :] + vecs[S1 : S1 + 1, :]
        low = combined.astype(bf16)
        low_out[rows, :] = low
        for cols in chunks:
            act, slope = gelu_both(dot_nt(low, up_weight[cols, :]) + up_bias[0:1, cols])
            act = act.astype(bf16)
            act_out[rows, cols] = act
            slopes[rows, cols] = slope.astype(bf16)
            combined = combined + dot_nt(act, down_weight[:, cols])
        unit, rstd = normalize(combined + vecs[DB : DB + 1, :])
        gain = vecs[G2 : G2 + 1, :]
        alive = alive_col[rows, 0:1].astype(f32)
        outputs[rows, :] = ((unit * gain + vecs[S2 : S2 + 1, :]) * alive).astype(bf16)
        grad = cot[rows, :].astype(f32) * alive
        sums[0] += partial_sum(grad * unit)
        sums[1] += partial_sum(grad)
        grad = normalize_back(grad, gain, unit, rstd)
        feed_back_rows(
            rows, chunks, grad, slopes, first_unit, first_rstd, vecs, down_weight, up_weight, out_weight,
            gb_out, gu_out, ga_out, gm_out, gctx_out, sums, up_sums,
        )


def feed_back_rows(
    rows, chunks, grad, slopes, unit, rstd, vecs, down_weight, up_weight, out_weight,
    gb_out, gu_out, ga_out, gm_out, gctx_out, sums, up_sums,
):
    branch = grad.astype(bf16)
    gb_out[rows, :] = branch
    sums[2] += partial_sum(branch.astype(f32))
    for cols in chunks:
        grad_up = (dot_nn(branch, down_weight[:, cols]) * slopes[rows, cols].astype(f32)).astype(bf16)
        gu_out[rows, cols] = grad_up
        up_sums[:, cols] += partial_sum(grad_up.astype(f32))
        grad = grad + dot_nn(grad_up, up_weight[cols, :])
    sums[3] += partial_sum(grad * unit)
    sums[4] += partial_sum(grad)
    grad = normalize_back(grad, vecs[G1 : G1 + 1, :], unit, rstd)
    gm_out[rows, :] = grad
    attn = grad.astype(bf16)
    ga_out[rows, :] = attn
    sums[5] += partial_sum(attn.astype(f32))
    gctx_out[rows, :] = dot_nn(attn, out_weight[...]).astype(bf16)


def top(core, ctx, resid, cot, alive_col, vecs, up_bias, out_weight, up_weight, down_weight):
    count, width = ctx.shape
    wide = up_bias.shape[1]
    tile = pl.BlockSpec((TILE, width), lambda i: (i, 0))
    broad = pl.BlockSpec((TILE, wide), lambda i: (i, 0))
    low = jax.ShapeDtypeStruct((count, width), bf16)
    low_wide = jax.ShapeDtypeStruct((count, wide), bf16)
    return pl.pallas_call(
        top_kernel,
        grid=(count // TILE,),
        in_specs=[SMEM, tile, tile, tile, pl.BlockSpec((TILE, 128), lambda i: (i, 0)), whole((8, width)),
                  whole((8, wide))] + [ANY] * 6,
        out_specs=[tile, tile, broad, tile, broad, tile, tile, tile, whole((6, 8, width)), whole((8, wide))],
        out_shape=[low, low, low_wide, low, low_wide, low, jax.ShapeDtypeStruct((count, width), f32), low,
                   jax.ShapeDtypeStruct((6, 8, width), f32), jax.ShapeDtypeStruct((8, wide), f32)],
        scratch_shapes=[
            pltpu.VMEM((width, width), bf16),
            pltpu.VMEM((wide, width), bf16),
            pltpu.VMEM((width, wide), bf16),
            pltpu.VMEM((TILE, wide), bf16),
            pltpu.SemaphoreType.DMA((3, 8)),
        ],
        compiler_params=params(),
        cost_estimate=pl.CostEstimate(
            flops=4 * count * width * (width + 2 * wide),
            bytes_accessed=count * (width * 22 + wide * 4), transcendentals=0),
        name="top",
    )(core, ctx, resid, cot, alive_col, vecs, up_bias, *out_weight, *up_weight, *down_weight)


def lower_kernel(
    core_ref, grads, gm, combined, slope, mixed, vecs, d_own, d_sib, u_own, u_sib,
    o_own, o_sib, q_own, q_sib,
    gb_out, gu_out, ga_out, gm_out, gctx_out, sums, up_sums, down_weight, up_weight, out_weight, weights, sems,
):
    core = core_ref[0]
    first = pl.program_id(0) == 0
    down_copies = piece_copies(core, (d_own, d_sib), down_weight, sems.at[0])
    up_copies = piece_copies(core, (u_own, u_sib), up_weight, sems.at[1])
    out_copies = piece_copies(core, (o_own, o_sib), out_weight, sems.at[2])
    copies = [
        piece_copies(core, (q_own, q_sib), weights.at[w], sems.at[3 + w], w) for w in range(3)
    ]

    @pl.when(first)
    def _():
        for group in copies:
            start_all(group)
        start_all(down_copies)
        start_all(up_copies)
        start_all(out_copies)
        sums[...] = jnp.zeros_like(sums)
        up_sums[...] = jnp.zeros_like(up_sums)
        for group in copies:
            wait_all(group)
        wait_all(down_copies)
        wait_all(up_copies)
        wait_all(out_copies)

    width = gm.shape[1]
    chunks = [slice(c * width, (c + 1) * width) for c in range(up_weight.shape[0] // width)]
    for part in range(gm.shape[0] // SUB):
        rows = slice(part * SUB, (part + 1) * SUB)
        grad = gm[rows, :]
        for w in range(3):
            grad = grad + dot_nn(grads[w, rows, :], weights[w])
        unit, rstd = normalize(combined[rows, :])
        sums[0] += partial_sum(grad * unit)
        sums[1] += partial_sum(grad)
        grad = normalize_back(grad, vecs[G2 : G2 + 1, :], unit, rstd)
        first_unit, first_rstd = normalize(mixed[rows, :])
        feed_back_rows(
            rows, chunks, grad, slope, first_unit, first_rstd, vecs, down_weight, up_weight, out_weight,
            gb_out, gu_out, ga_out, gm_out, gctx_out, sums, up_sums,
        )


def lower(core, grads, gm, combined, slope, mixed, vecs, down_weight, up_weight, out_weight, qkv):
    count, width = mixed.shape
    wide = slope.shape[1]
    tile = pl.BlockSpec((TILE, width), lambda i: (i, 0))
    broad = pl.BlockSpec((TILE, wide), lambda i: (i, 0))
    low = jax.ShapeDtypeStruct((count, width), bf16)
    return pl.pallas_call(
        lower_kernel,
        grid=(count // TILE,),
        in_specs=[SMEM, pl.BlockSpec((3, TILE, width), lambda i: (0, i, 0)), tile, tile, broad, tile,
                  whole((8, width))] + [ANY] * 8,
        out_specs=[tile, broad, tile, tile, tile, whole((6, 8, width)), whole((8, wide))],
        out_shape=[low, jax.ShapeDtypeStruct((count, wide), bf16), low, jax.ShapeDtypeStruct((count, width), f32), low,
                   jax.ShapeDtypeStruct((6, 8, width), f32), jax.ShapeDtypeStruct((8, wide), f32)],
        scratch_shapes=[
            pltpu.VMEM((width, wide), bf16),
            pltpu.VMEM((wide, width), bf16),
            pltpu.VMEM((width, width), bf16),
            pltpu.VMEM((3, width, width), bf16),
            pltpu.SemaphoreType.DMA((6, 8)),
        ],
        compiler_params=params(),
        cost_estimate=pl.CostEstimate(
            flops=2 * count * width * (4 * width + 2 * wide),
            bytes_accessed=count * (width * 30 + wide * 4), transcendentals=0),
        name="lower",
    )(core, grads, gm, combined, slope, mixed, vecs, *down_weight, *up_weight, *out_weight, *qkv)


def attend_back_kernel(
    q, k, v, gctx, lse, seg_col, alive_col, seg_row, *rest
):
    grads, sums, mask = rest[-3:]

    @pl.when(pl.program_id(1) == 0)
    def _():
        mask_into(mask, seg_col, alive_col, seg_row)

    length = q.shape[0]
    lane = lax.broadcasted_iota(jnp.int32, (length, 2 * HEAD), 1)
    scaling = HEAD**-0.5
    for pair in range(2):
        cols = slice(pair * 2 * HEAD, (pair + 1) * 2 * HEAD)
        kp, vp, go = k[:, cols], v[:, cols], gctx[:, cols]
        qp = q[:, cols] * bf16(scaling)
        kt = kp.T
        dq_parts = []
        dk = dv = None
        for h in range(2):
            here = (lane >= HEAD) if h else (lane < HEAD)
            zero = bf16(0)
            qm, gm = jnp.where(here, qp, zero), jnp.where(here, go, zero)
            scores = dot_nt(kp, qm) + mask[...]
            probs = jnp.exp(scores - lse[0, 0, pl.ds(2 * pair + h, 1), :])
            weighted = probs * dot_nt(vp, gm)
            inner = jnp.sum(weighted, axis=0, keepdims=True)
            grad_scores = (weighted - probs * inner).astype(bf16)
            dv_h = dot_nn(probs.astype(bf16), gm)
            dk_h = dot_nn(grad_scores, qm)
            dv = dv_h if dv is None else dv + dv_h
            dk = dk_h if dk is None else dk + dk_h
            dq_parts.append(dot_nn(kt[h * HEAD : (h + 1) * HEAD], grad_scores))
        dq = (jnp.concatenate(dq_parts, axis=0).T * scaling).astype(bf16)
        dv = dv.astype(bf16)
        grads[0, :, cols] = dq
        grads[1, :, cols] = dk.astype(bf16)
        grads[2, :, cols] = dv
        sums[0, 0, :, cols] = partial_sum(dq.astype(f32))
        sums[0, 1, :, cols] = partial_sum(dv.astype(f32))


def attend_back(q, k, v, gctx, lse, seg_col, alive_col, seg_row, start=0, stop=None, before=()):
    count, width = q.shape
    rows, _, length = seg_row.shape
    stop = rows if stop is None else stop
    col = pl.BlockSpec((length, 128), lambda r, j: (r + start, 0))
    block = pl.BlockSpec((length, QUAD), lambda r, j: (r + start, j))
    share = (stop - start) / rows
    return pl.pallas_call(
        attend_back_kernel,
        grid=(stop - start, width // QUAD),
        in_specs=[block] * 4 + [pl.BlockSpec((1, 1, 8, length), lambda r, j: (r + start, j, 0, 0)), col, col,
                                pl.BlockSpec((1, 1, length), lambda r, j: (r + start, 0, 0))] + [ANY] * len(before),
        out_specs=[pl.BlockSpec((3, length, QUAD), lambda r, j: (0, r + start, j)),
                   pl.BlockSpec((1, 2, 8, QUAD), lambda r, j: (r + start, 0, 0, j))],
        out_shape=[jax.ShapeDtypeStruct((3, count, width), bf16), jax.ShapeDtypeStruct((rows, 2, 8, width), f32)],
        scratch_shapes=[pltpu.VMEM((length, length), f32)],
        input_output_aliases={8 + i: i for i in range(len(before))},
        compiler_params=params(),
        cost_estimate=pl.CostEstimate(
            flops=int(share * 4 * 10 * count * length * width),
            bytes_accessed=int(share * count * width * 16), transcendentals=0),
        name="attend_back",
    )(q, k, v, gctx, lse, seg_col, alive_col, seg_row, *before)


def input_back_kernel(core_ref, grads, gm, own, sib, grad_out, weights, sems):
    core = core_ref[0]
    copies = [
        piece_copies(core, (own, sib), weights.at[w], sems.at[w], w)
        for w in range(3)
    ]

    @pl.when(pl.program_id(0) == 0)
    def _():
        for group in copies:
            start_all(group)
        for group in copies:
            wait_all(group)

    grad = gm[...]
    for w in range(3):
        grad = grad + dot_nn(grads[w], weights[w])
    grad_out[...] = grad


def input_back(core, grads, gm, qkv):
    count, width = gm.shape
    tile = pl.BlockSpec((TILE, width), lambda i: (i, 0))
    return pl.pallas_call(
        input_back_kernel,
        grid=(count // TILE,),
        in_specs=[SMEM, pl.BlockSpec((3, TILE, width), lambda i: (0, i, 0)), tile] + [ANY] * 2,
        out_specs=tile,
        out_shape=jax.ShapeDtypeStruct((count, width), f32),
        scratch_shapes=[pltpu.VMEM((3, width, width), bf16), pltpu.SemaphoreType.DMA((3, 8))],
        compiler_params=params(),
        cost_estimate=pl.CostEstimate(
            flops=2 * count * width * width * 3, bytes_accessed=count * width * 14, transcendentals=0),
        name="input_back",
    )(core, grads, gm, *qkv)


def weight_grad_kernel(layers, place_ref, *refs):
    grads, inputs = refs[:layers], refs[layers : 2 * layers]
    keep, send, turned = refs[2 * layers :]
    core, flip = place_ref[0], place_ref[1]
    rows = turned.shape[0] // 4
    span = grads[0].shape[-2]

    @pl.when(pl.program_id(1) == 0)
    def _():
        for layer in range(layers):
            flat = grads[layer][0].T
            for block in range(4):
                x, c = block // 2, block % 2
                slot = 2 * ((x + flip) % 2) + (c + core) % 2
                turned[pl.ds(pl.multiple_of(slot * rows, rows), rows), layer * span : (layer + 1) * span] = (
                    flat[block * rows : (block + 1) * rows]
                )

    total = None
    for layer in range(layers):
        term = dot_nn(turned[:, layer * span : (layer + 1) * span], inputs[layer][...])
        total = term if total is None else total + term
    total = total.astype(bf16)
    halves = keep.shape[1]
    wide = keep.shape[-1]
    for half in range(halves):
        for x in range(2):
            for c, out in ((0, keep), (1, send)):
                start = (2 * x + c) * rows
                out[0, half, x] = total[start : start + rows, half * wide : (half + 1) * wide]


def weight_grad(place, grads, inputs):
    layers = len(grads)
    count_w, span, n = grads[0].shape
    depth = inputs[0].shape[1]
    chunk = min(depth, n)
    chunks = depth // chunk
    halves = 2 if chunks == 1 else 1
    wide = chunk // halves
    per_half = depth // 2 // wide
    rows = n // 4
    if chunks == 1:
        out_spec = pl.BlockSpec((1, 2, 2, rows, wide), lambda w, j: (w, 0, 0, 0, 0))
    else:
        out_spec = pl.BlockSpec((1, 1, 2, rows, wide), lambda w, j: (w, j // per_half, 0, 0, j % per_half))
    out = jax.ShapeDtypeStruct((count_w, 2, 2, rows, depth // 2), bf16)
    return pl.pallas_call(
        partial(weight_grad_kernel, layers),
        grid=(count_w, chunks),
        in_specs=[SMEM] + [pl.BlockSpec((1, span, n), lambda w, j: (w, 0, 0))] * layers
        + [pl.BlockSpec((span, chunk), lambda w, j: (0, j))] * layers,
        out_specs=[out_spec, out_spec],
        out_shape=[out, out],
        scratch_shapes=[pltpu.VMEM((n, layers * span), bf16)],
        compiler_params=params(),
        cost_estimate=pl.CostEstimate(
            flops=2 * layers * span * n * depth * count_w,
            bytes_accessed=2 * layers * span * (n * count_w + depth) + 2 * n * depth * count_w, transcendentals=0),
        name="weight_grad",
    )(place, *grads, *inputs)


def joint_grad_kernel(layers, small, tall, place_ref, *refs):
    grads, inputs = refs[:layers], refs[layers : 2 * layers]
    bias_sums, norm_sums, up_sums = (refs[(2 + i) * layers : (3 + i) * layers] for i in range(3))
    keep, send, turned, totals, short = refs[5 * layers :]
    core, flip = place_ref[0], place_ref[1]
    which = pl.program_id(0)
    sides, _, blocks, _, half = keep.shape
    width = turned.shape[0]
    rows = width // 4
    span = inputs[0].shape[0]

    def slot(block):
        return 2 * ((block // 2 + flip) % 2) + (block % 2 + core) % 2

    for layer in range(layers):
        flat = grads[layer][0].T
        for block in range(4):
            turned[pl.ds(pl.multiple_of(slot(block) * rows, rows), rows), layer * span : (layer + 1) * span] = (
                flat[block * rows : (block + 1) * rows]
            )
    total = None
    for layer in range(layers):
        term = dot_nn(turned[:, layer * span : (layer + 1) * span], inputs[layer][...])
        total = term if total is None else total + term
    totals[which] = total

    @pl.when(which == 0)
    def _():
        bias = sum(jnp.sum(ref[...], axis=(0, 2)) for ref in bias_sums)
        norm = sum(jnp.sum(ref[...], axis=1) for ref in norm_sums)
        up = sum(jnp.sum(ref[...], axis=0, keepdims=True) for ref in up_sums)
        rest = [norm[n : n + 1] for n in (5, 3, 4, 2, 0, 1)]
        lines = jnp.concatenate([bias[0:1], bias[1:2], *rest], axis=0)
        short[...] = jnp.zeros_like(short)
        quarter = up.shape[1] // 4
        for block in range(4):
            place = slot(block)
            here = pltpu.roll(lines, lax.rem(width - place * rows, width), 1)
            above = jnp.where(place == 0, up[:, :quarter], 0.0)
            for index in range(1, 4):
                above = above + jnp.where(place == index, up[:, index * quarter : (index + 1) * quarter], 0.0)
            above = jnp.broadcast_to(above, (8, quarter))
            for zy in range(blocks):
                first = pltpu.roll(here, (width - zy * small) % width, 1)[:, :128]
                second = pltpu.roll(above, (quarter - zy * tall) % quarter, 1)[:, :128]
                short[block, zy, :, 0:128] = first
                short[block, zy, :, 128:256] = second

    @pl.when(which == pl.num_programs(0) - 1)
    def _():
        for block in range(4):
            out = (keep, send)[block % 2]
            for zy in range(blocks):
                start = block * rows + zy * small
                for side in range(sides):
                    cols = slice(side * half, (side + 1) * half)
                    parts = [totals[w, start : start + small, cols] for w in range(totals.shape[0])]
                    out[side, block // 2, zy] = jnp.concatenate([*parts, short[block, zy, :, cols]], axis=0).astype(bf16)


def joint_grad(place, grads, inputs, bias_sums, norm_sums, up_sums, small, tall):
    layers = len(grads)
    count, span, n = grads[0].shape
    depth = inputs[0].shape[1]
    blocks = n // 4 // small
    lines = count * small + 8
    out = jax.ShapeDtypeStruct((2, 2, blocks, lines, depth // 2), bf16)
    sums = [*bias_sums, *norm_sums, *up_sums]
    return pl.pallas_call(
        partial(joint_grad_kernel, layers, small, tall),
        grid=(count,),
        in_specs=[SMEM] + [pl.BlockSpec((1, span, n), lambda w: (w, 0, 0))] * layers + [whole((span, depth))] * layers
        + [whole(v.shape) for v in sums],
        out_specs=[whole(out.shape)] * 2,
        out_shape=[out, out],
        scratch_shapes=[
            pltpu.VMEM((n, layers * span), bf16),
            pltpu.VMEM((count, n, depth), f32),
            pltpu.VMEM((4, blocks, 8, depth), f32),
        ],
        compiler_params=params(),
        cost_estimate=pl.CostEstimate(
            flops=2 * layers * span * n * depth * count,
            bytes_accessed=2 * layers * span * (n * count + depth) + 2 * n * depth * count, transcendentals=0),
        name="joint_grad",
    )(place, *grads, *inputs, *sums)


def tall_grad_kernel(layers, place_ref, *refs):
    tall, tall_in, flat, flat_in = (refs[i * layers : (i + 1) * layers] for i in range(4))
    keep, send, turned, flat_total = refs[4 * layers :]
    step = pl.program_id(0)
    core, flip = place_ref[0], place_ref[1]
    sides, _, blocks, rows, half = keep.shape
    flat_rows = flat_total.shape[0] // 4
    small = flat_rows // blocks
    large = rows - small

    def product(left, right):
        total = None
        for layer in range(layers):
            term = dot_nn(left[layer][...].T, right[layer][...])
            total = term if total is None else total + term
        return total

    @pl.when(step == 0)
    def _():
        total = product(flat, flat_in)
        for block in range(4):
            slot = 2 * ((block // 2 + flip) % 2) + (block % 2 + core) % 2
            flat_total[pl.ds(pl.multiple_of(slot * flat_rows, flat_rows), flat_rows), :] = (
                total[block * flat_rows : (block + 1) * flat_rows]
            )

    @pl.when(step > 0)
    def _():
        turned[...] = product(tall, tall_in).astype(bf16)
        slot = step - 1
        for c, out in ((0, keep), (1, send)):
            @pl.when(slot % 2 == c)
            def _():
                for side in range(sides):
                    cols = slice(side * half, (side + 1) * half)
                    for block in range(blocks):
                        out[side, 0, block, :large, :] = turned[block * large : (block + 1) * large, cols]
                        start = pl.multiple_of(slot * flat_rows + block * small, 8)
                        out[side, 0, block, large:, :] = flat_total[pl.ds(start, small), cols].astype(bf16)


def tall_grad(place, tall, tall_in, flat, flat_in):
    layers = len(tall)
    span, n = tall[0].shape
    depth = tall_in[0].shape[1]
    flat_n = flat[0].shape[1]
    rows = n // 4

    def column(s, place):
        slot = jnp.maximum(s - 1, 0)
        return 0, 2 * ((slot // 2 + place[1]) % 2) + (slot % 2 + place[0]) % 2

    def fixed(shape):
        return pl.BlockSpec(shape, lambda s, place: (0, 0))

    blocks = 8
    share = (n + flat_n) // 4 // blocks
    out_spec = pl.BlockSpec(
        (2, 1, blocks, share, depth // 2), lambda s, place: (0, jnp.maximum(s - 1, 0) // 2, 0, 0, 0)
    )
    out = jax.ShapeDtypeStruct((2, 2, blocks, share, depth // 2), bf16)
    return pl.pallas_call(
        partial(tall_grad_kernel, layers),
        grid_spec=pltpu.PrefetchScalarGridSpec(
            num_scalar_prefetch=1,
            grid=(5,),
            in_specs=[pl.BlockSpec((span, rows), column)] * layers + [fixed((span, depth))] * layers
            + [fixed((span, flat_n))] * layers + [fixed((span, depth))] * layers,
            out_specs=[out_spec, out_spec],
            scratch_shapes=[pltpu.VMEM((rows, depth), bf16), pltpu.VMEM((flat_n, depth), f32)],
        ),
        out_shape=[out, out],
        compiler_params=params(),
        cost_estimate=pl.CostEstimate(
            flops=2 * layers * span * (n + flat_n) * depth,
            bytes_accessed=2 * layers * span * (n + flat_n + 2 * depth) + 2 * (n + flat_n) * depth, transcendentals=0),
        name="tall_grad",
    )(place, *tall, *tall_in, *flat, *flat_in)


def pack_kernel(weights, *refs):
    parts, out, rows = refs[:-2], refs[-2], refs[-1]
    rows[...] = jnp.zeros_like(rows)
    start = 0
    for part in parts[:weights]:
        rows[start : start + part.shape[0], :] = part[...].astype(f32)
        start += part.shape[0]
    for index, part in enumerate(parts[weights:-1]):
        rows[start + index : start + index + 1, : part.shape[1]] = part[...].astype(f32)
    rows[start : start + 1, 128 : 128 + parts[-1].shape[1]] = parts[-1][...].astype(f32)
    out[...] = rows[...].astype(bf16)


def pack(vectors, weights=()):
    parts = [*weights, *(vector[None] for vector in vectors)]
    shape = (sum(weight.shape[0] for weight in weights) + 8, weights[0].shape[1] if weights else 256)
    return pl.pallas_call(
        partial(pack_kernel, len(weights)),
        in_specs=[whole(part.shape) for part in parts],
        out_specs=whole(shape),
        out_shape=jax.ShapeDtypeStruct(shape, bf16),
        scratch_shapes=[pltpu.VMEM(shape, f32)],
        name="pack",
    )(*parts)


AXES = ("dp", "fsdp")


def halves(v):
    middle = v.shape[-1] // 2
    return v[..., :middle], v[..., middle:]


def tie(value, after):
    return value if after is None else lax.optimization_barrier((value, after))[0]


class Chain:
    def __init__(self, stages):
        self.stages, self.result, self.landed = stages, None, None
        self.step()

    def step(self, after=None):
        if self.stages is None:
            return self.landed
        try:
            self.landed = self.stages.send(after) if self.landed is not None else next(self.stages)
        except StopIteration as end:
            self.result = end.value
            self.stages = None
        return self.landed

    def finish(self, after=None):
        while self.stages is not None:
            self.step(after)
        return self.result


class Plain:
    def __init__(self, mesh):
        self.devices = math.prod(mesh.shape.values())

    def place(self):
        return jnp.zeros((2,), jnp.int32)

    def spread(self, shards, vectors=None):
        def pieces(full):
            blocks = full.reshape(full.shape[:-2] + (2, 2, full.shape[-2] // 4, full.shape[-1]))
            return tuple(jnp.stack(halves(blocks[..., core, :, :]), axis=-4) for core in range(2))

        full = [lax.all_gather(shard, AXES, axis=0, tiled=True) for shard in shards]
        yield full[0]
        if vectors is None:
            return [pieces(weight) for weight in full]
        return pieces(jnp.stack(full)), lax.all_gather(pack(vectors), AXES, axis=0, tiled=False)

    def reduce(self, keep, send):
        count, sides, xs, rows, half = keep.shape
        both = jnp.stack([keep, send], axis=3).astype(f32)
        full = jnp.moveaxis(both, 1, 4).reshape(count, xs * 2 * rows, sides * half)
        full = lax.psum_scatter(full, AXES, scatter_dimension=1, tiled=True)
        yield full
        return full

    def reduce_joined(self, keep, send, tall, flat):
        large = keep.shape[3] * tall // (tall + flat)
        results = []
        for rows in (slice(0, large), slice(large, None)):
            sides, xs, half = keep.shape[0], keep.shape[1], keep.shape[-1]
            parts = [v[:, :, :, rows].reshape(1, sides, xs, -1, half) for v in (keep, send)]
            results.append(Chain(self.reduce(*parts)).finish())
        yield results[0]
        return jnp.concatenate(results, axis=1)

    def joint_grad(self, place, grads, inputs, bias_sums, norm_sums, up_sums, small, tall):
        bias = sum(jnp.sum(v, axis=(0, 2)) for v in bias_sums)
        norm = sum(jnp.sum(v, axis=1) for v in norm_sums)
        up = sum(jnp.sum(v, axis=0) for v in up_sums)
        lines = jnp.stack([bias[0], bias[1], norm[5], norm[3], norm[4], norm[2], norm[0], norm[1]])
        lines = lines.reshape(8, self.devices, small).transpose(1, 0, 2)
        return (*weight_grad(place, grads, inputs), lines, up.reshape(self.devices, tall))

    def reduce_joint(self, keep, send, lines, up):
        full = Chain(self.reduce(keep, send)).finish()
        lines = lax.psum_scatter(lines, AXES, scatter_dimension=0, tiled=True)[0]
        up = lax.psum_scatter(up, AXES, scatter_dimension=0, tiled=True)
        rows = full.reshape(-1, full.shape[-1])
        yield rows
        short = jnp.zeros((8, full.shape[-1]), f32).at[:, : lines.shape[1]].set(lines).at[:1, 128 : 128 + up.shape[1]].set(up)
        return jnp.concatenate([rows, short], axis=0)


class Grid:
    def __init__(self, mesh):
        pass

    def where(self):
        dp, fsdp = lax.axis_index("dp"), lax.axis_index("fsdp")
        return dp // 2, dp % 2, fsdp // 2, fsdp % 2

    def place(self):
        x, core, _, _ = self.where()
        return jnp.stack([core, x]).astype(jnp.int32)

    def swap(self, value, x=0, core=0, z=0, y=0):
        flip = ((x * 2 + core) * 4 + z) * 2 + y
        return lax.ppermute(value, AXES, [(i, i ^ flip) for i in range(32)])

    def ordered(self, mine, other, side, axis=0):
        return jnp.stack([jnp.where(side == 0, mine, other), jnp.where(side == 0, other, mine)], axis=axis)

    def ordered_z(self, parts, z):
        odd, high = z % 2, z // 2
        parts = [jnp.where(odd == 0, parts[k], parts[k ^ 1]) for k in range(4)]
        return jnp.stack([jnp.where(high == 0, parts[k], parts[k ^ 2]) for k in range(4)])

    def spread(self, shards, vectors=None):
        x, core, z, y = self.where()
        if vectors is not None:
            payload = pack(vectors, shards)
        else:
            payload = jnp.concatenate(shards, axis=0) if len(shards) > 1 else shards[0]
        parts = [payload] + [self.swap(payload, z=k) for k in range(1, 4)]
        parts = tie(parts, (yield parts[1:]))
        left, right = halves(self.ordered_z(parts, z))
        got = self.swap(left, x=1), self.swap(right, y=1)
        got = tie(got, (yield got))
        left = self.ordered(left, got[0], x)
        right = self.ordered(right, got[1], y, axis=1)
        got = self.swap(left, y=1), self.swap(right, x=1)
        got = tie(got, (yield got))
        left = self.ordered(left, got[0], y, axis=2)
        right = self.ordered(right, got[1], x)
        own, start = [], 0
        for shard in shards:
            rows = shard.shape[0]
            own.append(jnp.stack([v[:, :, :, start : start + rows].reshape(2, 8 * rows, -1) for v in (left, right)]))
            start += rows
        if vectors is not None:
            own = [jnp.stack(own), left[:, :, :, start:, :256]]
        other = [self.swap(mine, core=1) for mine in own]
        other = tie(other, (yield other))
        if vectors is None:
            return list(zip(own, other))
        vectors = self.ordered(own[1], other[1], core, axis=1)
        return (own[0], other[0]), vectors.reshape(32, 8, 256)

    def reduce(self, keep, send):
        _, _, z, y = self.where()
        count, _, _, rows, half = keep.shape
        mine = rows // 8

        def add(a, b):
            return (a.astype(f32) + b.astype(f32)).astype(bf16)

        def pick(v, index, axis):
            return lax.dynamic_index_in_dim(v, index, axis, keepdims=False)

        got = self.swap(send, core=1)
        got = tie(got, (yield got))
        total = add(keep, got).reshape(count, 2, 2, 4, 2, mine, half)
        left, right = total[:, 0], total[:, 1]
        got = self.swap(left[:, 1], x=1), self.swap(pick(right, 1 - y, 3), y=1)
        got = tie(got, (yield got))
        left, right = add(left[:, 0], got[0]), add(pick(right, y, 3), got[1])
        got = self.swap(pick(left, 1 - y, 2), y=1), self.swap(right[:, 1], x=1)
        got = tie(got, (yield got))
        left, right = add(pick(left, y, 2), got[0]), add(right[:, 0], got[1])
        both = jnp.concatenate([left, right], axis=-1)
        got = [self.swap(pick(both, z ^ k, 1), z=k) for k in range(1, 4)]
        got = tie(got, (yield got))
        result = pick(both, z, 1).astype(f32)
        for part in got:
            result = result + part.astype(f32)
        return result

    def reduce_joined(self, keep, send, tall, flat):
        shape = (1, 2, 2, -1, keep.shape[-1])
        return self.reduce(keep.reshape(shape), send.reshape(shape))

    def joint_grad(self, *operands):
        return joint_grad(*operands)

    def reduce_joint(self, keep, send):
        shape = (1, 2, 2, -1, keep.shape[-1])
        result = yield from self.reduce(keep.reshape(shape), send.reshape(shape))
        return result[0]


def column_info(values, count):
    return jnp.broadcast_to(values.reshape(count, 1), (count, 128))


def body(
    exchange,
    tokens,
    cotangent,
    segment_ids,
    pad_mask,
    row_counts,
    query_weight,
    query_bias,
    key_weight,
    value_weight,
    value_bias,
    out_weight,
    out_bias,
    first_gain,
    first_shift,
    up_weight,
    up_bias,
    down_weight,
    down_bias,
    second_gain,
    second_shift,
):
    rows_here, row_len, width = tokens.shape
    count = rows_here * row_len
    small, tall = query_bias.shape[0], up_bias.shape[0]
    place = exchange.place()

    first = Chain(
        exchange.spread(
            [query_weight, key_weight, value_weight],
            [query_bias, value_bias, out_bias, first_gain, first_shift, down_bias, second_gain, second_shift, up_bias],
        )
    )
    z_landed = first.landed
    first.step()
    second = Chain(exchange.spread(tie([out_weight, up_weight], z_landed)))
    first.step()
    xy_landed = first.landed
    first.step()
    second.step(xy_landed)
    qkv, vectors = first.finish()
    vectors = vectors.astype(f32)
    devices = vectors.shape[0]
    wide = tall * devices
    vecs = vectors[:, :, :small].transpose(1, 0, 2).reshape(8, width)
    up_vec = jnp.broadcast_to(vectors[:, 0, 128 : 128 + tall].reshape(1, wide), (8, wide))

    present = (jnp.arange(rows_here, dtype=jnp.int32) < row_counts[0]).astype(jnp.int32)
    alive = pad_mask * present[:, None]
    alive_col = column_info(alive, count)
    seg_col = column_info(segment_ids, count)
    seg_row = segment_ids.reshape(rows_here, 1, row_len)
    info = (seg_col, alive_col, seg_row)
    flat = tokens.reshape(count, width)

    landed = second.landed
    second.step()
    third = Chain(exchange.spread([tie(down_weight, landed)]))
    lower_kept = attend_forward(place, tie(flat, landed), *info, vecs, qkv, 0, 1)
    third.step(lower_kept[3])
    lower_kept = attend_forward(place, flat, *info, vecs, qkv, 1, rows_here, lower_kept)
    second.step(lower_kept[3])
    third.step(lower_kept[3])
    out_w, up_w = second.finish()
    mixed, lower_low, lower_act, slope = widen(place, lower_kept[3], flat, vecs, up_vec, out_w, up_w)
    third.step(lower_low)
    (down_w,) = third.finish()
    combined, inputs = narrow(place, lower_act, mixed, vecs, down_w)

    upper_kept = attend_forward(place, inputs, *info, vecs, qkv)
    outputs, upper_low, upper_act, upper_gb, upper_gu, upper_ga, gm, gctx, sums, up_sums = top(
        place, upper_kept[3], combined, cotangent.reshape(count, width), alive_col, vecs, up_vec, out_w, up_w, down_w
    )
    upper_grads, bias_sums = attend_back(*upper_kept[:3], gctx, upper_kept[4], *info)
    lower_gb, lower_gu, lower_ga, gm, gctx, more_sums, more_up_sums = lower(
        place, upper_grads, gm, combined, slope, mixed, vecs, down_w, up_w, out_w, qkv
    )

    keep, send = weight_grad(place, [upper_gb[None], lower_gb[None]], [upper_act, lower_act])
    down_sum = Chain(exchange.reduce(keep, send))
    keep, send = tall_grad(
        place, [upper_gu, tie(lower_gu, keep)], [upper_low, lower_low], [upper_ga, lower_ga], [upper_kept[3], lower_kept[3]]
    )
    up_sum = Chain(exchange.reduce_joined(keep, send, tall, small))
    landed = down_sum.landed
    down_sum.step()
    part = attend_back(*lower_kept[:3], tie(gctx, (keep, landed)), lower_kept[4], *info, 0, 1)
    landed = (down_sum.landed, up_sum.landed)
    down_sum.step()
    up_sum.step()
    lower_grads, more_bias_sums = attend_back(
        *lower_kept[:3], tie(gctx, landed), lower_kept[4], *info, 1, rows_here, part
    )
    landed = (down_sum.landed, up_sum.landed)
    down_sum.step()
    up_sum.step()
    joint = exchange.joint_grad(
        place, [upper_grads, tie(lower_grads, landed)], [inputs, flat],
        [bias_sums, more_bias_sums], [sums, more_sums], [up_sums, more_up_sums], small, tall,
    )
    qkv_sum = Chain(exchange.reduce_joint(*joint))
    landed = (down_sum.landed, up_sum.landed)
    up_sum.step()
    tokens_grad = input_back(place, tie(lower_grads, (joint[0], landed)), gm, qkv)
    qkv_sum.step(tokens_grad)
    up_out = up_sum.finish()[0]
    joint = qkv_sum.finish()
    query_grad, key_grad, value_grad = (joint[i * small : (i + 1) * small] for i in range(3))
    lines = joint[3 * small :]
    piece = [lines[i, :small] for i in range(8)]
    return (
        outputs.reshape(rows_here, row_len, width),
        tokens_grad.reshape(rows_here, row_len, width),
        query_grad,
        piece[QB],
        key_grad,
        value_grad,
        piece[VB],
        up_out[tall:],
        piece[OB],
        piece[G1],
        piece[S1],
        up_out[:tall],
        lines[0, 128 : 128 + tall],
        down_sum.finish()[0],
        piece[DB],
        piece[G2],
        piece[S2],
    )


def solution(mesh):
    rows = P(AXES, None, None)
    flat = P(AXES, None)
    line = P(AXES)
    matrices = (flat, line, flat, flat, line, flat, line, line, line, flat, line, flat, line, line, line)
    exchange = Grid(mesh) if dict(mesh.shape) == {"dp": 4, "fsdp": 8} else Plain(mesh)
    return jax.shard_map(
        partial(body, exchange),
        mesh=mesh,
        in_specs=(rows, rows, flat, flat, line) + matrices,
        out_specs=(rows, rows) + matrices,
        check_vma=False,
    )
```

time: 505 us -> 452 us (0.90)
  waiting for transfers between devices: 96 us -> 71.8 us
  starting transfers between devices: 76.3 us -> 56.1 us
  Pallas kernels: 276 us -> 266 us
  other arithmetic: 24.1 us -> 30.8 us
    ppermute x68 -> x50, waiting for transfers between devices: 96 us -> 71.8 us  [swap(): return lax.ppermute(value, AXES, [(i, i ^ flip) for i in range(32)])]
    pallas_call x3 -> x1, Pallas kernels: 37.4 us -> 15.5 us  [weight_grad(): pl.pallas_call(partial(weight_grad_kernel, layers), grid=(count_w, chunks...]
    ppermute x68 -> x50, starting transfers between devices: 76.3 us -> 56.1 us  [swap(): return lax.ppermute(value, AXES, [(i, i ^ flip) for i in range(32)])]
    convert_element_type x20 -> x15, other arithmetic: 3.25 us -> 14.7 us  [add(): return (a.astype(f32) + b.astype(f32)).astype(bf16)]
    concatenate x3 -> x1, local copies, waits for them, and re-layouts: 6.31 us -> 0.01 us  [spread(): payload = jnp.concatenate(shards, axis=0) if len(shards) > 1 else shards[0]]
    pallas_call x11 -> x12, Pallas kernels: 211 us -> 217 us  [the longest x3 51.5 us: attend_back(): pl.pallas_call(attend_back_kernel, grid=(stop - start, width // QUAD), in...]
    pallas_call x1, Pallas kernels: 16.2 us -> 21.4 us  [tall_grad(): pl.pallas_call(partial(tall_grad_kernel, layers), grid_spec=pltpu.Prefetc...]
  transfers between devices with their start and end apart: 68 -> 50, of which waited for: 23 -> 19; matrix products, arithmetic and copies ran while one was open for 7% -> 9% of each run, Pallas kernels for 23% -> 27%
where the time goes in v2:
time: 452 us; the launch traced here: 447 us
  Pallas kernels  266 us (59%)
  waiting for transfers between devices  71.8 us (16%)
  starting transfers between devices  56.1 us (12%)
  other arithmetic  30.8 us (7%)
  local copies, waits for them, and re-layouts  19.5 us (4%)
    ppermute x50, waiting for transfers between devices, swap(): return lax.ppermute(value, AXES, [(i, i ^ flip) for i in range(32)])  71.8 us
    ppermute x50, starting transfers between devices, swap(): return lax.ppermute(value, AXES, [(i, i ^ flip) for i in range(32)])  56.1 us
    pallas_call x3, Pallas kernels, attend_back(): pl.pallas_call(attend_back_kernel, grid=(stop - start, width // QUAD), in...  51.5 us
    pallas_call x3, Pallas kernels, attend_forward(): pl.pallas_call(attend_forward_kernel, grid=(stop - start, quads), in_spec...  47.5 us
    pallas_call x1, Pallas kernels, top(): pl.pallas_call(top_kernel, grid=(count // TILE,), in_specs=[SMEM, tile, t...  41.2 us
    pallas_call x1, Pallas kernels, lower(): pl.pallas_call(lower_kernel, grid=(count // TILE,), in_specs=[SMEM, pl.Bl...  30.6 us
    pallas_call x1, Pallas kernels, tall_grad(): pl.pallas_call(partial(tall_grad_kernel, layers), grid_spec=pltpu.Prefetc...  21.4 us
    pallas_call x1, Pallas kernels, widen(): pl.pallas_call(widen_kernel, grid=(count // TILE,), in_specs=[SMEM, tile,...  18.2 us
  transfers between devices with their start and end apart: 50, of which 19 were waited for; matrix products, arithmetic and copies ran while one was open for 9% of the time, Pallas kernels for 27%

profile of v2, /device:TPU:0, one launch (start us, length us, event | category | flops | bytes accessed | tf_op | source)
XLA Modules:
  0.0 447.1 jit_solution(13658489357618447714)
XLA Ops:
  10.1 7.7 %collective-permute-done.1 = bf16[80,768]{1,0:T(8,128)(2,1)S(1)} collective-permute-done((bf16[80,768]{1,0:T(8,128)(2,1)}, bf16[80,768]{1,0:T(8,128)(2,1)S(1)}, u32[]{:S(2)}, u32[]{:S(2)}) %collective-permute-start.1) | collective-permute-done | bytes 122912 | tf_op jit(solution)/shard_map/ppermute | solution.py:947
  40.9 4.0 collective-permute-done.10
  48.9 4.9 %collective-permute-done.12 = bf16[4,120,384]{2,1,0:T(8,128)(2,1)S(1)} collective-permute-done((bf16[4,120,384]{2,1,0:T(8,128)(2,1)}, bf16[4,120,384]{2,1,0:T(8,128)(2,1)S(1)}, u32[]{:S(2)}, u32[]{:S(2)}) %collective-permute-start.12) | collective-permute-done | bytes 368672 | tf_op jit(solution)/shard_map/ppermute | solution.py:947
  55.3 4.4 collective-permute-start.18
  68.4 13.0 %attend_forward.3 = (bf16[1024,768]{1,0:T(8,128)(2,1)}, bf16[1024,768]{1,0:T(8,128)(2,1)}, bf16[1024,768]{1,0:T(8,128)(2,1)}, bf16[1024,768]{1,0:T(8,128)(2,1)}, f32[2,3,8,512]{3,2,1,0:T(8,128)}) custom-call(s32[2]{0:T(128)} %pad_add_fusion.core_ref.place_ref, bf16[1024,768]{1,0:T(8,128)(2,1)} %bitcast.319, s32[1024,128]{1,0:T(8,128)} %broadcast_in_dim.56.seg_col, ...), custom_call_target="tpu_custom_call" | custom-call | flops 5033164800 | bytes 7471104 | tf_op jit(solution)/shard_map/attend_forward/pallas_call | solution.py:164
  81.4 12.9 %attend_forward.4 = (bf16[1024,768]{1,0:T(8,128)(2,1)}, bf16[1024,768]{1,0:T(8,128)(2,1)}, bf16[1024,768]{1,0:T(8,128)(2,1)}, bf16[1024,768]{1,0:T(8,128)(2,1)}, f32[2,3,8,512]{3,2,1,0:T(8,128)}) custom-call(s32[2]{0:T(128)} %pad_add_fusion.core_ref.place_ref, ...), custom_call_target="tpu_custom_call", output_to_operand_aliasing={{0}: (8, {}), {1}: (9, {}), {2}: (10, {}), {3}: (11, {}), {... | custom-call | flops 5033164800 | bytes 7471104 | tf_op jit(solution)/shard_map/attend_forward/pallas_call | solution.py:164
  103.5 6.1 %collective-permute-done.21 = bf16[4,24,1536]{2,1,0:T(8,128)(2,1)S(1)} collective-permute-done((bf16[4,24,1536]{2,1,0:T(8,128)(2,1)S(1)}, bf16[4,24,1536]{2,1,0:T(8,128)(2,1)S(1)}, u32[]{:S(2)}, u32[]{:S(2)}) %collective-permute-start.21) | collective-permute-done | bytes 294944 | tf_op jit(solution)/shard_map/ppermute | solution.py:947
  115.5 18.2 %widen.1 = (f32[1024,768]{1,0:T(8,128)}, bf16[1024,768]{1,0:T(8,128)(2,1)}, bf16[1024,3072]{1,0:T(8,128)(2,1)}, bf16[1024,3072]{1,0:T(8,128)(2,1)}) custom-call(s32[2]{0:T(128)} %pad_add_fusion.core_ref.place_ref, bf16[1024,768]{1,0:T(8,128)(2,1)} %get-tuple-element.103.ctx.refs_7_, bf16[1024,768]{1,0:T(8,128)(2,1)} %bitcast.321, f32[8,768]{1,0:T(8,128)} %reshape.344.vecs, ...), custom_call_target="tpu_custom_call" | custom-call | flops 6039797760 | bytes 22020096 | tf_op jit(solution)/shard_map/widen/pallas_call | solution.py:236
  134.6 4.5 %collective-permute-done.25.d_sib = bf16[2,2,192,1536]{3,2,1,0:T(8,128)(2,1)S(1)} collective-permute-done((bf16[2,2,192,1536]{3,2,1,0:T(8,128)(2,1)S(1)}, bf16[2,2,192,1536]{3,2,1,0:T(8,128)(2,1)S(1)}, u32[]{:S(2)}, u32[]{:S(2)}) %collective-permute-start.25) | collective-permute-done | bytes 2359328 | tf_op jit(solution)/shard_map/ppermute | solution.py:947
  140.6 12.4 %narrow.1 = (f32[1024,768]{1,0:T(8,128)}, bf16[1024,768]{1,0:T(8,128)(2,1)}) custom-call(s32[2]{0:T(128)} %pad_add_fusion.core_ref.place_ref, bf16[1024,3072]{1,0:T(8,128)(2,1)} %get-tuple-element.106.act.refs_3_, f32[1024,768]{1,0:T(8,128)} %get-tuple-element.107.mixed, f32[8,768]{1,0:T(8,128)} %reshape.344.vecs, bf16[2,2,192,1536]{3,2,1,0:T(8,128)(2,1)} %copy-done.11, ...), custom_call_target="tpu_custom_call" | custom-call | flops 4831838208 | bytes 14155776 | tf_op jit(solution)/shard_map/narrow/pallas_call | solution.py:281
  152.9 21.7 %attend_forward.5 = (bf16[1024,768]{1,0:T(8,128)(2,1)}, bf16[1024,768]{1,0:T(8,128)(2,1)}, bf16[1024,768]{1,0:T(8,128)(2,1)}, bf16[1024,768]{1,0:T(8,128)(2,1)}, f32[2,3,8,512]{3,2,1,0:T(8,128)}) custom-call(s32[2]{0:T(128)} %pad_add_fusion.core_ref.place_ref, bf16[1024,768]{1,0:T(8,128)(2,1)} %get-tuple-element.118.x.refs_2_, ...), custom_call_target="tpu_custom_call" | custom-call | flops 10066329600 | bytes 11403264 | tf_op jit(solution)/shard_map/attend_forward/pallas_call | solution.py:164
  174.6 41.2 %top.1 = (bf16[1024,768]{1,0:T(8,128)(2,1)}, bf16[1024,768]{1,0:T(8,128)(2,1)}, bf16[1024,3072]{1,0:T(8,128)(2,1)}, bf16[1024,768]{1,0:T(8,128)(2,1)}, bf16[1024...) custom-call(s32[2]{0:T(128)} %pad_add_fusion.core_ref.place_ref, ...), custom_call_target="tpu_custom_call" | custom-call | flops 21743271936 | bytes 29884416 | tf_op jit(solution)/shard_map/top/pallas_call | solution.py:386
  215.8 24.3 %attend_back.3 = (bf16[3,1024,768]{2,1,0:T(8,128)(2,1)}, f32[2,2,8,768]{3,2,1,0:T(8,128)}) custom-call(bf16[1024,768]{1,0:T(8,128)(2,1)} %get-tuple-element.125.q, bf16[1024,768]{1,0:T(8,128)(2,1)} %get-tuple-element.126.k, bf16[1024,768]{1,0:T(8,128)(2,1)} %get-tuple-element.127.v, bf16[1024,768]{1,0:T(8,128)(2,1)} %get-tuple-element.128.gctx, ...), custom_call_target="tpu_custom_call" | custom-call | flops 16106127360 | bytes 12582912 | tf_op jit(solution)/shard_map/attend_back/pallas_call | solution.py:534
  240.0 30.6 %lower.1 = (bf16[1024,768]{1,0:T(8,128)(2,1)}, bf16[1024,3072]{1,0:T(8,128)(2,1)}, bf16[1024,768]{1,0:T(8,128)(2,1)}, f32[1024,768]{1,0:T(8,128)}, bf16[1024,768...) custom-call(s32[2]{0:T(128)} %pad_add_fusion.core_ref.place_ref, ...), custom_call_target="tpu_custom_call" | custom-call | flops 14495514624 | bytes 36175872 | tf_op jit(solution)/shard_map/lower/pallas_call | solution.py:462
  270.6 15.5 %weight_grad.1 = (bf16[1,2,2,192,1536]{4,3,2,1,0:T(8,128)(2,1)}, bf16[1,2,2,192,1536]{4,3,2,1,0:T(8,128)(2,1)}) custom-call(s32[2]{0:T(128)} %pad_add_fusion.core_ref.place_ref, bf16[1,1024,768]{2,1,0:T(8,128)(2,1)} %bitcast.324, bf16[1,1024,768]{2,1,0:T(8,128)(2,1)} %bitcast.325, bf16[1024,3072]{1,0:T(8,128)(2,1)} %get-tuple-element.136.refs_2_, ...), custom_call_target="tpu_custom_call" | custom-call | flops 9663676416 | bytes 20447232 | tf_op jit(solution)/shard_map/weight_grad/pallas_call | solution.py:636
  286.2 21.4 %tall_grad.1 = (bf16[2,2,8,120,384]{4,3,2,1,0:T(8,128)(2,1)}, bf16[2,2,8,120,384]{4,3,2,1,0:T(8,128)(2,1)}) custom-call(s32[2]{0:T(128)} %pad_add_fusion.core_ref.place_ref, bf16[1024,3072]{1,0:T(8,128)(2,1)} %get-tuple-element.139.refs_0_, bf16[1024,3072]{1,0:T(8,128)(2,1)} %get-tuple-element.141.refs_1_, bf16[1024,768]{1,0:T(8,128)(2,1)} %get-tuple-element.142.refs_2_, ...), custom_call_target="tpu_custom_call" | custom-call | flops 12079595520 | bytes 27918336 | tf_op jit(solution)/shard_map/tall_grad/pallas_call | solution.py:801
  314.4 13.5 %attend_back.4 = (bf16[3,1024,768]{2,1,0:T(8,128)(2,1)}, f32[2,2,8,768]{3,2,1,0:T(8,128)}) custom-call(bf16[1024,768]{1,0:T(8,128)(2,1)} %get-tuple-element.122.q, bf16[1024,768]{1,0:T(8,128)(2,1)} %get-tuple-element.123.k, bf16[1024,768]{1,0:T(8,128)(2,1)} %get-tuple-element.124.v, bf16[1024,768]{1,0:T(8,128)(2,1)} %get-tuple-element.149.gctx, ...), custom_call_target="tpu_custom_call" | custom-call | flops 8053063680 | bytes 6291456 | tf_op jit(solution)/shard_map/attend_back/pallas_call | solution.py:534
  341.7 13.7 %attend_back.5 = (bf16[3,1024,768]{2,1,0:T(8,128)(2,1)}, f32[2,2,8,768]{3,2,1,0:T(8,128)}) custom-call(bf16[1024,768]{1,0:T(8,128)(2,1)} %get-tuple-element.122.q, bf16[1024,768]{1,0:T(8,128)(2,1)} %get-tuple-element.123.k, bf16[1024,768]{1,0:T(8,128)(2,1)} %get-tuple-element.124.v, ...), custom_call_target="tpu_custom_call", output_to_operand_aliasing={{0}: (8, {}), {1}: (9, {})} | custom-call | flops 8053063680 | bytes 6291456 | tf_op jit(solution)/shard_map/attend_back/pallas_call | solution.py:534
  355.4 3.3 collective-permute-done.31
  367.8 16.4 %joint_grad.1 = (bf16[2,2,8,80,384]{4,3,2,1,0:T(8,128)(2,1)}, bf16[2,2,8,80,384]{4,3,2,1,0:T(8,128)(2,1)}) custom-call(s32[2]{0:T(128)} %pad_add_fusion.core_ref.place_ref, bf16[3,1024,768]{2,1,0:T(8,128)(2,1)} %get-tuple-element.130.grads.refs_0_, bf16[3,1024,768]{2,1,0:T(8,128)(2,1)} %get-tuple-element.161.refs_1_.grads, ...), custom_call_target="tpu_custom_call" | custom-call | flops 7247757312 | bytes 16121856 | tf_op jit(solution)/shard_map/joint_grad/pallas_call | solution.py:720
  388.1 8.6 %collective-permute-done.37 = bf16[1,4,120,384]{3,2,1,0:T(8,128)(2,1)S(1)} collective-permute-done((bf16[1,4,120,384]{3,2,1,0:T(8,128)(2,1)S(1)}, bf16[1,4,120,384]{3,2,1,0:T(8,128)(2,1)S(1)}, u32[]{:S(2)}, u32[]{:S(2)}) %collective-permute-start.37) | collective-permute-done | bytes 368672 | tf_op jit(solution)/shard_map/ppermute | solution.py:947
  402.4 10.1 %input_back.1 = f32[1024,768]{1,0:T(8,128)} custom-call(s32[2]{0:T(128)} %pad_add_fusion.core_ref.place_ref, bf16[3,1024,768]{2,1,0:T(8,128)(2,1)} %get-tuple-element.161.refs_1_.grads, f32[1024,768]{1,0:T(8,128)} %get-tuple-element.162.gm, bf16[3,2,2,192,384]{4,3,2,1,0:T(8,128)(2,1)} %copy-done, bf16[3,2,2,192,384]{4,3,2,1,0:T(8,128)(2,1)} %collective-permute-done.8.sib.q_sib), custom_call_target="tpu_custom_call" | custom-call | flops 3623878656 | bytes 11010048 | tf_op jit(solution)/shard_map/input_back/pallas_call | solution.py:575
  417.3 9.6 %collective-permute-done.42 = bf16[1,2,4,80,384]{4,3,2,1,0:T(8,128)(2,1)S(1)} collective-permute-done((bf16[1,2,4,80,384]{4,3,2,1,0:T(8,128)(2,1)S(1)}, bf16[1,2,4,80,384]{4,3,2,1,0:T(8,128)(2,1)S(1)}, u32[]{:S(2)}, u32[]{:S(2)}) %collective-permute-start.42) | collective-permute-done | bytes 491552 | tf_op jit(solution)/shard_map/ppermute | solution.py:947
  441.4 3.4 collective-permute-done.45
  (252 shorter events, 123.2 us)
Async XLA Ops:
  40.3 25.6 %collective-permute-start.8 = (bf16[3,2,2,192,384]{4,3,2,1,0:T(8,128)(2,1)S(1)}, bf16[3,2,2,192,384]{4,3,2,1,0:T(8,128)(2,1)}, u32[]{:S(2)}, u32[]{:S(2)}) collective-permute-start(bf16[3,2,2,192,384]{4,3,2,1,0:T(8,128)(2,1)S(1)} %pad_maximum_fusion.1.own.q_own), channel_id=1, source_target_pairs={{0,8},{1,9},{2,10},{3,11},{4,12},{5,13},{6,14},{7,15},{8,0},{9,1},... | collective-permute-start | bytes 5308424 | tf_op jit(solution)/shard_map/ppermute | solution.py:947
  55.3 26.1 %collective-permute-start.18 = (bf16[24,3072]{1,0:T(8,128)(2,1)}, bf16[24,3072]{1,0:T(8,128)(2,1)}, u32[]{:S(2)}, u32[]{:S(2)}) collective-permute-start(bf16[24,3072]{1,0:T(8,128)(2,1)} %param.36), channel_id=1, source_target_pairs={{0,2},{1,3},{2,0},{3,1},{4,6},{5,7},{6,4},{7,5},{8,10},{9,11},{10,... | collective-permute-start | bytes 442376 | tf_op jit(solution)/shard_map/ppermute | solution.py:947
  59.8 21.6 %collective-permute-start.19 = (bf16[24,3072]{1,0:T(8,128)(2,1)}, bf16[24,3072]{1,0:T(8,128)(2,1)}, u32[]{:S(2)}, u32[]{:S(2)}) collective-permute-start(bf16[24,3072]{1,0:T(8,128)(2,1)} %param.36), channel_id=1, source_target_pairs={{0,4},{1,5},{2,6},{3,7},{4,0},{5,1},{6,2},{7,3},{8,12},{9,13},{10,... | collective-permute-start | bytes 442376 | tf_op jit(solution)/shard_map/ppermute | solution.py:947
  59.8 21.6 %collective-permute-start.20 = (bf16[24,3072]{1,0:T(8,128)(2,1)}, bf16[24,3072]{1,0:T(8,128)(2,1)}, u32[]{:S(2)}, u32[]{:S(2)}) collective-permute-start(bf16[24,3072]{1,0:T(8,128)(2,1)} %param.36), channel_id=1, source_target_pairs={{0,6},{1,7},{2,4},{3,5},{4,2},{5,3},{6,0},{7,1},{8,14},{9,15},{10,... | collective-permute-start | bytes 442376 | tf_op jit(solution)/shard_map/ppermute | solution.py:947
  64.4 29.9 %collective-permute-start.15 = (bf16[4,2,120,384]{3,2,0,1:T(8,128)(2,1)}, bf16[4,2,120,384]{3,2,0,1:T(8,128)(2,1)S(1)}, u32[]{:S(2)}, u32[]{:S(2)}) collective-permute-start(bf16[4,2,120,384]{3,2,0,1:T(8,128)(2,1)} %pad_maximum_fusion.7), channel_id=1, source_target_pairs={{0,16},{1,17},{2,18},{3,19},{4,20},{5,21},{6,22},{7,23},{8,24},{9,... | collective-permute-start | bytes 2211848 | tf_op jit(solution)/shard_map/ppermute | solution.py:947
  65.9 28.4 %collective-permute-start.14 = (bf16[2,4,120,384]{3,2,1,0:T(8,128)(2,1)}, bf16[2,4,120,384]{3,2,1,0:T(8,128)(2,1)S(1)}, u32[]{:S(2)}, u32[]{:S(2)}) collective-permute-start(bf16[2,4,120,384]{3,2,1,0:T(8,128)(2,1)} %pad_maximum_fusion.6), channel_id=1, source_target_pairs={{0,1},{1,0},{2,3},{3,2},{4,5},{5,4},{6,7},{7,6},{8,9},{9,8},{10,11... | collective-permute-start | bytes 2211848 | tf_op jit(solution)/shard_map/ppermute | solution.py:947
  111.8 22.0 %collective-permute-start.24 = (bf16[4,2,24,1536]{3,2,0,1:T(8,128)(2,1)}, bf16[4,2,24,1536]{3,2,0,1:T(8,128)(2,1)S(1)}, u32[]{:S(2)}, u32[]{:S(2)}) collective-permute-start(bf16[4,2,24,1536]{3,2,0,1:T(8,128)(2,1)} %pad_maximum_fusion.11), channel_id=1, source_target_pairs={{0,16},{1,17},{2,18},{3,19},{4,20},{5,21},{6,22},{7,23},{8,24},{9,... | collective-permute-start | bytes 1769480 | tf_op jit(solution)/shard_map/ppermute | solution.py:947
  113.2 20.6 %collective-permute-start.23 = (bf16[2,4,24,1536]{3,2,1,0:T(8,128)(2,1)}, bf16[2,4,24,1536]{3,2,1,0:T(8,128)(2,1)S(1)}, u32[]{:S(2)}, u32[]{:S(2)}) collective-permute-start(bf16[2,4,24,1536]{3,2,1,0:T(8,128)(2,1)} %pad_maximum_fusion.10), channel_id=1, source_target_pairs={{0,1},{1,0},{2,3},{3,2},{4,5},{5,4},{6,7},{7,6},{8,9},{9,8},{10,11... | collective-permute-start | bytes 1769480 | tf_op jit(solution)/shard_map/ppermute | solution.py:947
  286.1 21.9 %collective-permute-start.26 = (bf16[1,2,2,192,1536]{4,3,2,1,0:T(8,128)(2,1)}, bf16[1,2,2,192,1536]{4,3,2,1,0:T(8,128)(2,1)}, u32[]{:S(2)}, u32[]{:S(2)}) collective-permute-start(bf16[1,2,2,192,1536]{4,3,2,1,0:T(8,128)(2,1)} %get-tuple-element.138), channel_id=1, source_target_pairs={{0,8},{1,9},{2,10},{3,11},{4,12},{5,13},{6,14},{7,15},{8,0},{9,1},... | collective-permute-start | bytes 7077896 | tf_op jit(solution)/shard_map/ppermute | solution.py:947
  307.6 20.3 %collective-permute-start.29 = (bf16[1,2,2,960,384]{4,3,2,1,0:T(8,128)(2,1)}, bf16[1,2,2,960,384]{4,3,2,1,0:T(8,128)(2,1)}, u32[]{:S(2)}, u32[]{:S(2)}) collective-permute-start(bf16[1,2,2,960,384]{4,3,2,1,0:T(8,128)(2,1)} %bitcast.316), channel_id=1, source_target_pairs={{0,8},{1,9},{2,10},{3,11},{4,12},{5,13},{6,14},{7,15},{8,0},{9,1},... | collective-permute-start | bytes 8847368 | tf_op jit(solution)/shard_map/ppermute | solution.py:947
  311.5 23.4 %collective-permute-start.28 = (bf16[1,2,4,24,1536]{4,3,2,1,0:T(8,128)(2,1)}, bf16[1,2,4,24,1536]{4,3,2,1,0:T(8,128)(2,1)}, u32[]{:S(2)}, u32[]{:S(2)}) collective-permute-start(bf16[1,2,4,24,1536]{4,3,2,1,0:T(8,128)(2,1)} %dynamic-slice_bitcast_fusion.1), channel_id=1, source_target_pairs={{0,1},{1,0},{2,3},{3,2},{4,5},{5,4},{6,7},{7,6},{8,9},{9,8},{10,11... | collective-permute-start | bytes 1769480 | tf_op jit(solution)/shard_map/ppermute | solution.py:947
  313.0 25.4 %collective-permute-start.27 = (bf16[1,4,2,24,1536]{4,3,1,2,0:T(8,128)(2,1)}, bf16[1,4,2,24,1536]{4,3,1,2,0:T(8,128)(2,1)}, u32[]{:S(2)}, u32[]{:S(2)}) collective-permute-start(bf16[1,4,2,24,1536]{4,3,1,2,0:T(8,128)(2,1)} %slice_bitcast_fusion.3), channel_id=1, source_target_pairs={{0,16},{1,17},{2,18},{3,19},{4,20},{5,21},{6,22},{7,23},{8,24},{9,... | collective-permute-start | bytes 1769480 | tf_op jit(solution)/shard_map/ppermute | solution.py:947
  331.7 33.5 %collective-permute-start.33 = (bf16[1,2,4,120,384]{4,3,2,1,0:T(8,128)(2,1)}, bf16[1,2,4,120,384]{4,3,2,1,0:T(8,128)(2,1)}, u32[]{:S(2)}, u32[]{:S(2)}) collective-permute-start(bf16[1,2,4,120,384]{4,3,2,1,0:T(8,128)(2,1)} %dynamic-slice_bitcast_fusion), channel_id=1, source_target_pairs={{0,1},{1,0},{2,3},{3,2},{4,5},{5,4},{6,7},{7,6},{8,9},{9,8},{10,11... | collective-permute-start | bytes 2211848 | tf_op jit(solution)/shard_map/ppermute | solution.py:947
  334.3 33.5 %collective-permute-start.32 = (bf16[1,4,2,120,384]{4,3,1,2,0:T(8,128)(2,1)}, bf16[1,4,2,120,384]{4,3,1,2,0:T(8,128)(2,1)}, u32[]{:S(2)}, u32[]{:S(2)}) collective-permute-start(bf16[1,4,2,120,384]{4,3,1,2,0:T(8,128)(2,1)} %slice_bitcast_fusion.1), channel_id=1, source_target_pairs={{0,16},{1,17},{2,18},{3,19},{4,20},{5,21},{6,22},{7,23},{8,24},{9,... | collective-permute-start | bytes 2211848 | tf_op jit(solution)/shard_map/ppermute | solution.py:947
  336.9 21.7 %collective-permute-start.31 = (bf16[1,4,24,1536]{3,2,1,0:T(8,128)(2,1)}, bf16[1,4,24,1536]{3,2,1,0:T(8,128)(2,1)}, u32[]{:S(2)}, u32[]{:S(2)}) collective-permute-start(bf16[1,4,24,1536]{3,2,1,0:T(8,128)(2,1)} %slice_bitcast_fusion.10), channel_id=1, source_target_pairs={{0,16},{1,17},{2,18},{3,19},{4,20},{5,21},{6,22},{7,23},{8,24},{9,... | collective-permute-start | bytes 884744 | tf_op jit(solution)/shard_map/ppermute | solution.py:947
  341.2 18.6 %collective-permute-start.30 = (bf16[1,4,24,1536]{3,2,1,0:T(8,128)(2,1)}, bf16[1,4,24,1536]{3,2,1,0:T(8,128)(2,1)S(1)}, u32[]{:S(2)}, u32[]{:S(2)}) collective-permute-start(bf16[1,4,24,1536]{3,2,1,0:T(8,128)(2,1)} %dynamic-slice_bitcast_fusion.4), channel_id=1, source_target_pairs={{0,1},{1,0},{2,3},{3,2},{4,5},{5,4},{6,7},{7,6},{8,9},{9,8},{10,11... | collective-permute-start | bytes 884744 | tf_op jit(solution)/shard_map/ppermute | solution.py:947
  360.8 24.9 %collective-permute-start.34 = (bf16[1,24,3072]{2,1,0:T(8,128)(2,1)}, bf16[1,24,3072]{2,1,0:T(8,128)(2,1)S(1)}, u32[]{:S(2)}, u32[]{:S(2)}) collective-permute-start(bf16[1,24,3072]{2,1,0:T(8,128)(2,1)} %get-tuple-element.213), channel_id=1, source_target_pairs={{0,2},{1,3},{2,0},{3,1},{4,6},{5,7},{6,4},{7,5},{8,10},{9,11},{10,... | collective-permute-start | bytes 442376 | tf_op jit(solution)/shard_map/ppermute | solution.py:947
  361.9 24.4 %collective-permute-start.35 = (bf16[1,24,3072]{2,1,0:T(8,128)(2,1)}, bf16[1,24,3072]{2,1,0:T(8,128)(2,1)}, u32[]{:S(2)}, u32[]{:S(2)}) collective-permute-start(bf16[1,24,3072]{2,1,0:T(8,128)(2,1)} %get-tuple-element.214), channel_id=1, source_target_pairs={{0,4},{1,5},{2,6},{3,7},{4,0},{5,1},{6,2},{7,3},{8,12},{9,13},{10,... | collective-permute-start | bytes 442376 | tf_op jit(solution)/shard_map/ppermute | solution.py:947
  362.8 23.5 %collective-permute-start.36 = (bf16[1,24,3072]{2,1,0:T(8,128)(2,1)}, bf16[1,24,3072]{2,1,0:T(8,128)(2,1)}, u32[]{:S(2)}, u32[]{:S(2)}) collective-permute-start(bf16[1,24,3072]{2,1,0:T(8,128)(2,1)} %get-tuple-element.212), channel_id=1, source_target_pairs={{0,6},{1,7},{2,4},{3,5},{4,2},{5,3},{6,0},{7,1},{8,14},{9,15},{10,... | collective-permute-start | bytes 442376 | tf_op jit(solution)/shard_map/ppermute | solution.py:947
  367.3 29.5 %collective-permute-start.38 = (bf16[1,4,120,384]{3,2,1,0:T(8,128)(2,1)}, bf16[1,4,120,384]{3,2,1,0:T(8,128)(2,1)}, u32[]{:S(2)}, u32[]{:S(2)}) collective-permute-start(bf16[1,4,120,384]{3,2,1,0:T(8,128)(2,1)} %slice_bitcast_fusion.7), channel_id=1, source_target_pairs={{0,16},{1,17},{2,18},{3,19},{4,20},{5,21},{6,22},{7,23},{8,24},{9,... | collective-permute-start | bytes 1105928 | tf_op jit(solution)/shard_map/ppermute | solution.py:947
  384.2 28.3 %collective-permute-start.39 = (bf16[1,2,2,640,384]{4,3,2,1,0:T(8,128)(2,1)}, bf16[1,2,2,640,384]{4,3,2,1,0:T(8,128)(2,1)}, u32[]{:S(2)}, u32[]{:S(2)}) collective-permute-start(bf16[1,2,2,640,384]{4,3,2,1,0:T(8,128)(2,1)} %bitcast.317), channel_id=1, source_target_pairs={{0,8},{1,9},{2,10},{3,11},{4,12},{5,13},{6,14},{7,15},{8,0},{9,1},... | collective-permute-start | bytes 5898248 | tf_op jit(solution)/shard_map/ppermute | solution.py:947
  398.0 19.2 %collective-permute-start.47 = (bf16[1,120,768]{2,1,0:T(8,128)(2,1)S(1)}, bf16[1,120,768]{2,1,0:T(8,128)(2,1)S(1)}, u32[]{:S(2)}, u32[]{:S(2)}) collective-permute-start(bf16[1,120,768]{2,1,0:T(8,128)(2,1)S(1)} %get-tuple-element.197), channel_id=1, source_target_pairs={{0,2},{1,3},{2,0},{3,1},{4,6},{5,7},{6,4},{7,5},{8,10},{9,11},{10,... | collective-permute-start | bytes 552968 | tf_op jit(solution)/shard_map/ppermute | solution.py:947
  398.3 18.9 %collective-permute-start.48 = (bf16[1,120,768]{2,1,0:T(8,128)(2,1)S(1)}, bf16[1,120,768]{2,1,0:T(8,128)(2,1)S(1)}, u32[]{:S(2)}, u32[]{:S(2)}) collective-permute-start(bf16[1,120,768]{2,1,0:T(8,128)(2,1)S(1)} %get-tuple-element.198), channel_id=1, source_target_pairs={{0,4},{1,5},{2,6},{3,7},{4,0},{5,1},{6,2},{7,3},{8,12},{9,13},{10,... | collective-permute-start | bytes 552968 | tf_op jit(solution)/shard_map/ppermute | solution.py:947
  400.1 17.1 %collective-permute-start.49 = (bf16[1,120,768]{2,1,0:T(8,128)(2,1)S(1)}, bf16[1,120,768]{2,1,0:T(8,128)(2,1)S(1)}, u32[]{:S(2)}, u32[]{:S(2)}) collective-permute-start(bf16[1,120,768]{2,1,0:T(8,128)(2,1)S(1)} %get-tuple-element.199), channel_id=1, source_target_pairs={{0,6},{1,7},{2,4},{3,5},{4,2},{5,3},{6,0},{7,1},{8,14},{9,15},{10,... | collective-permute-start | bytes 552968 | tf_op jit(solution)/shard_map/ppermute | solution.py:947
  (49 other events, 410.5 us)

commit v3 on v2

--- a/solution.py
+++ b/solution.py
@@ -30,6 +30,10 @@
     return lax.dot_general(left, right, (((1,), (0,)), ((), ())), preferred_element_type=f32)
 
 
+def dot_tn(left, right):
+    return lax.dot_general(left, right, (((0,), (0,)), ((), ())), preferred_element_type=f32)
+
+
 def normalize(v):
     mean = jnp.mean(v, axis=-1, keepdims=True)
     centered = v - mean
@@ -52,6 +56,11 @@
     copies = []
     for sibling, piece in enumerate(pieces):
         source = piece if which is None else piece.at[which]
+        if len(source.shape) == 2:
+            rows = source.shape[0] // 2
+            part = slice(sibling * rows, (sibling + 1) * rows)
+            copies.append(pltpu.make_async_copy(source.at[part, :], place.at[part, :], sems.at[4 * sibling]))
+            continue
         sides, _, rows, half = source.shape
         for side in range(sides):
             for x in range(2):
@@ -321,8 +330,6 @@
         sums[...] = jnp.zeros_like(sums)
         up_sums[...] = jnp.zeros_like(up_sums)
         wait_all(out_copies)
-        wait_all(up_copies)
-        wait_all(down_copies)
 
     width = ctx.shape[1]
     chunks = [slice(c * width, (c + 1) * width) for c in range(up_weight.shape[0] // width)]
@@ -334,6 +341,12 @@
         combined = first_unit * vecs[G1 : G1 + 1, :] + vecs[S1 : S1 + 1, :]
         low = combined.astype(bf16)
         low_out[rows, :] = low
+
+        @pl.when(first)
+        def _():
+            wait_all(up_copies)
+            wait_all(down_copies)
+
         for cols in chunks:
             act, slope = gelu_both(dot_nt(low, up_weight[cols, :]) + up_bias[0:1, cols])
             act = act.astype(bf16)
@@ -431,9 +444,6 @@
         up_sums[...] = jnp.zeros_like(up_sums)
         for group in copies:
             wait_all(group)
-        wait_all(down_copies)
-        wait_all(up_copies)
-        wait_all(out_copies)
 
     width = gm.shape[1]
     chunks = [slice(c * width, (c + 1) * width) for c in range(up_weight.shape[0] // width)]
@@ -447,6 +457,13 @@
         sums[1] += partial_sum(grad)
         grad = normalize_back(grad, vecs[G2 : G2 + 1, :], unit, rstd)
         first_unit, first_rstd = normalize(mixed[rows, :])
+
+        @pl.when(first)
+        def _():
+            wait_all(down_copies)
+            wait_all(up_copies)
+            wait_all(out_copies)
+
         feed_back_rows(
             rows, chunks, grad, slope, first_unit, first_rstd, vecs, down_weight, up_weight, out_weight,
             gb_out, gu_out, ga_out, gm_out, gctx_out, sums, up_sums,
@@ -586,36 +603,31 @@
     )(core, grads, gm, *qkv)
 
 
+def store_blocks(core, flip, total, put):
+    rows = total.shape[0] // 4
+    for block in range(4):
+        x, c = block // 2, block % 2
+        part = total[block * rows : (block + 1) * rows]
+        for side in range(2):
+            @pl.when(core == (c + side) % 2)
+            def _():
+                put(side, (x + flip) % 2, part)
+
+
 def weight_grad_kernel(layers, place_ref, *refs):
     grads, inputs = refs[:layers], refs[layers : 2 * layers]
-    keep, send, turned = refs[2 * layers :]
-    core, flip = place_ref[0], place_ref[1]
-    rows = turned.shape[0] // 4
-    span = grads[0].shape[-2]
-
-    @pl.when(pl.program_id(1) == 0)
-    def _():
-        for layer in range(layers):
-            flat = grads[layer][0].T
-            for block in range(4):
-                x, c = block // 2, block % 2
-                slot = 2 * ((x + flip) % 2) + (c + core) % 2
-                turned[pl.ds(pl.multiple_of(slot * rows, rows), rows), layer * span : (layer + 1) * span] = (
-                    flat[block * rows : (block + 1) * rows]
-                )
-
+    outs = refs[2 * layers :]
     total = None
     for layer in range(layers):
-        term = dot_nn(turned[:, layer * span : (layer + 1) * span], inputs[layer][...])
+        term = dot_tn(grads[layer][0], inputs[layer][...])
         total = term if total is None else total + term
-    total = total.astype(bf16)
-    halves = keep.shape[1]
-    wide = keep.shape[-1]
-    for half in range(halves):
-        for x in range(2):
-            for c, out in ((0, keep), (1, send)):
-                start = (2 * x + c) * rows
-                out[0, half, x] = total[start : start + rows, half * wide : (half + 1) * wide]
+    halves, wide = outs[0].shape[1], outs[0].shape[-1]
+
+    def put(side, x, part):
+        for half in range(halves):
+            outs[side][0, half, x] = part[:, half * wide : (half + 1) * wide]
+
+    store_blocks(place_ref[0], place_ref[1], total.astype(bf16), put)
 
 
 def weight_grad(place, grads, inputs):
@@ -640,7 +652,6 @@
         + [pl.BlockSpec((span, chunk), lambda w, j: (0, j))] * layers,
         out_specs=[out_spec, out_spec],
         out_shape=[out, out],
-        scratch_shapes=[pltpu.VMEM((n, layers * span), bf16)],
         compiler_params=params(),
         cost_estimate=pl.CostEstimate(
             flops=2 * layers * span * n * depth * count_w,
@@ -652,28 +663,22 @@
 def joint_grad_kernel(layers, small, tall, place_ref, *refs):
     grads, inputs = refs[:layers], refs[layers : 2 * layers]
     bias_sums, norm_sums, up_sums = (refs[(2 + i) * layers : (3 + i) * layers] for i in range(3))
-    keep, send, turned, totals, short = refs[5 * layers :]
+    keep, send, totals, short = refs[5 * layers :]
     core, flip = place_ref[0], place_ref[1]
     which = pl.program_id(0)
     sides, _, blocks, _, half = keep.shape
-    width = turned.shape[0]
+    width = totals.shape[1]
     rows = width // 4
-    span = inputs[0].shape[0]
 
     def slot(block):
         return 2 * ((block // 2 + flip) % 2) + (block % 2 + core) % 2
 
-    for layer in range(layers):
-        flat = grads[layer][0].T
-        for block in range(4):
-            turned[pl.ds(pl.multiple_of(slot(block) * rows, rows), rows), layer * span : (layer + 1) * span] = (
-                flat[block * rows : (block + 1) * rows]
-            )
     total = None
     for layer in range(layers):
-        term = dot_nn(turned[:, layer * span : (layer + 1) * span], inputs[layer][...])
+        term = dot_tn(grads[layer][0], inputs[layer][...])
         total = term if total is None else total + term
-    totals[which] = total
+    for block in range(4):
+        totals[which, pl.ds(pl.multiple_of(slot(block) * rows, rows), rows), :] = total[block * rows : (block + 1) * rows]
 
     @pl.when(which == 0)
     def _():
@@ -725,7 +730,6 @@
         out_specs=[whole(out.shape)] * 2,
         out_shape=[out, out],
         scratch_shapes=[
-            pltpu.VMEM((n, layers * span), bf16),
             pltpu.VMEM((count, n, depth), f32),
             pltpu.VMEM((4, blocks, 8, depth), f32),
         ],
@@ -750,7 +754,7 @@
     def product(left, right):
         total = None
         for layer in range(layers):
-            term = dot_nn(left[layer][...].T, right[layer][...])
+            term = dot_tn(left[layer][...], right[layer][...])
             total = term if total is None else total + term
         return total
 
@@ -1071,6 +1075,7 @@
     first.step()
     xy_landed = first.landed
     first.step()
+    down_full = lax.all_gather(tie(down_weight, (xy_landed, second.landed)), AXES, axis=0, tiled=True)
     second.step(xy_landed)
     qkv, vectors = first.finish()
     vectors = vectors.astype(f32)
@@ -1088,17 +1093,13 @@
     flat = tokens.reshape(count, width)
 
     landed = second.landed
-    second.step()
-    third = Chain(exchange.spread([tie(down_weight, landed)]))
-    lower_kept = attend_forward(place, tie(flat, landed), *info, vecs, qkv, 0, 1)
-    third.step(lower_kept[3])
-    lower_kept = attend_forward(place, flat, *info, vecs, qkv, 1, rows_here, lower_kept)
+    lower_kept = attend_forward(place, flat, *info, vecs, qkv, 0, 1)
     second.step(lower_kept[3])
-    third.step(lower_kept[3])
+    lower_kept = attend_forward(place, tie(flat, landed), *info, vecs, qkv, 1, rows_here, lower_kept)
+    second.step(lower_kept[3])
     out_w, up_w = second.finish()
     mixed, lower_low, lower_act, slope = widen(place, lower_kept[3], flat, vecs, up_vec, out_w, up_w)
-    third.step(lower_low)
-    (down_w,) = third.finish()
+    down_w = (down_full, down_full)
     combined, inputs = narrow(place, lower_act, mixed, vecs, down_w)
 
     upper_kept = attend_forward(place, inputs, *info, vecs, qkv)
@@ -1118,24 +1119,20 @@
     up_sum = Chain(exchange.reduce_joined(keep, send, tall, small))
     landed = down_sum.landed
     down_sum.step()
-    part = attend_back(*lower_kept[:3], tie(gctx, (keep, landed)), lower_kept[4], *info, 0, 1)
-    landed = (down_sum.landed, up_sum.landed)
+    lower_grads, more_bias_sums = attend_back(*lower_kept[:3], tie(gctx, (keep, landed)), lower_kept[4], *info)
+    landed = (up_sum.landed, down_sum.landed)
+    up_sum.step()
     down_sum.step()
-    up_sum.step()
-    lower_grads, more_bias_sums = attend_back(
-        *lower_kept[:3], tie(gctx, landed), lower_kept[4], *info, 1, rows_here, part
-    )
-    landed = (down_sum.landed, up_sum.landed)
-    down_sum.step()
-    up_sum.step()
     joint = exchange.joint_grad(
         place, [upper_grads, tie(lower_grads, landed)], [inputs, flat],
         [bias_sums, more_bias_sums], [sums, more_sums], [up_sums, more_up_sums], small, tall,
     )
     qkv_sum = Chain(exchange.reduce_joint(*joint))
-    landed = (down_sum.landed, up_sum.landed)
+    landed = (up_sum.landed, down_sum.landed)
     up_sum.step()
+    down_sum.step()
     tokens_grad = input_back(place, tie(lower_grads, (joint[0], landed)), gm, qkv)
+    up_sum.step(tokens_grad)
     qkv_sum.step(tokens_grad)
     up_out = up_sum.finish()[0]
     joint = qkv_sum.finish()

time: 452 us -> 429 us (0.949)
  between operations: 2.69 us -> 15.7 us
  other arithmetic: 30.8 us -> 20.9 us
  waiting for transfers between devices: 71.8 us -> 63.4 us
  Pallas kernels: 266 us -> 259 us
  starting transfers between devices: 56.1 us -> 50 us
    ppermute x50 -> x42, waiting for transfers between devices: 71.8 us -> 63.4 us  [swap(): return lax.ppermute(value, AXES, [(i, i ^ flip) for i in range(32)])]
    ppermute x50 -> x42, starting transfers between devices: 56.1 us -> 50 us  [swap(): return lax.ppermute(value, AXES, [(i, i ^ flip) for i in range(32)])]
    pallas_call x3 -> x2, Pallas kernels: 51.5 us -> 48.3 us  [attend_back(): pl.pallas_call(attend_back_kernel, grid=(stop - start, width // QUAD), in...]
  transfers between devices with their start and end apart: 50 -> 43, of which waited for: 19 -> 15; matrix products, arithmetic and copies ran while one was open for 9% -> 7% of each run, Pallas kernels for 27% -> 27%
where the time goes in v3:
time: 429 us; the launch traced here: 424 us
  Pallas kernels  259 us (60%)
  waiting for transfers between devices  63.4 us (15%)
  starting transfers between devices  50 us (12%)
  other arithmetic  20.9 us (5%)
  between operations  15.7 us (4%)
  local copies, waits for them, and re-layouts  15.2 us (4%)
    ppermute x42, waiting for transfers between devices, swap(): return lax.ppermute(value, AXES, [(i, i ^ flip) for i in range(32)])  63.4 us
    ppermute x42, starting transfers between devices, swap(): return lax.ppermute(value, AXES, [(i, i ^ flip) for i in range(32)])  50 us
    pallas_call x2, Pallas kernels, attend_back(): pl.pallas_call(attend_back_kernel, grid=(stop - start, width // QUAD), in...  48.3 us
    pallas_call x3, Pallas kernels, attend_forward(): pl.pallas_call(attend_forward_kernel, grid=(stop - start, quads), in_spec...  47.7 us
    pallas_call x1, Pallas kernels, top(): pl.pallas_call(top_kernel, grid=(count // TILE,), in_specs=[SMEM, tile, t...  41.2 us
    pallas_call x1, Pallas kernels, lower(): pl.pallas_call(lower_kernel, grid=(count // TILE,), in_specs=[SMEM, pl.Bl...  29.1 us
    pallas_call x1, Pallas kernels, tall_grad(): pl.pallas_call(partial(tall_grad_kernel, layers), grid_spec=pltpu.Prefetc...  21.6 us
    pallas_call x1, Pallas kernels, widen(): pl.pallas_call(widen_kernel, grid=(count // TILE,), in_specs=[SMEM, tile,...  18.3 us
  transfers between devices with their start and end apart: 43, of which 15 were waited for; matrix products, arithmetic and copies ran while one was open for 7% of the time, Pallas kernels for 27%

profile of v3, /device:TPU:0, one launch (start us, length us, event | category | flops | bytes accessed | tf_op | source)
XLA Modules:
  0.0 424.3 jit_solution(4807138793084542694)
XLA Ops:
  8.8 3.0 collective-permute-start
  16.7 7.7 %collective-permute-done.1 = bf16[80,768]{1,0:T(8,128)(2,1)S(1)} collective-permute-done((bf16[80,768]{1,0:T(8,128)(2,1)}, bf16[80,768]{1,0:T(8,128)(2,1)S(1)}, u32[]{:S(2)}, u32[]{:S(2)}) %collective-permute-start.1) | collective-permute-done | bytes 122912 | tf_op jit(solution)/shard_map/ppermute | solution.py:951
  28.5 3.2 collective-permute-done.6
  42.9 8.5 %collective-permute-done.4 = bf16[120,768]{1,0:T(8,128)(2,1)S(1)} collective-permute-done((bf16[120,768]{1,0:T(8,128)(2,1)S(1)}, bf16[120,768]{1,0:T(8,128)(2,1)S(1)}, u32[]{:S(2)}, u32[]{:S(2)}) %collective-permute-start.4) | collective-permute-done | bytes 184352 | tf_op jit(solution)/shard_map/ppermute | solution.py:951
  61.2 13.3 %attend_forward.3 = (bf16[1024,768]{1,0:T(8,128)(2,1)}, bf16[1024,768]{1,0:T(8,128)(2,1)}, bf16[1024,768]{1,0:T(8,128)(2,1)}, bf16[1024,768]{1,0:T(8,128)(2,1)}, f32[2,3,8,512]{3,2,1,0:T(8,128)}) custom-call(s32[2]{0:T(128)} %pad_add_fusion.core_ref.place_ref, bf16[1024,768]{1,0:T(8,128)(2,1)} %bitcast.293, s32[1024,128]{1,0:T(8,128)} %broadcast_in_dim.65.seg_col, ...), custom_call_target="tpu_custom_call" | custom-call | flops 5033164800 | bytes 7471104 | tf_op jit(solution)/shard_map/attend_forward/pallas_call | solution.py:173
  78.9 12.8 %attend_forward.4 = (bf16[1024,768]{1,0:T(8,128)(2,1)}, bf16[1024,768]{1,0:T(8,128)(2,1)}, bf16[1024,768]{1,0:T(8,128)(2,1)}, bf16[1024,768]{1,0:T(8,128)(2,1)}, f32[2,3,8,512]{3,2,1,0:T(8,128)}) custom-call(s32[2]{0:T(128)} %pad_add_fusion.core_ref.place_ref, ...), custom_call_target="tpu_custom_call", output_to_operand_aliasing={{0}: (8, {}), {1}: (9, {}), {2}: (10, {}), {3}: (11, {}), {... | custom-call | flops 5033164800 | bytes 7471104 | tf_op jit(solution)/shard_map/attend_forward/pallas_call | solution.py:173
  91.7 6.7 %collective-permute-done.15 = bf16[4,2,120,384]{3,2,0,1:T(8,128)(2,1)S(1)} collective-permute-done((bf16[4,2,120,384]{3,2,0,1:T(8,128)(2,1)S(1)}, bf16[4,2,120,384]{3,2,0,1:T(8,128)(2,1)S(1)}, u32[]{:S(2)}, u32[]{:S(2)}) %collective-permute-start.15) | collective-permute-done | bytes 737312 | tf_op jit(solution)/shard_map/ppermute | solution.py:951
  101.4 3.9 collective-permute-done.16.o_sib
  106.0 18.3 %widen.1 = (f32[1024,768]{1,0:T(8,128)}, bf16[1024,768]{1,0:T(8,128)(2,1)}, bf16[1024,3072]{1,0:T(8,128)(2,1)}, bf16[1024,3072]{1,0:T(8,128)(2,1)}) custom-call(s32[2]{0:T(128)} %pad_add_fusion.core_ref.place_ref, bf16[1024,768]{1,0:T(8,128)(2,1)} %get-tuple-element.96.ctx.refs_7_, bf16[1024,768]{1,0:T(8,128)(2,1)} %bitcast.295, f32[8,768]{1,0:T(8,128)} %reshape.340.vecs, ...), custom_call_target="tpu_custom_call" | custom-call | flops 6039797760 | bytes 22020096 | tf_op jit(solution)/shard_map/widen/pallas_call | solution.py:245
  124.3 12.1 %narrow.1 = (f32[1024,768]{1,0:T(8,128)}, bf16[1024,768]{1,0:T(8,128)(2,1)}) custom-call(s32[2]{0:T(128)} %pad_add_fusion.core_ref.place_ref, bf16[1024,3072]{1,0:T(8,128)(2,1)} %get-tuple-element.101.act.refs_3_, f32[1024,768]{1,0:T(8,128)} %get-tuple-element.102.mixed, f32[8,768]{1,0:T(8,128)} %reshape.340.vecs, ...), custom_call_target="tpu_custom_call" | custom-call | flops 4831838208 | bytes 14155776 | tf_op jit(solution)/shard_map/narrow/pallas_call | solution.py:290
  136.5 21.7 %attend_forward.5 = (bf16[1024,768]{1,0:T(8,128)(2,1)}, bf16[1024,768]{1,0:T(8,128)(2,1)}, bf16[1024,768]{1,0:T(8,128)(2,1)}, bf16[1024,768]{1,0:T(8,128)(2,1)}, f32[2,3,8,512]{3,2,1,0:T(8,128)}) custom-call(s32[2]{0:T(128)} %pad_add_fusion.core_ref.place_ref, bf16[1024,768]{1,0:T(8,128)(2,1)} %get-tuple-element.104.x.refs_2_, ...), custom_call_target="tpu_custom_call" | custom-call | flops 10066329600 | bytes 11403264 | tf_op jit(solution)/shard_map/attend_forward/pallas_call | solution.py:173
  158.2 41.2 %top.1 = (bf16[1024,768]{1,0:T(8,128)(2,1)}, bf16[1024,768]{1,0:T(8,128)(2,1)}, bf16[1024,3072]{1,0:T(8,128)(2,1)}, bf16[1024,768]{1,0:T(8,128)(2,1)}, bf16[1024...) custom-call(s32[2]{0:T(128)} %pad_add_fusion.core_ref.place_ref, ...), custom_call_target="tpu_custom_call" | custom-call | flops 21743271936 | bytes 29884416 | tf_op jit(solution)/shard_map/top/pallas_call | solution.py:399
  199.4 24.1 %attend_back.2 = (bf16[3,1024,768]{2,1,0:T(8,128)(2,1)}, f32[2,2,8,768]{3,2,1,0:T(8,128)}) custom-call(bf16[1024,768]{1,0:T(8,128)(2,1)} %get-tuple-element.111.q, bf16[1024,768]{1,0:T(8,128)(2,1)} %get-tuple-element.112.k, bf16[1024,768]{1,0:T(8,128)(2,1)} %get-tuple-element.113.v, bf16[1024,768]{1,0:T(8,128)(2,1)} %get-tuple-element.114.gctx, ...), custom_call_target="tpu_custom_call" | custom-call | flops 16106127360 | bytes 12582912 | tf_op jit(solution)/shard_map/attend_back/pallas_call | solution.py:551
  223.6 29.1 %lower.1 = (bf16[1024,768]{1,0:T(8,128)(2,1)}, bf16[1024,3072]{1,0:T(8,128)(2,1)}, bf16[1024,768]{1,0:T(8,128)(2,1)}, f32[1024,768]{1,0:T(8,128)}, bf16[1024,768...) custom-call(s32[2]{0:T(128)} %pad_add_fusion.core_ref.place_ref, ...), custom_call_target="tpu_custom_call" | custom-call | flops 14495514624 | bytes 36175872 | tf_op jit(solution)/shard_map/lower/pallas_call | solution.py:479
  252.6 15.2 %weight_grad.1 = (bf16[1,2,2,192,1536]{4,3,2,1,0:T(8,128)(2,1)}, bf16[1,2,2,192,1536]{4,3,2,1,0:T(8,128)(2,1)}) custom-call(s32[2]{0:T(128)} %pad_add_fusion.core_ref.place_ref, bf16[1,1024,768]{2,1,0:T(8,128)(2,1)} %bitcast.298, bf16[1,1024,768]{2,1,0:T(8,128)(2,1)} %bitcast.299, bf16[1024,3072]{1,0:T(8,128)(2,1)} %get-tuple-element.124.refs_2_, ...), custom_call_target="tpu_custom_call" | custom-call | flops 9663676416 | bytes 20447232 | tf_op jit(solution)/shard_map/weight_grad/pallas_call | solution.py:648
  268.0 21.6 %tall_grad.1 = (bf16[2,2,8,120,384]{4,3,2,1,0:T(8,128)(2,1)}, bf16[2,2,8,120,384]{4,3,2,1,0:T(8,128)(2,1)}) custom-call(s32[2]{0:T(128)} %pad_add_fusion.core_ref.place_ref, bf16[1024,3072]{1,0:T(8,128)(2,1)} %get-tuple-element.120.refs_0_, bf16[1024,3072]{1,0:T(8,128)(2,1)} %get-tuple-element.126.refs_1_, bf16[1024,768]{1,0:T(8,128)(2,1)} %get-tuple-element.127.refs_2_, ...), custom_call_target="tpu_custom_call" | custom-call | flops 12079595520 | bytes 27918336 | tf_op jit(solution)/shard_map/tall_grad/pallas_call | solution.py:805
  296.0 24.1 %attend_back.3 = (bf16[3,1024,768]{2,1,0:T(8,128)(2,1)}, f32[2,2,8,768]{3,2,1,0:T(8,128)}) custom-call(bf16[1024,768]{1,0:T(8,128)(2,1)} %get-tuple-element.108.q, bf16[1024,768]{1,0:T(8,128)(2,1)} %get-tuple-element.109.k, bf16[1024,768]{1,0:T(8,128)(2,1)} %get-tuple-element.110.v, bf16[1024,768]{1,0:T(8,128)(2,1)} %get-tuple-element.133.gctx, ...), custom_call_target="tpu_custom_call" | custom-call | flops 16106127360 | bytes 12582912 | tf_op jit(solution)/shard_map/attend_back/pallas_call | solution.py:551
  332.0 13.9 %joint_grad.1 = (bf16[2,2,8,80,384]{4,3,2,1,0:T(8,128)(2,1)}, bf16[2,2,8,80,384]{4,3,2,1,0:T(8,128)(2,1)}) custom-call(s32[2]{0:T(128)} %pad_add_fusion.core_ref.place_ref, bf16[3,1024,768]{2,1,0:T(8,128)(2,1)} %get-tuple-element.116.grads.refs_0_, bf16[3,1024,768]{2,1,0:T(8,128)(2,1)} %get-tuple-element.145.refs_1_.grads, ...), custom_call_target="tpu_custom_call" | custom-call | flops 7247757312 | bytes 16121856 | tf_op jit(solution)/shard_map/joint_grad/pallas_call | solution.py:725
  358.0 5.5 %collective-permute-done.40 = bf16[1,24,3072]{2,1,0:T(8,128)(2,1)S(1)} collective-permute-done((bf16[1,24,3072]{2,1,0:T(8,128)(2,1)S(1)}, bf16[1,24,3072]{2,1,0:T(8,128)(2,1)S(1)}, u32[]{:S(2)}, u32[]{:S(2)}) %collective-permute-start.40) | collective-permute-done | bytes 147488 | tf_op jit(solution)/shard_map/ppermute | solution.py:951
  364.3 9.9 %input_back.1 = f32[1024,768]{1,0:T(8,128)} custom-call(s32[2]{0:T(128)} %pad_add_fusion.core_ref.place_ref, bf16[3,1024,768]{2,1,0:T(8,128)(2,1)} %get-tuple-element.145.refs_1_.grads, f32[1024,768]{1,0:T(8,128)} %get-tuple-element.146.gm, bf16[3,2,2,192,384]{4,3,2,1,0:T(8,128)(2,1)} %copy-done, bf16[3,2,2,192,384]{4,3,2,1,0:T(8,128)(2,1)} %collective-permute-done.13.sib.q_sib), custom_call_target="tpu_custom_call" | custom-call | flops 3623878656 | bytes 11010048 | tf_op jit(solution)/shard_map/input_back/pallas_call | solution.py:592
  374.5 3.1 collective-permute-start.36
  385.2 8.8 %collective-permute-done.37 = bf16[1,120,768]{2,1,0:T(8,128)(2,1)S(1)} collective-permute-done((bf16[1,120,768]{2,1,0:T(8,128)(2,1)S(1)}, bf16[1,120,768]{2,1,0:T(8,128)(2,1)S(1)}, u32[]{:S(2)}, u32[]{:S(2)}) %collective-permute-start.37) | collective-permute-done | bytes 184352 | tf_op jit(solution)/shard_map/ppermute | solution.py:951
  398.3 2.9 collective-permute-done.30
  408.7 6.7 %collective-permute-done.32 = bf16[1,80,768]{2,1,0:T(8,128)(2,1)S(1)} collective-permute-done((bf16[1,80,768]{2,1,0:T(8,128)(2,1)S(1)}, bf16[1,80,768]{2,1,0:T(8,128)(2,1)S(1)}, u32[]{:S(2)}, u32[]{:S(2)}) %collective-permute-start.32) | collective-permute-done | bytes 122912 | tf_op jit(solution)/shard_map/ppermute | solution.py:951
  (199 shorter events, 91.0 us)
Async XLA Ops:
  7.2 117.1 %all-gather.2.cloned.1.call-start = ((), (), s32[]{:S(2)}) async-start(), calls=%async_computation | async-start | bytes 4866048 | tf_op jit(solution)/shard_map/all_gather | solution.py:1078
  11.8 12.5 %collective-permute-start.1 = (bf16[80,768]{1,0:T(8,128)(2,1)}, bf16[80,768]{1,0:T(8,128)(2,1)S(1)}, u32[]{:S(2)}, u32[]{:S(2)}) collective-permute-start(bf16[80,768]{1,0:T(8,128)(2,1)} %pack.1), channel_id=1, source_target_pairs={{0,4},{1,5},{2,6},{3,7},{4,0},{5,1},{6,2},{7,3},{8,12},{9,13},{10,... | collective-permute-start | bytes 368648 | tf_op jit(solution)/shard_map/ppermute | solution.py:951
  34.1 17.2 %collective-permute-start.7 = (bf16[2,4,80,384]{3,2,1,0:T(8,128)(2,1)S(1)}, bf16[2,4,80,384]{3,2,1,0:T(8,128)(2,1)S(1)}, u32[]{:S(2)}, u32[]{:S(2)}) collective-permute-start(bf16[2,4,80,384]{3,2,1,0:T(8,128)(2,1)S(1)} %pad_maximum_fusion.9), channel_id=1, source_target_pairs={{0,1},{1,0},{2,3},{3,2},{4,5},{5,4},{6,7},{7,6},{8,9},{9,8},{10,11... | collective-permute-start | bytes 1474568 | tf_op jit(solution)/shard_map/ppermute | solution.py:951
  35.8 15.6 %collective-permute-start.9 = (bf16[4,2,80,384]{3,2,0,1:T(8,128)(2,1)S(1)}, bf16[4,2,80,384]{3,2,0,1:T(8,128)(2,1)S(1)}, u32[]{:S(2)}, u32[]{:S(2)}) collective-permute-start(bf16[4,2,80,384]{3,2,0,1:T(8,128)(2,1)S(1)} %pad_maximum_fusion.10), channel_id=1, source_target_pairs={{0,16},{1,17},{2,18},{3,19},{4,20},{5,21},{6,22},{7,23},{8,24},{9,... | collective-permute-start | bytes 1474568 | tf_op jit(solution)/shard_map/ppermute | solution.py:951
  37.6 13.8 %collective-permute-start.4 = (bf16[120,768]{1,0:T(8,128)(2,1)S(1)}, bf16[120,768]{1,0:T(8,128)(2,1)S(1)}, u32[]{:S(2)}, u32[]{:S(2)}) collective-permute-start(bf16[120,768]{1,0:T(8,128)(2,1)S(1)} %constant_dynamic-update-slice_fusion), channel_id=1, source_target_pairs={{0,4},{1,5},{2,6},{3,7},{4,0},{5,1},{6,2},{7,3},{8,12},{9,13},{10,... | collective-permute-start | bytes 552968 | tf_op jit(solution)/shard_map/ppermute | solution.py:951
  56.3 18.2 %collective-permute-start.10 = (bf16[4,120,384]{2,1,0:T(8,128)(2,1)}, bf16[4,120,384]{2,1,0:T(8,128)(2,1)}, u32[]{:S(2)}, u32[]{:S(2)}) collective-permute-start(bf16[4,120,384]{2,1,0:T(8,128)(2,1)} %get-tuple-element.181), channel_id=1, source_target_pairs={{0,16},{1,17},{2,18},{3,19},{4,20},{5,21},{6,22},{7,23},{8,24},{9,... | collective-permute-start | bytes 1105928 | tf_op jit(solution)/shard_map/ppermute | solution.py:951
  57.8 16.7 %collective-permute-start.11 = (bf16[4,120,384]{2,1,0:T(8,128)(2,1)}, bf16[4,120,384]{2,1,0:T(8,128)(2,1)}, u32[]{:S(2)}, u32[]{:S(2)}) collective-permute-start(bf16[4,120,384]{2,1,0:T(8,128)(2,1)} %get-tuple-element.180), channel_id=1, source_target_pairs={{0,1},{1,0},{2,3},{3,2},{4,5},{5,4},{6,7},{7,6},{8,9},{9,8},{10,11... | collective-permute-start | bytes 1105928 | tf_op jit(solution)/shard_map/ppermute | solution.py:951
  75.8 22.6 %collective-permute-start.15 = (bf16[4,2,120,384]{3,2,0,1:T(8,128)(2,1)S(1)}, bf16[4,2,120,384]{3,2,0,1:T(8,128)(2,1)S(1)}, u32[]{:S(2)}, u32[]{:S(2)}) collective-permute-start(bf16[4,2,120,384]{3,2,0,1:T(8,128)(2,1)S(1)} %pad_maximum_fusion.6), channel_id=1, source_target_pairs={{0,16},{1,17},{2,18},{3,19},{4,20},{5,21},{6,22},{7,23},{8,24},{9,... | collective-permute-start | bytes 2211848 | tf_op jit(solution)/shard_map/ppermute | solution.py:951
  77.4 21.0 %collective-permute-start.14 = (bf16[2,4,120,384]{3,2,1,0:T(8,128)(2,1)}, bf16[2,4,120,384]{3,2,1,0:T(8,128)(2,1)S(1)}, u32[]{:S(2)}, u32[]{:S(2)}) collective-permute-start(bf16[2,4,120,384]{3,2,1,0:T(8,128)(2,1)} %pad_maximum_fusion.5), channel_id=1, source_target_pairs={{0,1},{1,0},{2,3},{3,2},{4,5},{5,4},{6,7},{7,6},{8,9},{9,8},{10,11... | collective-permute-start | bytes 2211848 | tf_op jit(solution)/shard_map/ppermute | solution.py:951
  267.8 22.1 %collective-permute-start.18 = (bf16[1,2,2,192,1536]{4,3,2,1,0:T(8,128)(2,1)}, bf16[1,2,2,192,1536]{4,3,2,1,0:T(8,128)(2,1)}, u32[]{:S(2)}, u32[]{:S(2)}) collective-permute-start(bf16[1,2,2,192,1536]{4,3,2,1,0:T(8,128)(2,1)} %get-tuple-element.132), channel_id=1, source_target_pairs={{0,8},{1,9},{2,10},{3,11},{4,12},{5,13},{6,14},{7,15},{8,0},{9,1},... | collective-permute-start | bytes 7077896 | tf_op jit(solution)/shard_map/ppermute | solution.py:951
  289.6 34.3 %collective-permute-start.19 = (bf16[1,2,2,960,384]{4,3,2,1,0:T(8,128)(2,1)}, bf16[1,2,2,960,384]{4,3,2,1,0:T(8,128)(2,1)}, u32[]{:S(2)}, u32[]{:S(2)}) collective-permute-start(bf16[1,2,2,960,384]{4,3,2,1,0:T(8,128)(2,1)} %bitcast.290), channel_id=1, source_target_pairs={{0,8},{1,9},{2,10},{3,11},{4,12},{5,13},{6,14},{7,15},{8,0},{9,1},... | collective-permute-start | bytes 8847368 | tf_op jit(solution)/shard_map/ppermute | solution.py:951
  292.5 27.7 %collective-permute-start.21 = (bf16[1,2,4,24,1536]{4,3,2,1,0:T(8,128)(2,1)S(1)}, bf16[1,2,4,24,1536]{4,3,2,1,0:T(8,128)(2,1)}, u32[]{:S(2)}, u32[]{:S(2)}) collective-permute-start(bf16[1,2,4,24,1536]{4,3,2,1,0:T(8,128)(2,1)S(1)} %dynamic-slice_bitcast_fusion.1), channel_id=1, source_target_pairs={{0,1},{1,0},{2,3},{3,2},{4,5},{5,4},{6,7},{7,6},{8,9},{9,8},{10,11... | collective-permute-start | bytes 1769480 | tf_op jit(solution)/shard_map/ppermute | solution.py:951
  294.5 28.2 %collective-permute-start.20 = (bf16[1,4,2,24,1536]{4,3,1,2,0:T(8,128)(2,1)S(1)}, bf16[1,4,2,24,1536]{4,3,1,2,0:T(8,128)(2,1)S(1)}, u32[]{:S(2)}, u32[]{:S(2)}) collective-permute-start(bf16[1,4,2,24,1536]{4,3,1,2,0:T(8,128)(2,1)S(1)} %slice_bitcast_fusion.3), channel_id=1, source_target_pairs={{0,16},{1,17},{2,18},{3,19},{4,20},{5,21},{6,22},{7,23},{8,24},{9,... | collective-permute-start | bytes 1769480 | tf_op jit(solution)/shard_map/ppermute | solution.py:951
  322.1 23.8 %collective-permute-start.25 = (bf16[1,4,24,1536]{3,2,1,0:T(8,128)(2,1)}, bf16[1,4,24,1536]{3,2,1,0:T(8,128)(2,1)}, u32[]{:S(2)}, u32[]{:S(2)}) collective-permute-start(bf16[1,4,24,1536]{3,2,1,0:T(8,128)(2,1)} %slice_bitcast_fusion.10), channel_id=1, source_target_pairs={{0,16},{1,17},{2,18},{3,19},{4,20},{5,21},{6,22},{7,23},{8,24},{9,... | collective-permute-start | bytes 884744 | tf_op jit(solution)/shard_map/ppermute | solution.py:951
  323.6 23.3 %collective-permute-start.24 = (bf16[1,4,24,1536]{3,2,1,0:T(8,128)(2,1)}, bf16[1,4,24,1536]{3,2,1,0:T(8,128)(2,1)}, u32[]{:S(2)}, u32[]{:S(2)}) collective-permute-start(bf16[1,4,24,1536]{3,2,1,0:T(8,128)(2,1)} %dynamic-slice_bitcast_fusion.4), channel_id=1, source_target_pairs={{0,1},{1,0},{2,3},{3,2},{4,5},{5,4},{6,7},{7,6},{8,9},{9,8},{10,11... | collective-permute-start | bytes 884744 | tf_op jit(solution)/shard_map/ppermute | solution.py:951
  327.7 23.4 %collective-permute-start.23 = (bf16[1,2,4,120,384]{4,3,2,1,0:T(8,128)(2,1)}, bf16[1,2,4,120,384]{4,3,2,1,0:T(8,128)(2,1)}, u32[]{:S(2)}, u32[]{:S(2)}) collective-permute-start(bf16[1,2,4,120,384]{4,3,2,1,0:T(8,128)(2,1)} %dynamic-slice_bitcast_fusion), channel_id=1, source_target_pairs={{0,1},{1,0},{2,3},{3,2},{4,5},{5,4},{6,7},{7,6},{8,9},{9,8},{10,11... | collective-permute-start | bytes 2211848 | tf_op jit(solution)/shard_map/ppermute | solution.py:951
  330.6 23.3 %collective-permute-start.22 = (bf16[1,4,2,120,384]{4,3,1,2,0:T(8,128)(2,1)}, bf16[1,4,2,120,384]{4,3,1,2,0:T(8,128)(2,1)}, u32[]{:S(2)}, u32[]{:S(2)}) collective-permute-start(bf16[1,4,2,120,384]{4,3,1,2,0:T(8,128)(2,1)} %slice_bitcast_fusion.1), channel_id=1, source_target_pairs={{0,16},{1,17},{2,18},{3,19},{4,20},{5,21},{6,22},{7,23},{8,24},{9,... | collective-permute-start | bytes 2211848 | tf_op jit(solution)/shard_map/ppermute | solution.py:951
  345.9 34.6 %collective-permute-start.26 = (bf16[1,2,2,640,384]{4,3,2,1,0:T(8,128)(2,1)}, bf16[1,2,2,640,384]{4,3,2,1,0:T(8,128)(2,1)}, u32[]{:S(2)}, u32[]{:S(2)}) collective-permute-start(bf16[1,2,2,640,384]{4,3,2,1,0:T(8,128)(2,1)} %bitcast.291), channel_id=1, source_target_pairs={{0,8},{1,9},{2,10},{3,11},{4,12},{5,13},{6,14},{7,15},{8,0},{9,1},... | collective-permute-start | bytes 5898248 | tf_op jit(solution)/shard_map/ppermute | solution.py:951
  349.5 13.9 %collective-permute-start.40 = (bf16[1,24,3072]{2,1,0:T(8,128)(2,1)S(1)}, bf16[1,24,3072]{2,1,0:T(8,128)(2,1)S(1)}, u32[]{:S(2)}, u32[]{:S(2)}) collective-permute-start(bf16[1,24,3072]{2,1,0:T(8,128)(2,1)S(1)} %get-tuple-element.191), channel_id=1, source_target_pairs={{0,4},{1,5},{2,6},{3,7},{4,0},{5,1},{6,2},{7,3},{8,12},{9,13},{10,... | collective-permute-start | bytes 442376 | tf_op jit(solution)/shard_map/ppermute | solution.py:951
  353.9 20.4 %collective-permute-start.35 = (bf16[1,4,120,384]{3,2,1,0:T(8,128)(2,1)S(1)}, bf16[1,4,120,384]{3,2,1,0:T(8,128)(2,1)S(1)}, u32[]{:S(2)}, u32[]{:S(2)}) collective-permute-start(bf16[1,4,120,384]{3,2,1,0:T(8,128)(2,1)S(1)} %slice_bitcast_fusion.7), channel_id=1, source_target_pairs={{0,16},{1,17},{2,18},{3,19},{4,20},{5,21},{6,22},{7,23},{8,24},{9,... | collective-permute-start | bytes 1105928 | tf_op jit(solution)/shard_map/ppermute | solution.py:951
  357.3 16.9 %collective-permute-start.34 = (bf16[1,4,120,384]{3,2,1,0:T(8,128)(2,1)S(1)}, bf16[1,4,120,384]{3,2,1,0:T(8,128)(2,1)S(1)}, u32[]{:S(2)}, u32[]{:S(2)}) collective-permute-start(bf16[1,4,120,384]{3,2,1,0:T(8,128)(2,1)S(1)} %dynamic-slice_bitcast_fusion.3), channel_id=1, source_target_pairs={{0,1},{1,0},{2,3},{3,2},{4,5},{5,4},{6,7},{7,6},{8,9},{9,8},{10,11... | collective-permute-start | bytes 1105928 | tf_op jit(solution)/shard_map/ppermute | solution.py:951
  377.6 16.4 %collective-permute-start.37 = (bf16[1,120,768]{2,1,0:T(8,128)(2,1)S(1)}, bf16[1,120,768]{2,1,0:T(8,128)(2,1)S(1)}, u32[]{:S(2)}, u32[]{:S(2)}) collective-permute-start(bf16[1,120,768]{2,1,0:T(8,128)(2,1)S(1)} %get-tuple-element.176), channel_id=1, source_target_pairs={{0,4},{1,5},{2,6},{3,7},{4,0},{5,1},{6,2},{7,3},{8,12},{9,13},{10,... | collective-permute-start | bytes 552968 | tf_op jit(solution)/shard_map/ppermute | solution.py:951
  379.1 14.9 %collective-permute-start.38 = (bf16[1,120,768]{2,1,0:T(8,128)(2,1)S(1)}, bf16[1,120,768]{2,1,0:T(8,128)(2,1)S(1)}, u32[]{:S(2)}, u32[]{:S(2)}) collective-permute-start(bf16[1,120,768]{2,1,0:T(8,128)(2,1)S(1)} %get-tuple-element.177), channel_id=1, source_target_pairs={{0,6},{1,7},{2,4},{3,5},{4,2},{5,3},{6,0},{7,1},{8,14},{9,15},{10,... | collective-permute-start | bytes 552968 | tf_op jit(solution)/shard_map/ppermute | solution.py:951
  383.7 12.9 %collective-permute-start.27 = (bf16[1,4,2,80,384]{4,3,1,2,0:T(8,128)(2,1)S(1)}, bf16[1,4,2,80,384]{4,3,1,2,0:T(8,128)(2,1)S(1)}, u32[]{:S(2)}, u32[]{:S(2)}) collective-permute-start(bf16[1,4,2,80,384]{4,3,1,2,0:T(8,128)(2,1)S(1)} %slice_bitcast_fusion.4), channel_id=1, source_target_pairs={{0,16},{1,17},{2,18},{3,19},{4,20},{5,21},{6,22},{7,23},{8,24},{9,... | collective-permute-start | bytes 1474568 | tf_op jit(solution)/shard_map/ppermute | solution.py:951
  (29 other events, 206.2 us)
Sparse Core Ops, SparseCore 0:
  51.5 67.3 all-gather.1

commit v4 on v3

--- a/solution.py
+++ b/solution.py
@@ -13,6 +13,7 @@
 QUAD = 4 * HEAD
 TILE = 256
 SUB = 256
+TOP_TILE = 512
 norm_eps = 1e-06
 masked_score = -1000000000.0
 VMEM = 60 * 1024 * 1024
@@ -108,12 +109,12 @@
 
 
 def attend_forward_kernel(
-    core_ref, x, seg_col, alive_col, seg_row, vecs, own, sib, *rest
+    start, core_ref, x, seg_col, alive_col, seg_row, vecs, own, sib, *rest
 ):
     q_out, k_out, v_out, ctx_out, lse_out, weights, mask, sems = rest[-8:]
-    row, quad = pl.program_id(0), pl.program_id(1)
+    quad = (pl.program_id(0) + start) % (weights.shape[1] // QUAD)
     core = core_ref[0]
-    first = (row == 0) & (quad == 0)
+    first = pl.program_id(0) == 0
     copies = [
         piece_copies(core, (own, sib), weights.at[w], sems.at[w], w)
         for w in range(3)
@@ -124,7 +125,7 @@
         for group in copies:
             start_all(group)
 
-    @pl.when(quad == 0)
+    @pl.when(first | (quad == 0))
     def _():
         mask_into(mask, seg_col, alive_col, seg_row)
 
@@ -163,19 +164,26 @@
 def attend_forward(core, x, seg_col, alive_col, seg_row, vecs, qkv, start=0, stop=None, before=()):
     count, width = x.shape
     rows, _, length = seg_row.shape
-    stop = rows if stop is None else stop
     quads = width // QUAD
-    full = pl.BlockSpec((length, width), lambda r, j: (r + start, 0))
-    col = pl.BlockSpec((length, 128), lambda r, j: (r + start, 0))
-    block = pl.BlockSpec((length, QUAD), lambda r, j: (r + start, j))
+    stop = rows * quads if stop is None else stop
+
+    def row(s):
+        return (s + start) // quads
+
+    def quad(s):
+        return (s + start) % quads
+
+    full = pl.BlockSpec((length, width), lambda s: (row(s), 0))
+    col = pl.BlockSpec((length, 128), lambda s: (row(s), 0))
+    block = pl.BlockSpec((length, QUAD), lambda s: (row(s), quad(s)))
     low = jax.ShapeDtypeStruct((count, width), bf16)
-    share = (stop - start) / rows
+    share = (stop - start) / (rows * quads)
     return pl.pallas_call(
-        attend_forward_kernel,
-        grid=(stop - start, quads),
-        in_specs=[SMEM, full, col, col, pl.BlockSpec((1, 1, length), lambda r, j: (r + start, 0, 0)),
-                  pl.BlockSpec((8, QUAD), lambda r, j: (0, j)), ANY, ANY] + [ANY] * len(before),
-        out_specs=[block] * 4 + [pl.BlockSpec((1, 1, 8, length), lambda r, j: (r + start, j, 0, 0))],
+        partial(attend_forward_kernel, start),
+        grid=(stop - start,),
+        in_specs=[SMEM, full, col, col, pl.BlockSpec((1, 1, length), lambda s: (row(s), 0, 0)),
+                  pl.BlockSpec((8, QUAD), lambda s: (0, quad(s))), ANY, ANY] + [ANY] * len(before),
+        out_specs=[block] * 4 + [pl.BlockSpec((1, 1, 8, length), lambda s: (row(s), quad(s), 0, 0))],
         out_shape=[low] * 4 + [jax.ShapeDtypeStruct((rows, quads, 8, length), f32)],
         scratch_shapes=[
             pltpu.VMEM((3, width, width), bf16),
@@ -310,6 +318,16 @@
         out[index] += partial_sum(value)
 
 
+def in_turn(parts, first, landed):
+    live = parts
+    turn = 0
+    while live:
+        live = [part for part in live if next(part, live) is not live]
+        if turn == 0:
+            pl.when(first)(landed)
+        turn += 1
+
+
 def top_kernel(
     core_ref, ctx, resid, cot, alive_col, vecs, up_bias,
     o_own, o_sib, u_own, u_sib, d_own, d_sib,
@@ -333,26 +351,21 @@
 
     width = ctx.shape[1]
     chunks = [slice(c * width, (c + 1) * width) for c in range(up_weight.shape[0] // width)]
-    for part in range(ctx.shape[0] // SUB):
-        rows = slice(part * SUB, (part + 1) * SUB)
+    def work(rows):
         hidden = normalize(resid[rows, :])[0] * vecs[G2 : G2 + 1, :] + vecs[S2 : S2 + 1, :]
         mixed = hidden + dot_nt(ctx[rows, :], out_weight[...]) + vecs[OB : OB + 1, :]
         first_unit, first_rstd = normalize(mixed)
         combined = first_unit * vecs[G1 : G1 + 1, :] + vecs[S1 : S1 + 1, :]
         low = combined.astype(bf16)
         low_out[rows, :] = low
-
-        @pl.when(first)
-        def _():
-            wait_all(up_copies)
-            wait_all(down_copies)
-
+        yield
         for cols in chunks:
             act, slope = gelu_both(dot_nt(low, up_weight[cols, :]) + up_bias[0:1, cols])
             act = act.astype(bf16)
             act_out[rows, cols] = act
             slopes[rows, cols] = slope.astype(bf16)
             combined = combined + dot_nt(act, down_weight[:, cols])
+            yield
         unit, rstd = normalize(combined + vecs[DB : DB + 1, :])
         gain = vecs[G2 : G2 + 1, :]
         alive = alive_col[rows, 0:1].astype(f32)
@@ -361,10 +374,17 @@
         sums[0] += partial_sum(grad * unit)
         sums[1] += partial_sum(grad)
         grad = normalize_back(grad, gain, unit, rstd)
-        feed_back_rows(
+        yield
+        yield from feed_back_rows(
             rows, chunks, grad, slopes, first_unit, first_rstd, vecs, down_weight, up_weight, out_weight,
             gb_out, gu_out, ga_out, gm_out, gctx_out, sums, up_sums,
         )
+
+    def landed():
+        wait_all(up_copies)
+        wait_all(down_copies)
+
+    in_turn([work(slice(p * SUB, (p + 1) * SUB)) for p in range(ctx.shape[0] // SUB)], first, landed)
 
 
 def feed_back_rows(
@@ -379,6 +399,7 @@
         gu_out[rows, cols] = grad_up
         up_sums[:, cols] += partial_sum(grad_up.astype(f32))
         grad = grad + dot_nn(grad_up, up_weight[cols, :])
+        yield
     sums[3] += partial_sum(grad * unit)
     sums[4] += partial_sum(grad)
     grad = normalize_back(grad, vecs[G1 : G1 + 1, :], unit, rstd)
@@ -386,20 +407,21 @@
     attn = grad.astype(bf16)
     ga_out[rows, :] = attn
     sums[5] += partial_sum(attn.astype(f32))
+    yield
     gctx_out[rows, :] = dot_nn(attn, out_weight[...]).astype(bf16)
 
 
 def top(core, ctx, resid, cot, alive_col, vecs, up_bias, out_weight, up_weight, down_weight):
     count, width = ctx.shape
     wide = up_bias.shape[1]
-    tile = pl.BlockSpec((TILE, width), lambda i: (i, 0))
-    broad = pl.BlockSpec((TILE, wide), lambda i: (i, 0))
+    tile = pl.BlockSpec((TOP_TILE, width), lambda i: (i, 0))
+    broad = pl.BlockSpec((TOP_TILE, wide), lambda i: (i, 0))
     low = jax.ShapeDtypeStruct((count, width), bf16)
     low_wide = jax.ShapeDtypeStruct((count, wide), bf16)
     return pl.pallas_call(
         top_kernel,
-        grid=(count // TILE,),
-        in_specs=[SMEM, tile, tile, tile, pl.BlockSpec((TILE, 128), lambda i: (i, 0)), whole((8, width)),
+        grid=(count // TOP_TILE,),
+        in_specs=[SMEM, tile, tile, tile, pl.BlockSpec((TOP_TILE, 128), lambda i: (i, 0)), whole((8, width)),
                   whole((8, wide))] + [ANY] * 6,
         out_specs=[tile, tile, broad, tile, broad, tile, tile, tile, whole((6, 8, width)), whole((8, wide))],
         out_shape=[low, low, low_wide, low, low_wide, low, jax.ShapeDtypeStruct((count, width), f32), low,
@@ -408,7 +430,7 @@
             pltpu.VMEM((width, width), bf16),
             pltpu.VMEM((wide, width), bf16),
             pltpu.VMEM((width, wide), bf16),
-            pltpu.VMEM((TILE, wide), bf16),
+            pltpu.VMEM((TOP_TILE, wide), bf16),
             pltpu.SemaphoreType.DMA((3, 8)),
         ],
         compiler_params=params(),
@@ -447,8 +469,7 @@
 
     width = gm.shape[1]
     chunks = [slice(c * width, (c + 1) * width) for c in range(up_weight.shape[0] // width)]
-    for part in range(gm.shape[0] // SUB):
-        rows = slice(part * SUB, (part + 1) * SUB)
+    def work(rows):
         grad = gm[rows, :]
         for w in range(3):
             grad = grad + dot_nn(grads[w, rows, :], weights[w])
@@ -457,17 +478,18 @@
         sums[1] += partial_sum(grad)
         grad = normalize_back(grad, vecs[G2 : G2 + 1, :], unit, rstd)
         first_unit, first_rstd = normalize(mixed[rows, :])
-
-        @pl.when(first)
-        def _():
-            wait_all(down_copies)
-            wait_all(up_copies)
-            wait_all(out_copies)
-
-        feed_back_rows(
+        yield
+        yield from feed_back_rows(
             rows, chunks, grad, slope, first_unit, first_rstd, vecs, down_weight, up_weight, out_weight,
             gb_out, gu_out, ga_out, gm_out, gctx_out, sums, up_sums,
         )
+
+    def landed():
+        wait_all(down_copies)
+        wait_all(up_copies)
+        wait_all(out_copies)
+
+    in_turn([work(slice(p * SUB, (p + 1) * SUB)) for p in range(gm.shape[0] // SUB)], first, landed)
 
 
 def lower(core, grads, gm, combined, slope, mixed, vecs, down_weight, up_weight, out_weight, qkv):
@@ -634,7 +656,7 @@
     layers = len(grads)
     count_w, span, n = grads[0].shape
     depth = inputs[0].shape[1]
-    chunk = min(depth, n)
+    chunk = depth if depth <= n else depth // 6
     chunks = depth // chunk
     halves = 2 if chunks == 1 else 1
     wide = chunk // halves
@@ -883,6 +905,7 @@
 class Plain:
     def __init__(self, mesh):
         self.devices = math.prod(mesh.shape.values())
+        self.sent = None
 
     def place(self):
         return jnp.zeros((2,), jnp.int32)
@@ -936,7 +959,7 @@
 
 class Grid:
     def __init__(self, mesh):
-        pass
+        self.sent = None
 
     def where(self):
         dp, fsdp = lax.axis_index("dp"), lax.axis_index("fsdp")
@@ -1004,10 +1027,12 @@
         got = tie(got, (yield got))
         total = add(keep, got).reshape(count, 2, 2, 4, 2, mine, half)
         left, right = total[:, 0], total[:, 1]
-        got = self.swap(left[:, 1], x=1), self.swap(pick(right, 1 - y, 3), y=1)
+        self.sent = left[:, 1], pick(right, 1 - y, 3)
+        got = self.swap(self.sent[0], x=1), self.swap(self.sent[1], y=1)
         got = tie(got, (yield got))
         left, right = add(left[:, 0], got[0]), add(pick(right, y, 3), got[1])
-        got = self.swap(pick(left, 1 - y, 2), y=1), self.swap(right[:, 1], x=1)
+        self.sent = pick(left, 1 - y, 2), right[:, 1]
+        got = self.swap(self.sent[0], y=1), self.swap(self.sent[1], x=1)
         got = tie(got, (yield got))
         left, right = add(pick(left, y, 2), got[0]), add(right[:, 0], got[1])
         both = jnp.concatenate([left, right], axis=-1)
@@ -1093,9 +1118,9 @@
     flat = tokens.reshape(count, width)
 
     landed = second.landed
-    lower_kept = attend_forward(place, flat, *info, vecs, qkv, 0, 1)
+    lower_kept = attend_forward(place, flat, *info, vecs, qkv, 0, 2)
     second.step(lower_kept[3])
-    lower_kept = attend_forward(place, tie(flat, landed), *info, vecs, qkv, 1, rows_here, lower_kept)
+    lower_kept = attend_forward(place, tie(flat, landed), *info, vecs, qkv, 2, None, lower_kept)
     second.step(lower_kept[3])
     out_w, up_w = second.finish()
     mixed, lower_low, lower_act, slope = widen(place, lower_kept[3], flat, vecs, up_vec, out_w, up_w)
@@ -1130,10 +1155,12 @@
     qkv_sum = Chain(exchange.reduce_joint(*joint))
     landed = (up_sum.landed, down_sum.landed)
     up_sum.step()
+    ready = exchange.sent
     down_sum.step()
-    tokens_grad = input_back(place, tie(lower_grads, (joint[0], landed)), gm, qkv)
-    up_sum.step(tokens_grad)
+    tokens_grad = input_back(place, tie(lower_grads, (joint[0], landed, ready) if ready is not None else joint[0]), gm, qkv)
     qkv_sum.step(tokens_grad)
+    up_sum.step(tokens_grad if exchange.sent is None else (tokens_grad, exchange.sent))
+    down_grad = down_sum.finish(tokens_grad)[0]
     up_out = up_sum.finish()[0]
     joint = qkv_sum.finish()
     query_grad, key_grad, value_grad = (joint[i * small : (i + 1) * small] for i in range(3))
@@ -1153,7 +1180,7 @@
         piece[S1],
         up_out[:tall],
         lines[0, 128 : 128 + tall],
-        down_sum.finish()[0],
+        down_grad,
         piece[DB],
         piece[G2],
         piece[S2],

time: 429 us -> 427 us (level)
  transfers between devices with their start and end apart: 43 -> 43, of which waited for: 15 -> 17; matrix products, arithmetic and copies ran while one was open for 7% -> 8% of each run, Pallas kernels for 27% -> 27%
where the time goes in v4:
time: 427 us; the launch traced here: 422 us
  Pallas kernels  258 us (60%)
  waiting for transfers between devices  60.9 us (14%)
  starting transfers between devices  47 us (11%)
  other arithmetic  24.3 us (6%)
  local copies, waits for them, and re-layouts  16.1 us (4%)
  between operations  15.7 us (4%)
    ppermute x42, waiting for transfers between devices, swap(): return lax.ppermute(value, AXES, [(i, i ^ flip) for i in range(32)])  60.8 us
    pallas_call x2, Pallas kernels, attend_back(): pl.pallas_call(attend_back_kernel, grid=(stop - start, width // QUAD), in...  48.2 us
    pallas_call x3, Pallas kernels, attend_forward(): pl.pallas_call(partial(attend_forward_kernel, start), grid=(stop - start,...  48.1 us
    ppermute x42, starting transfers between devices, swap(): return lax.ppermute(value, AXES, [(i, i ^ flip) for i in range(32)])  47 us
    pallas_call x1, Pallas kernels, top(): pl.pallas_call(top_kernel, grid=(count // TOP_TILE,), in_specs=[SMEM, til...  40 us
    pallas_call x1, Pallas kernels, lower(): pl.pallas_call(lower_kernel, grid=(count // TILE,), in_specs=[SMEM, pl.Bl...  29 us
    pallas_call x1, Pallas kernels, tall_grad(): pl.pallas_call(partial(tall_grad_kernel, layers), grid_spec=pltpu.Prefetc...  21.5 us
    pallas_call x1, Pallas kernels, widen(): pl.pallas_call(widen_kernel, grid=(count // TILE,), in_specs=[SMEM, tile,...  18.4 us
  transfers between devices with their start and end apart: 43, of which 17 were waited for; matrix products, arithmetic and copies ran while one was open for 8% of the time, Pallas kernels for 27%

profile of v4, /device:TPU:0, one launch (start us, length us, event | category | flops | bytes accessed | tf_op | source)
XLA Modules:
  0.0 422.4 jit_solution(17054396607319657661)
XLA Ops:
  8.8 3.0 collective-permute-start
  16.7 7.7 %collective-permute-done.1 = bf16[80,768]{1,0:T(8,128)(2,1)S(1)} collective-permute-done((bf16[80,768]{1,0:T(8,128)(2,1)}, bf16[80,768]{1,0:T(8,128)(2,1)S(1)}, u32[]{:S(2)}, u32[]{:S(2)}) %collective-permute-start.1) | collective-permute-done | bytes 122912 | tf_op jit(solution)/shard_map/ppermute | solution.py:974
  28.5 3.2 collective-permute-done.6
  42.9 8.5 %collective-permute-done.4 = bf16[120,768]{1,0:T(8,128)(2,1)S(1)} collective-permute-done((bf16[120,768]{1,0:T(8,128)(2,1)S(1)}, bf16[120,768]{1,0:T(8,128)(2,1)S(1)}, u32[]{:S(2)}, u32[]{:S(2)}) %collective-permute-start.4) | collective-permute-done | bytes 184352 | tf_op jit(solution)/shard_map/ppermute | solution.py:974
  61.2 10.1 %attend_forward.3 = (bf16[1024,768]{1,0:T(8,128)(2,1)}, bf16[1024,768]{1,0:T(8,128)(2,1)}, bf16[1024,768]{1,0:T(8,128)(2,1)}, bf16[1024,768]{1,0:T(8,128)(2,1)}, f32[2,3,8,512]{3,2,1,0:T(8,128)}) custom-call(s32[2]{0:T(128)} %pad_add_fusion.core_ref.place_ref, bf16[1024,768]{1,0:T(8,128)(2,1)} %bitcast.293, s32[1024,128]{1,0:T(8,128)} %broadcast_in_dim.65.seg_col, ...), custom_call_target="tpu_custom_call" | custom-call | flops 3355443200 | bytes 6160384 | tf_op jit(solution)/shard_map/attend_forward/pallas_call | solution.py:181
  75.8 16.1 %attend_forward.4 = (bf16[1024,768]{1,0:T(8,128)(2,1)}, bf16[1024,768]{1,0:T(8,128)(2,1)}, bf16[1024,768]{1,0:T(8,128)(2,1)}, bf16[1024,768]{1,0:T(8,128)(2,1)}, f32[2,3,8,512]{3,2,1,0:T(8,128)}) custom-call(s32[2]{0:T(128)} %pad_add_fusion.core_ref.place_ref, ...), custom_call_target="tpu_custom_call", output_to_operand_aliasing={{0}: (8, {}), {1}: (9, {}), {2}: (10, {}), {3}: (11, {}), {... | custom-call | flops 6710886400 | bytes 8781824 | tf_op jit(solution)/shard_map/attend_forward/pallas_call | solution.py:181
  91.9 3.3 collective-permute-done.15
  98.2 4.7 %collective-permute-done.16.o_sib = bf16[2,2,192,384]{3,2,1,0:T(8,128)(2,1)} collective-permute-done((bf16[2,2,192,384]{3,2,1,0:T(8,128)(2,1)S(1)}, bf16[2,2,192,384]{3,2,1,0:T(8,128)(2,1)}, u32[]{:S(2)}, u32[]{:S(2)}) %collective-permute-start.16) | collective-permute-done | bytes 589856 | tf_op jit(solution)/shard_map/ppermute | solution.py:974
  103.5 18.4 %widen.1 = (f32[1024,768]{1,0:T(8,128)}, bf16[1024,768]{1,0:T(8,128)(2,1)}, bf16[1024,3072]{1,0:T(8,128)(2,1)}, bf16[1024,3072]{1,0:T(8,128)(2,1)}) custom-call(s32[2]{0:T(128)} %pad_add_fusion.core_ref.place_ref, bf16[1024,768]{1,0:T(8,128)(2,1)} %get-tuple-element.99.ctx.refs_7_, bf16[1024,768]{1,0:T(8,128)(2,1)} %bitcast.295, f32[8,768]{1,0:T(8,128)} %reshape.340.vecs, ...), custom_call_target="tpu_custom_call" | custom-call | flops 6039797760 | bytes 22020096 | tf_op jit(solution)/shard_map/widen/pallas_call | solution.py:253
  121.9 12.4 %narrow.1 = (f32[1024,768]{1,0:T(8,128)}, bf16[1024,768]{1,0:T(8,128)(2,1)}) custom-call(s32[2]{0:T(128)} %pad_add_fusion.core_ref.place_ref, bf16[1024,3072]{1,0:T(8,128)(2,1)} %get-tuple-element.104.act.refs_3_, f32[1024,768]{1,0:T(8,128)} %get-tuple-element.105.mixed, f32[8,768]{1,0:T(8,128)} %reshape.340.vecs, ...), custom_call_target="tpu_custom_call" | custom-call | flops 4831838208 | bytes 14155776 | tf_op jit(solution)/shard_map/narrow/pallas_call | solution.py:298
  134.3 21.8 %attend_forward.5 = (bf16[1024,768]{1,0:T(8,128)(2,1)}, bf16[1024,768]{1,0:T(8,128)(2,1)}, bf16[1024,768]{1,0:T(8,128)(2,1)}, bf16[1024,768]{1,0:T(8,128)(2,1)}, f32[2,3,8,512]{3,2,1,0:T(8,128)}) custom-call(s32[2]{0:T(128)} %pad_add_fusion.core_ref.place_ref, bf16[1024,768]{1,0:T(8,128)(2,1)} %get-tuple-element.107.x.refs_2_, ...), custom_call_target="tpu_custom_call" | custom-call | flops 10066329600 | bytes 11403264 | tf_op jit(solution)/shard_map/attend_forward/pallas_call | solution.py:181
  156.2 40.0 %top.1 = (bf16[1024,768]{1,0:T(8,128)(2,1)}, bf16[1024,768]{1,0:T(8,128)(2,1)}, bf16[1024,3072]{1,0:T(8,128)(2,1)}, bf16[1024,768]{1,0:T(8,128)(2,1)}, bf16[1024...) custom-call(s32[2]{0:T(128)} %pad_add_fusion.core_ref.place_ref, ...), custom_call_target="tpu_custom_call" | custom-call | flops 21743271936 | bytes 29884416 | tf_op jit(solution)/shard_map/top/pallas_call | solution.py:421
  196.2 24.1 %attend_back.2 = (bf16[3,1024,768]{2,1,0:T(8,128)(2,1)}, f32[2,2,8,768]{3,2,1,0:T(8,128)}) custom-call(bf16[1024,768]{1,0:T(8,128)(2,1)} %get-tuple-element.114.q, bf16[1024,768]{1,0:T(8,128)(2,1)} %get-tuple-element.115.k, bf16[1024,768]{1,0:T(8,128)(2,1)} %get-tuple-element.116.v, bf16[1024,768]{1,0:T(8,128)(2,1)} %get-tuple-element.117.gctx, ...), custom_call_target="tpu_custom_call" | custom-call | flops 16106127360 | bytes 12582912 | tf_op jit(solution)/shard_map/attend_back/pallas_call | solution.py:573
  220.3 29.0 %lower.1 = (bf16[1024,768]{1,0:T(8,128)(2,1)}, bf16[1024,3072]{1,0:T(8,128)(2,1)}, bf16[1024,768]{1,0:T(8,128)(2,1)}, f32[1024,768]{1,0:T(8,128)}, bf16[1024,768...) custom-call(s32[2]{0:T(128)} %pad_add_fusion.core_ref.place_ref, ...), custom_call_target="tpu_custom_call" | custom-call | flops 14495514624 | bytes 36175872 | tf_op jit(solution)/shard_map/lower/pallas_call | solution.py:501
  249.3 15.3 %weight_grad.1 = (bf16[1,2,2,192,1536]{4,3,2,1,0:T(8,128)(2,1)}, bf16[1,2,2,192,1536]{4,3,2,1,0:T(8,128)(2,1)}) custom-call(s32[2]{0:T(128)} %pad_add_fusion.core_ref.place_ref, bf16[1,1024,768]{2,1,0:T(8,128)(2,1)} %bitcast.298, bf16[1,1024,768]{2,1,0:T(8,128)(2,1)} %bitcast.299, bf16[1024,3072]{1,0:T(8,128)(2,1)} %get-tuple-element.127.refs_2_, ...), custom_call_target="tpu_custom_call" | custom-call | flops 9663676416 | bytes 20447232 | tf_op jit(solution)/shard_map/weight_grad/pallas_call | solution.py:670
  264.8 21.5 %tall_grad.1 = (bf16[2,2,8,120,384]{4,3,2,1,0:T(8,128)(2,1)}, bf16[2,2,8,120,384]{4,3,2,1,0:T(8,128)(2,1)}) custom-call(s32[2]{0:T(128)} %pad_add_fusion.core_ref.place_ref, bf16[1024,3072]{1,0:T(8,128)(2,1)} %get-tuple-element.123.refs_0_, bf16[1024,3072]{1,0:T(8,128)(2,1)} %get-tuple-element.129.refs_1_, bf16[1024,768]{1,0:T(8,128)(2,1)} %get-tuple-element.130.refs_2_, ...), custom_call_target="tpu_custom_call" | custom-call | flops 12079595520 | bytes 27918336 | tf_op jit(solution)/shard_map/tall_grad/pallas_call | solution.py:827
  291.8 24.1 %attend_back.3 = (bf16[3,1024,768]{2,1,0:T(8,128)(2,1)}, f32[2,2,8,768]{3,2,1,0:T(8,128)}) custom-call(bf16[1024,768]{1,0:T(8,128)(2,1)} %get-tuple-element.111.q, bf16[1024,768]{1,0:T(8,128)(2,1)} %get-tuple-element.112.k, bf16[1024,768]{1,0:T(8,128)(2,1)} %get-tuple-element.113.v, bf16[1024,768]{1,0:T(8,128)(2,1)} %get-tuple-element.136.gctx, ...), custom_call_target="tpu_custom_call" | custom-call | flops 16106127360 | bytes 12582912 | tf_op jit(solution)/shard_map/attend_back/pallas_call | solution.py:573
  327.7 14.0 %joint_grad.1 = (bf16[2,2,8,80,384]{4,3,2,1,0:T(8,128)(2,1)}, bf16[2,2,8,80,384]{4,3,2,1,0:T(8,128)(2,1)}) custom-call(s32[2]{0:T(128)} %pad_add_fusion.core_ref.place_ref, bf16[3,1024,768]{2,1,0:T(8,128)(2,1)} %get-tuple-element.119.grads.refs_0_, bf16[3,1024,768]{2,1,0:T(8,128)(2,1)} %get-tuple-element.148.refs_1_.grads, ...), custom_call_target="tpu_custom_call" | custom-call | flops 7247757312 | bytes 16121856 | tf_op jit(solution)/shard_map/joint_grad/pallas_call | solution.py:747
  355.9 10.0 %input_back.1 = f32[1024,768]{1,0:T(8,128)} custom-call(s32[2]{0:T(128)} %pad_add_fusion.core_ref.place_ref, bf16[3,1024,768]{2,1,0:T(8,128)(2,1)} %get-tuple-element.148.refs_1_.grads, f32[1024,768]{1,0:T(8,128)} %get-tuple-element.149.gm, bf16[3,2,2,192,384]{4,3,2,1,0:T(8,128)(2,1)} %copy-done, bf16[3,2,2,192,384]{4,3,2,1,0:T(8,128)(2,1)} %collective-permute-done.13.sib.q_sib), custom_call_target="tpu_custom_call" | custom-call | flops 3623878656 | bytes 11010048 | tf_op jit(solution)/shard_map/input_back/pallas_call | solution.py:614
  371.1 6.3 %collective-permute-done.34 = bf16[1,4,120,384]{3,2,1,0:T(8,128)(2,1)S(1)} collective-permute-done((bf16[1,4,120,384]{3,2,1,0:T(8,128)(2,1)S(1)}, bf16[1,4,120,384]{3,2,1,0:T(8,128)(2,1)S(1)}, u32[]{:S(2)}, u32[]{:S(2)}) %collective-permute-start.34) | collective-permute-done | bytes 368672 | tf_op jit(solution)/shard_map/ppermute | solution.py:974
  387.6 6.0 %collective-permute-done.37 = bf16[1,120,768]{2,1,0:T(8,128)(2,1)S(1)} collective-permute-done((bf16[1,120,768]{2,1,0:T(8,128)(2,1)S(1)}, bf16[1,120,768]{2,1,0:T(8,128)(2,1)S(1)}, u32[]{:S(2)}, u32[]{:S(2)}) %collective-permute-start.37) | collective-permute-done | bytes 184352 | tf_op jit(solution)/shard_map/ppermute | solution.py:974
  394.3 2.9 collective-permute-done.27
  400.2 3.5 collective-permute-done.28
  403.9 2.9 collective-permute-start.32
  (203 shorter events, 97.9 us)
Async XLA Ops:
  7.2 114.7 %all-gather.2.cloned.1.call-start = ((), (), s32[]{:S(2)}) async-start(), calls=%async_computation | async-start | bytes 4866048 | tf_op jit(solution)/shard_map/all_gather | solution.py:1103
  11.8 12.5 %collective-permute-start.1 = (bf16[80,768]{1,0:T(8,128)(2,1)}, bf16[80,768]{1,0:T(8,128)(2,1)S(1)}, u32[]{:S(2)}, u32[]{:S(2)}) collective-permute-start(bf16[80,768]{1,0:T(8,128)(2,1)} %pack.1), channel_id=1, source_target_pairs={{0,4},{1,5},{2,6},{3,7},{4,0},{5,1},{6,2},{7,3},{8,12},{9,13},{10,... | collective-permute-start | bytes 368648 | tf_op jit(solution)/shard_map/ppermute | solution.py:974
  34.1 17.2 %collective-permute-start.7 = (bf16[2,4,80,384]{3,2,1,0:T(8,128)(2,1)S(1)}, bf16[2,4,80,384]{3,2,1,0:T(8,128)(2,1)S(1)}, u32[]{:S(2)}, u32[]{:S(2)}) collective-permute-start(bf16[2,4,80,384]{3,2,1,0:T(8,128)(2,1)S(1)} %pad_maximum_fusion.9), channel_id=1, source_target_pairs={{0,1},{1,0},{2,3},{3,2},{4,5},{5,4},{6,7},{7,6},{8,9},{9,8},{10,11... | collective-permute-start | bytes 1474568 | tf_op jit(solution)/shard_map/ppermute | solution.py:974
  35.8 15.6 %collective-permute-start.9 = (bf16[4,2,80,384]{3,2,0,1:T(8,128)(2,1)S(1)}, bf16[4,2,80,384]{3,2,0,1:T(8,128)(2,1)S(1)}, u32[]{:S(2)}, u32[]{:S(2)}) collective-permute-start(bf16[4,2,80,384]{3,2,0,1:T(8,128)(2,1)S(1)} %pad_maximum_fusion.10), channel_id=1, source_target_pairs={{0,16},{1,17},{2,18},{3,19},{4,20},{5,21},{6,22},{7,23},{8,24},{9,... | collective-permute-start | bytes 1474568 | tf_op jit(solution)/shard_map/ppermute | solution.py:974
  37.6 13.8 %collective-permute-start.4 = (bf16[120,768]{1,0:T(8,128)(2,1)S(1)}, bf16[120,768]{1,0:T(8,128)(2,1)S(1)}, u32[]{:S(2)}, u32[]{:S(2)}) collective-permute-start(bf16[120,768]{1,0:T(8,128)(2,1)S(1)} %constant_dynamic-update-slice_fusion), channel_id=1, source_target_pairs={{0,4},{1,5},{2,6},{3,7},{4,0},{5,1},{6,2},{7,3},{8,12},{9,13},{10,... | collective-permute-start | bytes 552968 | tf_op jit(solution)/shard_map/ppermute | solution.py:974
  56.3 15.0 %collective-permute-start.10 = (bf16[4,120,384]{2,1,0:T(8,128)(2,1)}, bf16[4,120,384]{2,1,0:T(8,128)(2,1)}, u32[]{:S(2)}, u32[]{:S(2)}) collective-permute-start(bf16[4,120,384]{2,1,0:T(8,128)(2,1)} %get-tuple-element.187), channel_id=1, source_target_pairs={{0,16},{1,17},{2,18},{3,19},{4,20},{5,21},{6,22},{7,23},{8,24},{9,... | collective-permute-start | bytes 1105928 | tf_op jit(solution)/shard_map/ppermute | solution.py:974
  57.8 13.5 %collective-permute-start.11 = (bf16[4,120,384]{2,1,0:T(8,128)(2,1)}, bf16[4,120,384]{2,1,0:T(8,128)(2,1)}, u32[]{:S(2)}, u32[]{:S(2)}) collective-permute-start(bf16[4,120,384]{2,1,0:T(8,128)(2,1)} %get-tuple-element.186), channel_id=1, source_target_pairs={{0,1},{1,0},{2,3},{3,2},{4,5},{5,4},{6,7},{7,6},{8,9},{9,8},{10,11... | collective-permute-start | bytes 1105928 | tf_op jit(solution)/shard_map/ppermute | solution.py:974
  72.7 22.5 %collective-permute-start.15 = (bf16[4,2,120,384]{3,2,0,1:T(8,128)(2,1)S(1)}, bf16[4,2,120,384]{3,2,0,1:T(8,128)(2,1)S(1)}, u32[]{:S(2)}, u32[]{:S(2)}) collective-permute-start(bf16[4,2,120,384]{3,2,0,1:T(8,128)(2,1)S(1)} %pad_maximum_fusion.6), channel_id=1, source_target_pairs={{0,16},{1,17},{2,18},{3,19},{4,20},{5,21},{6,22},{7,23},{8,24},{9,... | collective-permute-start | bytes 2211848 | tf_op jit(solution)/shard_map/ppermute | solution.py:974
  74.2 21.0 %collective-permute-start.14 = (bf16[2,4,120,384]{3,2,1,0:T(8,128)(2,1)}, bf16[2,4,120,384]{3,2,1,0:T(8,128)(2,1)S(1)}, u32[]{:S(2)}, u32[]{:S(2)}) collective-permute-start(bf16[2,4,120,384]{3,2,1,0:T(8,128)(2,1)} %pad_maximum_fusion.5), channel_id=1, source_target_pairs={{0,1},{1,0},{2,3},{3,2},{4,5},{5,4},{6,7},{7,6},{8,9},{9,8},{10,11... | collective-permute-start | bytes 2211848 | tf_op jit(solution)/shard_map/ppermute | solution.py:974
  264.7 21.9 %collective-permute-start.18 = (bf16[1,2,2,192,1536]{4,3,2,1,0:T(8,128)(2,1)}, bf16[1,2,2,192,1536]{4,3,2,1,0:T(8,128)(2,1)}, u32[]{:S(2)}, u32[]{:S(2)}) collective-permute-start(bf16[1,2,2,192,1536]{4,3,2,1,0:T(8,128)(2,1)} %get-tuple-element.135), channel_id=1, source_target_pairs={{0,8},{1,9},{2,10},{3,11},{4,12},{5,13},{6,14},{7,15},{8,0},{9,1},... | collective-permute-start | bytes 7077896 | tf_op jit(solution)/shard_map/ppermute | solution.py:974
  286.3 34.3 %collective-permute-start.19 = (bf16[1,2,2,960,384]{4,3,2,1,0:T(8,128)(2,1)}, bf16[1,2,2,960,384]{4,3,2,1,0:T(8,128)(2,1)}, u32[]{:S(2)}, u32[]{:S(2)}) collective-permute-start(bf16[1,2,2,960,384]{4,3,2,1,0:T(8,128)(2,1)} %bitcast.290), channel_id=1, source_target_pairs={{0,8},{1,9},{2,10},{3,11},{4,12},{5,13},{6,14},{7,15},{8,0},{9,1},... | collective-permute-start | bytes 8847368 | tf_op jit(solution)/shard_map/ppermute | solution.py:974
  289.2 26.7 %collective-permute-start.21 = (bf16[1,2,4,24,1536]{4,3,2,1,0:T(8,128)(2,1)S(1)}, bf16[1,2,4,24,1536]{4,3,2,1,0:T(8,128)(2,1)}, u32[]{:S(2)}, u32[]{:S(2)}) collective-permute-start(bf16[1,2,4,24,1536]{4,3,2,1,0:T(8,128)(2,1)S(1)} %dynamic-slice_bitcast_fusion.1), channel_id=1, source_target_pairs={{0,1},{1,0},{2,3},{3,2},{4,5},{5,4},{6,7},{7,6},{8,9},{9,8},{10,11... | collective-permute-start | bytes 1769480 | tf_op jit(solution)/shard_map/ppermute | solution.py:974
  290.9 28.1 %collective-permute-start.20 = (bf16[1,4,2,24,1536]{4,3,1,2,0:T(8,128)(2,1)S(1)}, bf16[1,4,2,24,1536]{4,3,1,2,0:T(8,128)(2,1)S(1)}, u32[]{:S(2)}, u32[]{:S(2)}) collective-permute-start(bf16[1,4,2,24,1536]{4,3,1,2,0:T(8,128)(2,1)S(1)} %slice_bitcast_fusion.3), channel_id=1, source_target_pairs={{0,16},{1,17},{2,18},{3,19},{4,20},{5,21},{6,22},{7,23},{8,24},{9,... | collective-permute-start | bytes 1769480 | tf_op jit(solution)/shard_map/ppermute | solution.py:974
  317.8 24.0 %collective-permute-start.25 = (bf16[1,4,24,1536]{3,2,1,0:T(8,128)(2,1)}, bf16[1,4,24,1536]{3,2,1,0:T(8,128)(2,1)}, u32[]{:S(2)}, u32[]{:S(2)}) collective-permute-start(bf16[1,4,24,1536]{3,2,1,0:T(8,128)(2,1)} %slice_bitcast_fusion.10), channel_id=1, source_target_pairs={{0,16},{1,17},{2,18},{3,19},{4,20},{5,21},{6,22},{7,23},{8,24},{9,... | collective-permute-start | bytes 884744 | tf_op jit(solution)/shard_map/ppermute | solution.py:974
  320.0 22.8 %collective-permute-start.24 = (bf16[1,4,24,1536]{3,2,1,0:T(8,128)(2,1)}, bf16[1,4,24,1536]{3,2,1,0:T(8,128)(2,1)}, u32[]{:S(2)}, u32[]{:S(2)}) collective-permute-start(bf16[1,4,24,1536]{3,2,1,0:T(8,128)(2,1)} %dynamic-slice_bitcast_fusion.4), channel_id=1, source_target_pairs={{0,1},{1,0},{2,3},{3,2},{4,5},{5,4},{6,7},{7,6},{8,9},{9,8},{10,11... | collective-permute-start | bytes 884744 | tf_op jit(solution)/shard_map/ppermute | solution.py:974
  324.4 24.6 %collective-permute-start.23 = (bf16[1,2,4,120,384]{4,3,2,1,0:T(8,128)(2,1)}, bf16[1,2,4,120,384]{4,3,2,1,0:T(8,128)(2,1)}, u32[]{:S(2)}, u32[]{:S(2)}) collective-permute-start(bf16[1,2,4,120,384]{4,3,2,1,0:T(8,128)(2,1)} %dynamic-slice_bitcast_fusion), channel_id=1, source_target_pairs={{0,1},{1,0},{2,3},{3,2},{4,5},{5,4},{6,7},{7,6},{8,9},{9,8},{10,11... | collective-permute-start | bytes 2211848 | tf_op jit(solution)/shard_map/ppermute | solution.py:974
  326.9 25.7 %collective-permute-start.22 = (bf16[1,4,2,120,384]{4,3,1,2,0:T(8,128)(2,1)}, bf16[1,4,2,120,384]{4,3,1,2,0:T(8,128)(2,1)}, u32[]{:S(2)}, u32[]{:S(2)}) collective-permute-start(bf16[1,4,2,120,384]{4,3,1,2,0:T(8,128)(2,1)} %slice_bitcast_fusion.1), channel_id=1, source_target_pairs={{0,16},{1,17},{2,18},{3,19},{4,20},{5,21},{6,22},{7,23},{8,24},{9,... | collective-permute-start | bytes 2211848 | tf_op jit(solution)/shard_map/ppermute | solution.py:974
  341.8 24.8 %collective-permute-start.26 = (bf16[1,2,2,640,384]{4,3,2,1,0:T(8,128)(2,1)}, bf16[1,2,2,640,384]{4,3,2,1,0:T(8,128)(2,1)}, u32[]{:S(2)}, u32[]{:S(2)}) collective-permute-start(bf16[1,2,2,640,384]{4,3,2,1,0:T(8,128)(2,1)} %bitcast.291), channel_id=1, source_target_pairs={{0,8},{1,9},{2,10},{3,11},{4,12},{5,13},{6,14},{7,15},{8,0},{9,1},... | collective-permute-start | bytes 5898248 | tf_op jit(solution)/shard_map/ppermute | solution.py:974
  344.8 21.0 %collective-permute-start.39 = (bf16[1,24,3072]{2,1,0:T(8,128)(2,1)}, bf16[1,24,3072]{2,1,0:T(8,128)(2,1)S(1)}, u32[]{:S(2)}, u32[]{:S(2)}) collective-permute-start(bf16[1,24,3072]{2,1,0:T(8,128)(2,1)} %get-tuple-element.197), channel_id=1, source_target_pairs={{0,2},{1,3},{2,0},{3,1},{4,6},{5,7},{6,4},{7,5},{8,10},{9,11},{10,... | collective-permute-start | bytes 442376 | tf_op jit(solution)/shard_map/ppermute | solution.py:974
  347.3 19.2 %collective-permute-start.40 = (bf16[1,24,3072]{2,1,0:T(8,128)(2,1)}, bf16[1,24,3072]{2,1,0:T(8,128)(2,1)}, u32[]{:S(2)}, u32[]{:S(2)}) collective-permute-start(bf16[1,24,3072]{2,1,0:T(8,128)(2,1)} %get-tuple-element.198), channel_id=1, source_target_pairs={{0,4},{1,5},{2,6},{3,7},{4,0},{5,1},{6,2},{7,3},{8,12},{9,13},{10,... | collective-permute-start | bytes 442376 | tf_op jit(solution)/shard_map/ppermute | solution.py:974
  349.0 17.6 %collective-permute-start.41 = (bf16[1,24,3072]{2,1,0:T(8,128)(2,1)}, bf16[1,24,3072]{2,1,0:T(8,128)(2,1)}, u32[]{:S(2)}, u32[]{:S(2)}) collective-permute-start(bf16[1,24,3072]{2,1,0:T(8,128)(2,1)} %get-tuple-element.196), channel_id=1, source_target_pairs={{0,6},{1,7},{2,4},{3,5},{4,2},{5,3},{6,0},{7,1},{8,14},{9,15},{10,... | collective-permute-start | bytes 442376 | tf_op jit(solution)/shard_map/ppermute | solution.py:974
  352.6 18.5 %collective-permute-start.35 = (bf16[1,4,120,384]{3,2,1,0:T(8,128)(2,1)}, bf16[1,4,120,384]{3,2,1,0:T(8,128)(2,1)}, u32[]{:S(2)}, u32[]{:S(2)}) collective-permute-start(bf16[1,4,120,384]{3,2,1,0:T(8,128)(2,1)} %slice_bitcast_fusion.7), channel_id=1, source_target_pairs={{0,16},{1,17},{2,18},{3,19},{4,20},{5,21},{6,22},{7,23},{8,24},{9,... | collective-permute-start | bytes 1105928 | tf_op jit(solution)/shard_map/ppermute | solution.py:974
  369.6 24.1 %collective-permute-start.29 = (bf16[1,2,4,80,384]{4,3,2,1,0:T(8,128)(2,1)S(1)}, bf16[1,2,4,80,384]{4,3,2,1,0:T(8,128)(2,1)S(1)}, u32[]{:S(2)}, u32[]{:S(2)}) collective-permute-start(bf16[1,2,4,80,384]{4,3,2,1,0:T(8,128)(2,1)S(1)} %dynamic-slice_bitcast_fusion.2), channel_id=1, source_target_pairs={{0,1},{1,0},{2,3},{3,2},{4,5},{5,4},{6,7},{7,6},{8,9},{9,8},{10,11... | collective-permute-start | bytes 1474568 | tf_op jit(solution)/shard_map/ppermute | solution.py:974
  379.3 14.3 %collective-permute-start.37 = (bf16[1,120,768]{2,1,0:T(8,128)(2,1)S(1)}, bf16[1,120,768]{2,1,0:T(8,128)(2,1)S(1)}, u32[]{:S(2)}, u32[]{:S(2)}) collective-permute-start(bf16[1,120,768]{2,1,0:T(8,128)(2,1)S(1)} %get-tuple-element.182), channel_id=1, source_target_pairs={{0,4},{1,5},{2,6},{3,7},{4,0},{5,1},{6,2},{7,3},{8,12},{9,13},{10,... | collective-permute-start | bytes 552968 | tf_op jit(solution)/shard_map/ppermute | solution.py:974
  (31 other events, 218.6 us)
Sparse Core Ops, SparseCore 0:
  51.5 67.3 all-gather.1

commit v5 on v4

--- a/solution.py
+++ b/solution.py
@@ -1088,6 +1088,11 @@
     small, tall = query_bias.shape[0], up_bias.shape[0]
     place = exchange.place()
 
+    present = (jnp.arange(rows_here, dtype=jnp.int32) < row_counts[0]).astype(jnp.int32)
+    alive = pad_mask * present[:, None]
+    alive_col = column_info(alive, count)
+    seg_col = column_info(segment_ids, count)
+
     first = Chain(
         exchange.spread(
             [query_weight, key_weight, value_weight],
@@ -1099,7 +1104,7 @@
     second = Chain(exchange.spread(tie([out_weight, up_weight], z_landed)))
     first.step()
     xy_landed = first.landed
-    first.step()
+    first.step((seg_col, alive_col))
     down_full = lax.all_gather(tie(down_weight, (xy_landed, second.landed)), AXES, axis=0, tiled=True)
     second.step(xy_landed)
     qkv, vectors = first.finish()
@@ -1109,10 +1114,6 @@
     vecs = vectors[:, :, :small].transpose(1, 0, 2).reshape(8, width)
     up_vec = jnp.broadcast_to(vectors[:, 0, 128 : 128 + tall].reshape(1, wide), (8, wide))
 
-    present = (jnp.arange(rows_here, dtype=jnp.int32) < row_counts[0]).astype(jnp.int32)
-    alive = pad_mask * present[:, None]
-    alive_col = column_info(alive, count)
-    seg_col = column_info(segment_ids, count)
     seg_row = segment_ids.reshape(rows_here, 1, row_len)
     info = (seg_col, alive_col, seg_row)
     flat = tokens.reshape(count, width)

time: 427 us -> 428 us (level)
  transfers between devices with their start and end apart: 43 -> 43, of which waited for: 17 -> 17; matrix products, arithmetic and copies ran while one was open for 8% -> 9% of each run, Pallas kernels for 27% -> 27%
where the time goes in v5:
time: 428 us; the launch traced here: 423 us
  Pallas kernels  258 us (60%)
  waiting for transfers between devices  60.4 us (14%)
  starting transfers between devices  46.5 us (11%)
  other arithmetic  24.3 us (6%)
  local copies, waits for them, and re-layouts  18.3 us (4%)
  between operations  15.8 us (4%)
    ppermute x42, waiting for transfers between devices, swap(): return lax.ppermute(value, AXES, [(i, i ^ flip) for i in range(32)])  60.4 us
    pallas_call x2, Pallas kernels, attend_back(): pl.pallas_call(attend_back_kernel, grid=(stop - start, width // QUAD), in...  48.2 us
    pallas_call x3, Pallas kernels, attend_forward(): pl.pallas_call(partial(attend_forward_kernel, start), grid=(stop - start,...  47.9 us
    ppermute x42, starting transfers between devices, swap(): return lax.ppermute(value, AXES, [(i, i ^ flip) for i in range(32)])  46.4 us
    pallas_call x1, Pallas kernels, top(): pl.pallas_call(top_kernel, grid=(count // TOP_TILE,), in_specs=[SMEM, til...  40 us
    pallas_call x1, Pallas kernels, lower(): pl.pallas_call(lower_kernel, grid=(count // TILE,), in_specs=[SMEM, pl.Bl...  29 us
    pallas_call x1, Pallas kernels, tall_grad(): pl.pallas_call(partial(tall_grad_kernel, layers), grid_spec=pltpu.Prefetc...  21.4 us
    pallas_call x1, Pallas kernels, widen(): pl.pallas_call(widen_kernel, grid=(count // TILE,), in_specs=[SMEM, tile,...  18.3 us
  transfers between devices with their start and end apart: 43, of which 17 were waited for; matrix products, arithmetic and copies ran while one was open for 9% of the time, Pallas kernels for 27%

profile of v5, /device:TPU:0, one launch (start us, length us, event | category | flops | bytes accessed | tf_op | source)
XLA Modules:
  0.0 423.3 jit_solution(14380636777787187050)
XLA Ops:
  8.8 3.0 collective-permute-start
  16.7 7.7 %collective-permute-done.1 = bf16[80,768]{1,0:T(8,128)(2,1)S(1)} collective-permute-done((bf16[80,768]{1,0:T(8,128)(2,1)}, bf16[80,768]{1,0:T(8,128)(2,1)S(1)}, u32[]{:S(2)}, u32[]{:S(2)}) %collective-permute-start.1) | collective-permute-done | bytes 122912 | tf_op jit(solution)/shard_map/ppermute | solution.py:974
  28.5 3.2 collective-permute-done.6
  42.4 9.0 %collective-permute-done.4 = bf16[120,768]{1,0:T(8,128)(2,1)S(1)} collective-permute-done((bf16[120,768]{1,0:T(8,128)(2,1)S(1)}, bf16[120,768]{1,0:T(8,128)(2,1)S(1)}, u32[]{:S(2)}, u32[]{:S(2)}) %collective-permute-start.4) | collective-permute-done | bytes 184352 | tf_op jit(solution)/shard_map/ppermute | solution.py:974
  62.5 10.1 %attend_forward.3 = (bf16[1024,768]{1,0:T(8,128)(2,1)}, bf16[1024,768]{1,0:T(8,128)(2,1)}, bf16[1024,768]{1,0:T(8,128)(2,1)}, bf16[1024,768]{1,0:T(8,128)(2,1)}, f32[2,3,8,512]{3,2,1,0:T(8,128)}) custom-call(s32[2]{0:T(128)} %pad_add_fusion.core_ref.place_ref, bf16[1024,768]{1,0:T(8,128)(2,1)} %bitcast.293, s32[1024,128]{1,0:T(8,128)} %broadcast_in_dim.65.seg_col, ...), custom_call_target="tpu_custom_call" | custom-call | flops 3355443200 | bytes 6160384 | tf_op jit(solution)/shard_map/attend_forward/pallas_call | solution.py:181
  77.1 16.0 %attend_forward.4 = (bf16[1024,768]{1,0:T(8,128)(2,1)}, bf16[1024,768]{1,0:T(8,128)(2,1)}, bf16[1024,768]{1,0:T(8,128)(2,1)}, bf16[1024,768]{1,0:T(8,128)(2,1)}, f32[2,3,8,512]{3,2,1,0:T(8,128)}) custom-call(s32[2]{0:T(128)} %pad_add_fusion.core_ref.place_ref, ...), custom_call_target="tpu_custom_call", output_to_operand_aliasing={{0}: (8, {}), {1}: (9, {}), {2}: (10, {}), {3}: (11, {}), {... | custom-call | flops 6710886400 | bytes 8781824 | tf_op jit(solution)/shard_map/attend_forward/pallas_call | solution.py:181
  93.1 3.2 collective-permute-done.15
  100.3 3.6 collective-permute-done.16.o_sib
  104.6 18.3 %widen.1 = (f32[1024,768]{1,0:T(8,128)}, bf16[1024,768]{1,0:T(8,128)(2,1)}, bf16[1024,3072]{1,0:T(8,128)(2,1)}, bf16[1024,3072]{1,0:T(8,128)(2,1)}) custom-call(s32[2]{0:T(128)} %pad_add_fusion.core_ref.place_ref, bf16[1024,768]{1,0:T(8,128)(2,1)} %get-tuple-element.103.ctx.refs_7_, bf16[1024,768]{1,0:T(8,128)(2,1)} %bitcast.295, f32[8,768]{1,0:T(8,128)} %reshape.340.vecs, ...), custom_call_target="tpu_custom_call" | custom-call | flops 6039797760 | bytes 22020096 | tf_op jit(solution)/shard_map/widen/pallas_call | solution.py:253
  123.0 12.4 %narrow.1 = (f32[1024,768]{1,0:T(8,128)}, bf16[1024,768]{1,0:T(8,128)(2,1)}) custom-call(s32[2]{0:T(128)} %pad_add_fusion.core_ref.place_ref, bf16[1024,3072]{1,0:T(8,128)(2,1)} %get-tuple-element.108.act.refs_3_, f32[1024,768]{1,0:T(8,128)} %get-tuple-element.109.mixed, f32[8,768]{1,0:T(8,128)} %reshape.340.vecs, ...), custom_call_target="tpu_custom_call" | custom-call | flops 4831838208 | bytes 14155776 | tf_op jit(solution)/shard_map/narrow/pallas_call | solution.py:298
  135.3 21.8 %attend_forward.5 = (bf16[1024,768]{1,0:T(8,128)(2,1)}, bf16[1024,768]{1,0:T(8,128)(2,1)}, bf16[1024,768]{1,0:T(8,128)(2,1)}, bf16[1024,768]{1,0:T(8,128)(2,1)}, f32[2,3,8,512]{3,2,1,0:T(8,128)}) custom-call(s32[2]{0:T(128)} %pad_add_fusion.core_ref.place_ref, bf16[1024,768]{1,0:T(8,128)(2,1)} %get-tuple-element.111.x.refs_2_, ...), custom_call_target="tpu_custom_call" | custom-call | flops 10066329600 | bytes 11403264 | tf_op jit(solution)/shard_map/attend_forward/pallas_call | solution.py:181
  157.2 40.0 %top.1 = (bf16[1024,768]{1,0:T(8,128)(2,1)}, bf16[1024,768]{1,0:T(8,128)(2,1)}, bf16[1024,3072]{1,0:T(8,128)(2,1)}, bf16[1024,768]{1,0:T(8,128)(2,1)}, bf16[1024...) custom-call(s32[2]{0:T(128)} %pad_add_fusion.core_ref.place_ref, ...), custom_call_target="tpu_custom_call" | custom-call | flops 21743271936 | bytes 29884416 | tf_op jit(solution)/shard_map/top/pallas_call | solution.py:421
  197.2 24.1 %attend_back.2 = (bf16[3,1024,768]{2,1,0:T(8,128)(2,1)}, f32[2,2,8,768]{3,2,1,0:T(8,128)}) custom-call(bf16[1024,768]{1,0:T(8,128)(2,1)} %get-tuple-element.118.q, bf16[1024,768]{1,0:T(8,128)(2,1)} %get-tuple-element.119.k, bf16[1024,768]{1,0:T(8,128)(2,1)} %get-tuple-element.120.v, bf16[1024,768]{1,0:T(8,128)(2,1)} %get-tuple-element.121.gctx, ...), custom_call_target="tpu_custom_call" | custom-call | flops 16106127360 | bytes 12582912 | tf_op jit(solution)/shard_map/attend_back/pallas_call | solution.py:573
  221.3 29.0 %lower.1 = (bf16[1024,768]{1,0:T(8,128)(2,1)}, bf16[1024,3072]{1,0:T(8,128)(2,1)}, bf16[1024,768]{1,0:T(8,128)(2,1)}, f32[1024,768]{1,0:T(8,128)}, bf16[1024,768...) custom-call(s32[2]{0:T(128)} %pad_add_fusion.core_ref.place_ref, ...), custom_call_target="tpu_custom_call" | custom-call | flops 14495514624 | bytes 36175872 | tf_op jit(solution)/shard_map/lower/pallas_call | solution.py:501
  250.4 15.3 %weight_grad.1 = (bf16[1,2,2,192,1536]{4,3,2,1,0:T(8,128)(2,1)}, bf16[1,2,2,192,1536]{4,3,2,1,0:T(8,128)(2,1)}) custom-call(s32[2]{0:T(128)} %pad_add_fusion.core_ref.place_ref, bf16[1,1024,768]{2,1,0:T(8,128)(2,1)} %bitcast.298, bf16[1,1024,768]{2,1,0:T(8,128)(2,1)} %bitcast.299, bf16[1024,3072]{1,0:T(8,128)(2,1)} %get-tuple-element.131.refs_2_, ...), custom_call_target="tpu_custom_call" | custom-call | flops 9663676416 | bytes 20447232 | tf_op jit(solution)/shard_map/weight_grad/pallas_call | solution.py:670
  265.8 21.4 %tall_grad.1 = (bf16[2,2,8,120,384]{4,3,2,1,0:T(8,128)(2,1)}, bf16[2,2,8,120,384]{4,3,2,1,0:T(8,128)(2,1)}) custom-call(s32[2]{0:T(128)} %pad_add_fusion.core_ref.place_ref, bf16[1024,3072]{1,0:T(8,128)(2,1)} %get-tuple-element.127.refs_0_, bf16[1024,3072]{1,0:T(8,128)(2,1)} %get-tuple-element.133.refs_1_, bf16[1024,768]{1,0:T(8,128)(2,1)} %get-tuple-element.134.refs_2_, ...), custom_call_target="tpu_custom_call" | custom-call | flops 12079595520 | bytes 27918336 | tf_op jit(solution)/shard_map/tall_grad/pallas_call | solution.py:827
  292.8 24.1 %attend_back.3 = (bf16[3,1024,768]{2,1,0:T(8,128)(2,1)}, f32[2,2,8,768]{3,2,1,0:T(8,128)}) custom-call(bf16[1024,768]{1,0:T(8,128)(2,1)} %get-tuple-element.115.q, bf16[1024,768]{1,0:T(8,128)(2,1)} %get-tuple-element.116.k, bf16[1024,768]{1,0:T(8,128)(2,1)} %get-tuple-element.117.v, bf16[1024,768]{1,0:T(8,128)(2,1)} %get-tuple-element.140.gctx, ...), custom_call_target="tpu_custom_call" | custom-call | flops 16106127360 | bytes 12582912 | tf_op jit(solution)/shard_map/attend_back/pallas_call | solution.py:573
  328.8 14.0 %joint_grad.1 = (bf16[2,2,8,80,384]{4,3,2,1,0:T(8,128)(2,1)}, bf16[2,2,8,80,384]{4,3,2,1,0:T(8,128)(2,1)}) custom-call(s32[2]{0:T(128)} %pad_add_fusion.core_ref.place_ref, bf16[3,1024,768]{2,1,0:T(8,128)(2,1)} %get-tuple-element.123.grads.refs_0_, bf16[3,1024,768]{2,1,0:T(8,128)(2,1)} %get-tuple-element.152.refs_1_.grads, ...), custom_call_target="tpu_custom_call" | custom-call | flops 7247757312 | bytes 16121856 | tf_op jit(solution)/shard_map/joint_grad/pallas_call | solution.py:747
  356.7 10.0 %input_back.1 = f32[1024,768]{1,0:T(8,128)} custom-call(s32[2]{0:T(128)} %pad_add_fusion.core_ref.place_ref, bf16[3,1024,768]{2,1,0:T(8,128)(2,1)} %get-tuple-element.152.refs_1_.grads, f32[1024,768]{1,0:T(8,128)} %get-tuple-element.153.gm, bf16[3,2,2,192,384]{4,3,2,1,0:T(8,128)(2,1)} %copy-done, bf16[3,2,2,192,384]{4,3,2,1,0:T(8,128)(2,1)} %collective-permute-done.13.sib.q_sib), custom_call_target="tpu_custom_call" | custom-call | flops 3623878656 | bytes 11010048 | tf_op jit(solution)/shard_map/input_back/pallas_call | solution.py:614
  372.0 6.3 %collective-permute-done.34 = bf16[1,4,120,384]{3,2,1,0:T(8,128)(2,1)S(1)} collective-permute-done((bf16[1,4,120,384]{3,2,1,0:T(8,128)(2,1)S(1)}, bf16[1,4,120,384]{3,2,1,0:T(8,128)(2,1)S(1)}, u32[]{:S(2)}, u32[]{:S(2)}) %collective-permute-start.34) | collective-permute-done | bytes 368672 | tf_op jit(solution)/shard_map/ppermute | solution.py:974
  388.4 6.0 %collective-permute-done.37 = bf16[1,120,768]{2,1,0:T(8,128)(2,1)S(1)} collective-permute-done((bf16[1,120,768]{2,1,0:T(8,128)(2,1)S(1)}, bf16[1,120,768]{2,1,0:T(8,128)(2,1)S(1)}, u32[]{:S(2)}, u32[]{:S(2)}) %collective-permute-start.37) | collective-permute-done | bytes 184352 | tf_op jit(solution)/shard_map/ppermute | solution.py:974
  395.1 3.0 collective-permute-done.27
  401.1 3.4 collective-permute-done.28
  404.7 2.9 collective-permute-start.32
  (209 shorter events, 99.6 us)
Async XLA Ops:
  7.2 115.8 %all-gather.2.cloned.1.call-start = ((), (), s32[]{:S(2)}) async-start(), calls=%async_computation | async-start | bytes 4866048 | tf_op jit(solution)/shard_map/all_gather | solution.py:1108
  11.8 12.5 %collective-permute-start.1 = (bf16[80,768]{1,0:T(8,128)(2,1)}, bf16[80,768]{1,0:T(8,128)(2,1)S(1)}, u32[]{:S(2)}, u32[]{:S(2)}) collective-permute-start(bf16[80,768]{1,0:T(8,128)(2,1)} %pack.1), channel_id=1, source_target_pairs={{0,4},{1,5},{2,6},{3,7},{4,0},{5,1},{6,2},{7,3},{8,12},{9,13},{10,... | collective-permute-start | bytes 368648 | tf_op jit(solution)/shard_map/ppermute | solution.py:974
  34.0 17.4 %collective-permute-start.9 = (bf16[4,2,80,384]{3,2,0,1:T(8,128)(2,1)S(1)}, bf16[4,2,80,384]{3,2,0,1:T(8,128)(2,1)S(1)}, u32[]{:S(2)}, u32[]{:S(2)}) collective-permute-start(bf16[4,2,80,384]{3,2,0,1:T(8,128)(2,1)S(1)} %pad_maximum_fusion.10), channel_id=1, source_target_pairs={{0,16},{1,17},{2,18},{3,19},{4,20},{5,21},{6,22},{7,23},{8,24},{9,... | collective-permute-start | bytes 1474568 | tf_op jit(solution)/shard_map/ppermute | solution.py:974
  34.1 17.9 %collective-permute-start.7 = (bf16[2,4,80,384]{3,2,1,0:T(8,128)(2,1)S(1)}, bf16[2,4,80,384]{3,2,1,0:T(8,128)(2,1)S(1)}, u32[]{:S(2)}, u32[]{:S(2)}) collective-permute-start(bf16[2,4,80,384]{3,2,1,0:T(8,128)(2,1)S(1)} %pad_maximum_fusion.9), channel_id=1, source_target_pairs={{0,1},{1,0},{2,3},{3,2},{4,5},{5,4},{6,7},{7,6},{8,9},{9,8},{10,11... | collective-permute-start | bytes 1474568 | tf_op jit(solution)/shard_map/ppermute | solution.py:974
  37.6 13.8 %collective-permute-start.4 = (bf16[120,768]{1,0:T(8,128)(2,1)S(1)}, bf16[120,768]{1,0:T(8,128)(2,1)S(1)}, u32[]{:S(2)}, u32[]{:S(2)}) collective-permute-start(bf16[120,768]{1,0:T(8,128)(2,1)S(1)} %constant_dynamic-update-slice_fusion), channel_id=1, source_target_pairs={{0,4},{1,5},{2,6},{3,7},{4,0},{5,1},{6,2},{7,3},{8,12},{9,13},{10,... | collective-permute-start | bytes 552968 | tf_op jit(solution)/shard_map/ppermute | solution.py:974
  38.9 12.5 %collective-permute-start.5 = (bf16[120,768]{1,0:T(8,128)(2,1)S(1)}, bf16[120,768]{1,0:T(8,128)(2,1)S(1)}, u32[]{:S(2)}, u32[]{:S(2)}) collective-permute-start(bf16[120,768]{1,0:T(8,128)(2,1)S(1)} %constant_dynamic-update-slice_fusion), channel_id=1, source_target_pairs={{0,6},{1,7},{2,4},{3,5},{4,2},{5,3},{6,0},{7,1},{8,14},{9,15},{10,... | collective-permute-start | bytes 552968 | tf_op jit(solution)/shard_map/ppermute | solution.py:974
  59.0 13.7 %collective-permute-start.10 = (bf16[4,120,384]{2,1,0:T(8,128)(2,1)}, bf16[4,120,384]{2,1,0:T(8,128)(2,1)}, u32[]{:S(2)}, u32[]{:S(2)}) collective-permute-start(bf16[4,120,384]{2,1,0:T(8,128)(2,1)} %get-tuple-element.191), channel_id=1, source_target_pairs={{0,16},{1,17},{2,18},{3,19},{4,20},{5,21},{6,22},{7,23},{8,24},{9,... | collective-permute-start | bytes 1105928 | tf_op jit(solution)/shard_map/ppermute | solution.py:974
  74.0 22.3 %collective-permute-start.15 = (bf16[4,2,120,384]{3,2,0,1:T(8,128)(2,1)S(1)}, bf16[4,2,120,384]{3,2,0,1:T(8,128)(2,1)S(1)}, u32[]{:S(2)}, u32[]{:S(2)}) collective-permute-start(bf16[4,2,120,384]{3,2,0,1:T(8,128)(2,1)S(1)} %pad_maximum_fusion.6), channel_id=1, source_target_pairs={{0,16},{1,17},{2,18},{3,19},{4,20},{5,21},{6,22},{7,23},{8,24},{9,... | collective-permute-start | bytes 2211848 | tf_op jit(solution)/shard_map/ppermute | solution.py:974
  75.6 20.7 %collective-permute-start.14 = (bf16[2,4,120,384]{3,2,1,0:T(8,128)(2,1)}, bf16[2,4,120,384]{3,2,1,0:T(8,128)(2,1)S(1)}, u32[]{:S(2)}, u32[]{:S(2)}) collective-permute-start(bf16[2,4,120,384]{3,2,1,0:T(8,128)(2,1)} %pad_maximum_fusion.5), channel_id=1, source_target_pairs={{0,1},{1,0},{2,3},{3,2},{4,5},{5,4},{6,7},{7,6},{8,9},{9,8},{10,11... | collective-permute-start | bytes 2211848 | tf_op jit(solution)/shard_map/ppermute | solution.py:974
  265.7 21.9 %collective-permute-start.18 = (bf16[1,2,2,192,1536]{4,3,2,1,0:T(8,128)(2,1)}, bf16[1,2,2,192,1536]{4,3,2,1,0:T(8,128)(2,1)}, u32[]{:S(2)}, u32[]{:S(2)}) collective-permute-start(bf16[1,2,2,192,1536]{4,3,2,1,0:T(8,128)(2,1)} %get-tuple-element.139), channel_id=1, source_target_pairs={{0,8},{1,9},{2,10},{3,11},{4,12},{5,13},{6,14},{7,15},{8,0},{9,1},... | collective-permute-start | bytes 7077896 | tf_op jit(solution)/shard_map/ppermute | solution.py:974
  287.2 34.4 %collective-permute-start.19 = (bf16[1,2,2,960,384]{4,3,2,1,0:T(8,128)(2,1)}, bf16[1,2,2,960,384]{4,3,2,1,0:T(8,128)(2,1)}, u32[]{:S(2)}, u32[]{:S(2)}) collective-permute-start(bf16[1,2,2,960,384]{4,3,2,1,0:T(8,128)(2,1)} %bitcast.290), channel_id=1, source_target_pairs={{0,8},{1,9},{2,10},{3,11},{4,12},{5,13},{6,14},{7,15},{8,0},{9,1},... | collective-permute-start | bytes 8847368 | tf_op jit(solution)/shard_map/ppermute | solution.py:974
  290.2 26.7 %collective-permute-start.21 = (bf16[1,2,4,24,1536]{4,3,2,1,0:T(8,128)(2,1)S(1)}, bf16[1,2,4,24,1536]{4,3,2,1,0:T(8,128)(2,1)}, u32[]{:S(2)}, u32[]{:S(2)}) collective-permute-start(bf16[1,2,4,24,1536]{4,3,2,1,0:T(8,128)(2,1)S(1)} %dynamic-slice_bitcast_fusion.1), channel_id=1, source_target_pairs={{0,1},{1,0},{2,3},{3,2},{4,5},{5,4},{6,7},{7,6},{8,9},{9,8},{10,11... | collective-permute-start | bytes 1769480 | tf_op jit(solution)/shard_map/ppermute | solution.py:974
  291.9 28.1 %collective-permute-start.20 = (bf16[1,4,2,24,1536]{4,3,1,2,0:T(8,128)(2,1)S(1)}, bf16[1,4,2,24,1536]{4,3,1,2,0:T(8,128)(2,1)S(1)}, u32[]{:S(2)}, u32[]{:S(2)}) collective-permute-start(bf16[1,4,2,24,1536]{4,3,1,2,0:T(8,128)(2,1)S(1)} %slice_bitcast_fusion.3), channel_id=1, source_target_pairs={{0,16},{1,17},{2,18},{3,19},{4,20},{5,21},{6,22},{7,23},{8,24},{9,... | collective-permute-start | bytes 1769480 | tf_op jit(solution)/shard_map/ppermute | solution.py:974
  318.9 23.9 %collective-permute-start.25 = (bf16[1,4,24,1536]{3,2,1,0:T(8,128)(2,1)}, bf16[1,4,24,1536]{3,2,1,0:T(8,128)(2,1)}, u32[]{:S(2)}, u32[]{:S(2)}) collective-permute-start(bf16[1,4,24,1536]{3,2,1,0:T(8,128)(2,1)} %slice_bitcast_fusion.10), channel_id=1, source_target_pairs={{0,16},{1,17},{2,18},{3,19},{4,20},{5,21},{6,22},{7,23},{8,24},{9,... | collective-permute-start | bytes 884744 | tf_op jit(solution)/shard_map/ppermute | solution.py:974
  321.0 22.8 %collective-permute-start.24 = (bf16[1,4,24,1536]{3,2,1,0:T(8,128)(2,1)}, bf16[1,4,24,1536]{3,2,1,0:T(8,128)(2,1)}, u32[]{:S(2)}, u32[]{:S(2)}) collective-permute-start(bf16[1,4,24,1536]{3,2,1,0:T(8,128)(2,1)} %dynamic-slice_bitcast_fusion.4), channel_id=1, source_target_pairs={{0,1},{1,0},{2,3},{3,2},{4,5},{5,4},{6,7},{7,6},{8,9},{9,8},{10,11... | collective-permute-start | bytes 884744 | tf_op jit(solution)/shard_map/ppermute | solution.py:974
  325.4 24.6 %collective-permute-start.23 = (bf16[1,2,4,120,384]{4,3,2,1,0:T(8,128)(2,1)}, bf16[1,2,4,120,384]{4,3,2,1,0:T(8,128)(2,1)}, u32[]{:S(2)}, u32[]{:S(2)}) collective-permute-start(bf16[1,2,4,120,384]{4,3,2,1,0:T(8,128)(2,1)} %dynamic-slice_bitcast_fusion), channel_id=1, source_target_pairs={{0,1},{1,0},{2,3},{3,2},{4,5},{5,4},{6,7},{7,6},{8,9},{9,8},{10,11... | collective-permute-start | bytes 2211848 | tf_op jit(solution)/shard_map/ppermute | solution.py:974
  328.0 25.7 %collective-permute-start.22 = (bf16[1,4,2,120,384]{4,3,1,2,0:T(8,128)(2,1)}, bf16[1,4,2,120,384]{4,3,1,2,0:T(8,128)(2,1)}, u32[]{:S(2)}, u32[]{:S(2)}) collective-permute-start(bf16[1,4,2,120,384]{4,3,1,2,0:T(8,128)(2,1)} %slice_bitcast_fusion.1), channel_id=1, source_target_pairs={{0,16},{1,17},{2,18},{3,19},{4,20},{5,21},{6,22},{7,23},{8,24},{9,... | collective-permute-start | bytes 2211848 | tf_op jit(solution)/shard_map/ppermute | solution.py:974
  342.7 24.6 %collective-permute-start.26 = (bf16[1,2,2,640,384]{4,3,2,1,0:T(8,128)(2,1)}, bf16[1,2,2,640,384]{4,3,2,1,0:T(8,128)(2,1)}, u32[]{:S(2)}, u32[]{:S(2)}) collective-permute-start(bf16[1,2,2,640,384]{4,3,2,1,0:T(8,128)(2,1)} %bitcast.291), channel_id=1, source_target_pairs={{0,8},{1,9},{2,10},{3,11},{4,12},{5,13},{6,14},{7,15},{8,0},{9,1},... | collective-permute-start | bytes 5898248 | tf_op jit(solution)/shard_map/ppermute | solution.py:974
  345.8 20.9 %collective-permute-start.39 = (bf16[1,24,3072]{2,1,0:T(8,128)(2,1)}, bf16[1,24,3072]{2,1,0:T(8,128)(2,1)S(1)}, u32[]{:S(2)}, u32[]{:S(2)}) collective-permute-start(bf16[1,24,3072]{2,1,0:T(8,128)(2,1)} %get-tuple-element.201), channel_id=1, source_target_pairs={{0,2},{1,3},{2,0},{3,1},{4,6},{5,7},{6,4},{7,5},{8,10},{9,11},{10,... | collective-permute-start | bytes 442376 | tf_op jit(solution)/shard_map/ppermute | solution.py:974
  348.3 19.1 %collective-permute-start.40 = (bf16[1,24,3072]{2,1,0:T(8,128)(2,1)}, bf16[1,24,3072]{2,1,0:T(8,128)(2,1)}, u32[]{:S(2)}, u32[]{:S(2)}) collective-permute-start(bf16[1,24,3072]{2,1,0:T(8,128)(2,1)} %get-tuple-element.202), channel_id=1, source_target_pairs={{0,4},{1,5},{2,6},{3,7},{4,0},{5,1},{6,2},{7,3},{8,12},{9,13},{10,... | collective-permute-start | bytes 442376 | tf_op jit(solution)/shard_map/ppermute | solution.py:974
  350.0 17.4 %collective-permute-start.41 = (bf16[1,24,3072]{2,1,0:T(8,128)(2,1)}, bf16[1,24,3072]{2,1,0:T(8,128)(2,1)}, u32[]{:S(2)}, u32[]{:S(2)}) collective-permute-start(bf16[1,24,3072]{2,1,0:T(8,128)(2,1)} %get-tuple-element.200), channel_id=1, source_target_pairs={{0,6},{1,7},{2,4},{3,5},{4,2},{5,3},{6,0},{7,1},{8,14},{9,15},{10,... | collective-permute-start | bytes 442376 | tf_op jit(solution)/shard_map/ppermute | solution.py:974
  353.6 18.3 %collective-permute-start.35 = (bf16[1,4,120,384]{3,2,1,0:T(8,128)(2,1)}, bf16[1,4,120,384]{3,2,1,0:T(8,128)(2,1)}, u32[]{:S(2)}, u32[]{:S(2)}) collective-permute-start(bf16[1,4,120,384]{3,2,1,0:T(8,128)(2,1)} %slice_bitcast_fusion.7), channel_id=1, source_target_pairs={{0,16},{1,17},{2,18},{3,19},{4,20},{5,21},{6,22},{7,23},{8,24},{9,... | collective-permute-start | bytes 1105928 | tf_op jit(solution)/shard_map/ppermute | solution.py:974
  370.4 24.2 %collective-permute-start.29 = (bf16[1,2,4,80,384]{4,3,2,1,0:T(8,128)(2,1)S(1)}, bf16[1,2,4,80,384]{4,3,2,1,0:T(8,128)(2,1)S(1)}, u32[]{:S(2)}, u32[]{:S(2)}) collective-permute-start(bf16[1,2,4,80,384]{4,3,2,1,0:T(8,128)(2,1)S(1)} %dynamic-slice_bitcast_fusion.2), channel_id=1, source_target_pairs={{0,1},{1,0},{2,3},{3,2},{4,5},{5,4},{6,7},{7,6},{8,9},{9,8},{10,11... | collective-permute-start | bytes 1474568 | tf_op jit(solution)/shard_map/ppermute | solution.py:974
  380.1 14.3 %collective-permute-start.37 = (bf16[1,120,768]{2,1,0:T(8,128)(2,1)S(1)}, bf16[1,120,768]{2,1,0:T(8,128)(2,1)S(1)}, u32[]{:S(2)}, u32[]{:S(2)}) collective-permute-start(bf16[1,120,768]{2,1,0:T(8,128)(2,1)S(1)} %get-tuple-element.186), channel_id=1, source_target_pairs={{0,4},{1,5},{2,6},{3,7},{4,0},{5,1},{6,2},{7,3},{8,12},{9,13},{10,... | collective-permute-start | bytes 552968 | tf_op jit(solution)/shard_map/ppermute | solution.py:974
  (34 other events, 257.8 us)
Sparse Core Ops, SparseCore 0:
  52.2 67.3 all-gather.1
